TPU v7x, 256 devices: a whole 4x4x8 slice. The times are simulated.
256 devices in a mesh: lev: 4 (over z_hi), lat: 64 (over y, x, z_lo, core).
Axes of the slice: x: 4, y: 4, z: 8 (z_hi: 4, z_lo: 2; z = z_hi * 2 + z_lo), core: 2. Of those that a mesh axis runs over, the one named last changes fastest.
Arguments:
- field: bfloat16 [12, 256, 360, 128], P('lev', 'lat'), may hold values from -6 to 6
- level_count: int32 [4], replicated, may hold values from 1 to 3, as said below
- tap_rows: int32 [256, 8], replicated, may hold values from -2 to 2
- tap_lons: int32 [256, 8], replicated, may hold values from -4 to 4
- tap_values: float32 [256, 8, 4], replicated, may hold values from -2.1 to 2.1
- norm_gain: float32 [2, 128], replicated, may hold values from 0.5 to 1.5
- disco_weight: bfloat16 [2, 512, 128], replicated, may hold values from -0.25 to 0.25
- vert_weight: bfloat16 [2, 384, 128], replicated, may hold values from -0.3125 to 0.3125
Outputs:
- result: bfloat16 [12, 256, 360, 128], P('lev', 'lat')
Inputs may be any that keep to these rules, and one draw needn't show every extreme that they name: Group g holds the next level_count[g] levels from the lowest up; the entries sum to 9 and the largest equals 3.
All inputs are finite; a program needn't handle non-finite values.
Results may differ from a plain program's by a relative error of at most 0.008.
Values may be sent and summed in bfloat16 or wider, within the bound.
No kernel may reach another device: no remote copies, remote signals or barrier semaphores. Data moves between devices by JAX's collectives and lax.ppermute only.
A program may use at most 64 MiB of HBM per device.

v0:
```python
import jax
import jax.numpy as jnp
from jax import lax
from jax.sharding import PartitionSpec as P

K = 4
TAPS = 8
H = 2
WLON = 4
PASSES = 2


EPSILON = 1e-06


def from_behind(block, axis, distance):
    devices = range(lax.axis_size(axis))
    route = [(i - distance, i) for i in devices if i - distance in devices]
    return lax.ppermute(block, axis, route)


def with_halo(cells, sides, width):
    for axis, dim in sides:
        count = lax.axis_size(axis)
        ends = count - 1
        head = lax.slice_in_dim(cells, 0, width, axis=dim)
        tail = lax.slice_in_dim(cells, cells.shape[dim] - width, cells.shape[dim], axis=dim)
        cells = jnp.concatenate(
            [
                lax.ppermute(tail, axis, [(i, (i + 1) % count) for i in range(ends)]),
                cells,
                lax.ppermute(head, axis, [((i + 1) % count, i) for i in range(ends)]),
            ],
            axis=dim,
        )
    return cells


def normalize(values, gain):
    widened = values.astype(jnp.float32)
    mean_square = jnp.mean(widened * widened, axis=-1, keepdims=True)
    return (widened * lax.rsqrt(mean_square + EPSILON) * gain).astype(jnp.bfloat16)


def filter_band(padded, row_table, lon_table, value_table, weight):
    slot_total = padded.shape[0]
    lon_count = padded.shape[2]
    channels = padded.shape[3]
    row_count = row_table.shape[0]
    wrapped = jnp.concatenate(
        [padded[:, :, lon_count - WLON :], padded, padded[:, :, :WLON]], axis=2
    )

    def one_row(row_index, output):
        total = jnp.zeros((slot_total, lon_count, K, channels), jnp.float32)
        for tap_index in range(TAPS):
            source_row = row_index + row_table[row_index, tap_index] + H
            source_lon = lon_table[row_index, tap_index] + WLON
            picked = lax.dynamic_slice(
                wrapped, (0, source_row, source_lon, 0), (slot_total, 1, lon_count, channels)
            )
            factors = value_table[row_index, tap_index]
            total = (
                total
                + factors[None, None, :, None] * picked[:, 0].astype(jnp.float32)[:, :, None, :]
            )
        filtered = total.astype(jnp.bfloat16).reshape(slot_total * lon_count, K * channels)
        mixed = jnp.dot(filtered, weight, preferred_element_type=jnp.float32)
        mixed = mixed.astype(jnp.bfloat16).reshape(slot_total, 1, lon_count, channels)
        return lax.dynamic_update_slice(output, mixed, (0, row_index, 0, 0))

    output = jnp.zeros((slot_total, row_count, lon_count, channels), jnp.bfloat16)
    return lax.fori_loop(0, row_count, one_row, output)


def mix_levels(disco, residual, own_count, vertical_weight):
    slot_total = disco.shape[0]
    channels = disco.shape[-1]
    top_plane = lax.dynamic_index_in_dim(disco, own_count - 1, 0, keepdims=False)
    from_below = from_behind(top_plane, "lev", 1)
    from_above = from_behind(disco[0], "lev", -1)
    slot_ids = jnp.arange(slot_total, dtype=jnp.int32)
    below = jnp.concatenate([from_below[None], disco[:-1]], axis=0)
    shifted_up = jnp.concatenate([disco[1:], from_above[None]], axis=0)
    above = jnp.where((slot_ids + 1 < own_count)[:, None, None, None], shifted_up, from_above[None])
    stacked = jnp.concatenate([below, disco, above], axis=-1)
    vertical = jnp.dot(
        stacked.reshape(-1, 3 * channels), vertical_weight, preferred_element_type=jnp.float32
    )
    vertical = vertical.reshape(disco.shape)
    updated = residual.astype(jnp.float32) + jax.nn.gelu(vertical, approximate=False)
    alive = (slot_ids < own_count)[:, None, None, None]
    return (updated, alive)


def on_device(
    field, level_count, tap_rows, tap_lons, tap_values, norm_gain, disco_weight, vert_weight
):
    band_rows = field.shape[1]
    first_row = lax.axis_index("lat") * band_rows
    own_count = level_count[lax.axis_index("lev")]
    table_margin = PASSES * H
    padded_rows = jnp.pad(tap_rows, ((table_margin, table_margin), (0, 0)))
    padded_lons = jnp.pad(tap_lons, ((table_margin, table_margin), (0, 0)))
    padded_values = jnp.pad(tap_values, ((table_margin, table_margin), (0, 0), (0, 0)))
    start_row = first_row - 0 + table_margin
    row_total = band_rows + 2 * 0
    row_part = lax.dynamic_slice_in_dim(padded_rows, start_row, row_total, 0)
    lon_part = lax.dynamic_slice_in_dim(padded_lons, start_row, row_total, 0)
    value_part = lax.dynamic_slice_in_dim(padded_values, start_row, row_total, 0)
    row_part, lon_part, value_part = (row_part, lon_part, value_part)
    current = field
    for pass_index in range(PASSES):
        normed = normalize(current, norm_gain[pass_index])
        padded = with_halo(normed, (("lat", 1),), H)
        disco = filter_band(padded, row_part, lon_part, value_part, disco_weight[pass_index])
        updated, alive = mix_levels(disco, current, own_count, vert_weight[pass_index])
        current = jnp.where(alive, updated, 0.0).astype(jnp.bfloat16)
    return current


def solution(mesh):
    return jax.shard_map(
        on_device,
        mesh=mesh,
        in_specs=(P("lev", "lat", None, None), P(), P(), P(), P(), P(), P(), P()),
        out_specs=P("lev", "lat", None, None),
        check_vma=False,
    )
```

profile of v0, /device:TPU:49, one launch (start us, length us, event | category | flops | bytes accessed | tf_op | source)
XLA Modules:
  0.0 276.7 jit_solution(3542496063259606404)
XLA Ops:
  0.8 1.9 fusion.54
  2.8 1.8 fusion.56
  4.7 3.2 %collective-permute-start = (bf16[3,2,360,128]{3,2,1,0:T(8,128)(2,1)S(1)}, bf16[3,2,360,128]{3,2,1,0:T(8,128)(2,1)}, u32[]{:S(2)}, u32[]{:S(2)}) collective-permute-start(bf16[3,2,360,128]{3,2,1,0:T(8,128)(2,1)S(1)} %get-tuple-element.565), channel_id=1, source_target_pairs={{0,1},{1,2},{2,3},{3,4},{4,5},{5,6},{6,7},{7,8},{8,9},{9,10},{10,1... | collective-permute-start | bytes 1658888 | tf_op jit(solution)/shard_map/ppermute | solution.py:30
  7.9 1.9 collective-permute-start.1
  17.0 5.5 %collective-permute-done.1 = bf16[3,2,360,128]{3,2,1,0:T(8,128)(2,1)} collective-permute-done((bf16[3,2,360,128]{3,2,1,0:T(8,128)(2,1)S(1)}, bf16[3,2,360,128]{3,2,1,0:T(8,128)(2,1)}, u32[]{:S(2)}, u32[]{:S(2)}) %collective-permute-start.1) | collective-permute-done | bytes 552992 | tf_op jit(solution)/shard_map/ppermute | solution.py:32
  22.4 3.6 %fusion.52 = bf16[3,8,368,128]{3,2,1,0:T(8,128)(2,1)S(1)} fusion(bf16[3,2,360,128]{3,2,1,0:T(8,128)(2,1)} %collective-permute-done.1, bf16[3,4,360,128]{3,2,1,0:T(8,128)(2,1)S(1)} %fusion.56, bf16[3,2,360,128]{3,2,1,0:T(8,128)(2,1)} %collective-permute-done), kind=kLoop, calls=%fused_computation.163 | loop fusion | flops 20348928 | bytes 4472832 | tf_op jit(solution)/shard_map/concatenate | solution.py:50
  26.2 84.8 %while.32 = (s32[]{:T(128)}, bf16[3,4,360,128]{3,2,0,1:T(8,128)(2,1)S(1)}, f32[4,8,4]{2,1,0:T(8,128)S(1)}, s32[4,8]{1,0:T(4,128)S(1)}, s32[4,8]{1,0:T(4,128)S(1)...) while((s32[]{:T(128)}, ...), condition=%wide.region_2.3_spmd, body=%wide.region_1.2_spmd.sunk | while | flops 151649360 | bytes 47967780 | solution.py:73
  112.4 5.7 %collective-permute-start.2 = (bf16[4,360,128]{2,1,0:T(8,128)(2,1)S(1)}, bf16[4,360,128]{2,1,0:T(8,128)(2,1)S(1)}, u32[]{:S(2)}, u32[]{:S(2)}) collective-permute-start(bf16[4,360,128]{2,1,0:T(8,128)(2,1)S(1)} %dynamic-slice_bitcast_fusion.1), channel_id=1, source_target_pairs={{0,64},{64,128},{128,192},{1,65},{65,129},{129,193},{2,66},{66,130... | collective-permute-start | bytes 1105928 | tf_op jit(solution)/shard_map/ppermute | solution.py:19
  118.3 5.1 %collective-permute-done.3 = bf16[4,360,128]{2,1,0:T(8,128)(2,1)S(1)} collective-permute-done((bf16[4,360,128]{2,1,0:T(8,128)(2,1)S(1)}, bf16[4,360,128]{2,1,0:T(8,128)(2,1)S(1)}, u32[]{:S(2)}, u32[]{:S(2)}) %collective-permute-start.3) | collective-permute-done | bytes 368672 | tf_op jit(solution)/shard_map/ppermute | solution.py:19
  123.6 9.5 %collective-permute-done.2 = bf16[4,360,128]{2,1,0:T(8,128)(2,1)S(1)} collective-permute-done((bf16[4,360,128]{2,1,0:T(8,128)(2,1)S(1)}, bf16[4,360,128]{2,1,0:T(8,128)(2,1)S(1)}, u32[]{:S(2)}, u32[]{:S(2)}) %collective-permute-start.2) | collective-permute-done | bytes 368672 | tf_op jit(solution)/shard_map/ppermute | solution.py:19
  133.1 7.1 %fusion.61 = (f32[3,4,360]{2,1,0:T(4,128)S(1)}, bf16[3,4,360,128]{3,2,1,0:T(8,128)(2,1)S(1)}) fusion(bf16[2,384,128]{2,1,0:T(8,128)(2,1)S(1)} %copy-done.8, bf16[3,4,360,128]{3,2,1,0:T(8,128)(2,1)S(1)} %maximum_select_fusion, bf16[2,4,360,128]{3,2,1,0:T(8,128)(2,1)S(1)} %get-tuple-element.563, bf16[1,4,360,128]{3,2,1,0:T(8,128)(2,1)S(1)} %bitcast.553, ...), kind=kOutput, calls=%fused_computation.175 | convolution fusion | flops 477200160 | bytes 5645696 | tf_op jit(solution)/shard_map/dot_general | solution.py:87
  141.2 1.9 collective-permute-start.4
  143.1 2.6 collective-permute-start.5
  145.7 6.4 %collective-permute-done.4 = bf16[3,2,360,128]{3,2,1,0:T(8,128)(2,1)S(1)} collective-permute-done((bf16[3,2,360,128]{3,2,1,0:T(8,128)(2,1)S(1)}, bf16[3,2,360,128]{3,2,1,0:T(8,128)(2,1)S(1)}, u32[]{:S(2)}, u32[]{:S(2)}) %collective-permute-start.4) | collective-permute-done | bytes 552992 | tf_op jit(solution)/shard_map/ppermute | solution.py:30
  153.0 5.1 %collective-permute-done.5 = bf16[3,2,360,128]{3,2,1,0:T(8,128)(2,1)} collective-permute-done((bf16[3,2,360,128]{3,2,1,0:T(8,128)(2,1)S(1)}, bf16[3,2,360,128]{3,2,1,0:T(8,128)(2,1)}, u32[]{:S(2)}, u32[]{:S(2)}) %collective-permute-start.5) | collective-permute-done | bytes 552992 | tf_op jit(solution)/shard_map/ppermute | solution.py:32
  158.1 3.6 %fusion.50 = bf16[3,8,368,128]{3,2,1,0:T(8,128)(2,1)S(1)} fusion(bf16[3,2,360,128]{3,2,1,0:T(8,128)(2,1)} %collective-permute-done.5, bf16[3,4,360,128]{3,2,1,0:T(8,128)(2,1)S(1)} %fusion.63, bf16[3,2,360,128]{3,2,1,0:T(8,128)(2,1)} %copy-done.4), kind=kLoop, calls=%fused_computation.157 | loop fusion | flops 20348928 | bytes 4472832 | tf_op jit(solution)/shard_map/concatenate | solution.py:50
  161.9 84.8 %while.33 = (s32[]{:T(128)}, bf16[3,4,360,128]{3,2,0,1:T(8,128)(2,1)S(1)}, f32[4,8,4]{2,1,0:T(8,128)S(1)}, s32[4,8]{1,0:T(4,128)S(1)}, s32[4,8]{1,0:T(4,128)S(1)...) while((s32[]{:T(128)}, ...), condition=%wide.region_5.6_spmd, body=%wide.region_4.5_spmd.sunk | while | flops 151649360 | bytes 47443464 | solution.py:73
  181.3 1.7 convolution_convert_fusion.5
  223.7 1.7 convolution_convert_fusion.5
  244.9 1.7 convolution_convert_fusion.5
  248.1 5.8 %collective-permute-start.6 = (bf16[4,360,128]{2,1,0:T(8,128)(2,1)S(1)}, bf16[4,360,128]{2,1,0:T(8,128)(2,1)S(1)}, u32[]{:S(2)}, u32[]{:S(2)}) collective-permute-start(bf16[4,360,128]{2,1,0:T(8,128)(2,1)S(1)} %dynamic-slice_bitcast_fusion), channel_id=1, source_target_pairs={{0,64},{64,128},{128,192},{1,65},{65,129},{129,193},{2,66},{66,130... | collective-permute-start | bytes 1105928 | tf_op jit(solution)/shard_map/ppermute | solution.py:19
  254.1 6.0 %collective-permute-done.7 = bf16[4,360,128]{2,1,0:T(8,128)(2,1)S(1)} collective-permute-done((bf16[4,360,128]{2,1,0:T(8,128)(2,1)S(1)}, bf16[4,360,128]{2,1,0:T(8,128)(2,1)S(1)}, u32[]{:S(2)}, u32[]{:S(2)}) %collective-permute-start.7) | collective-permute-done | bytes 368672 | tf_op jit(solution)/shard_map/ppermute | solution.py:19
  260.2 9.5 %collective-permute-done.6 = bf16[4,360,128]{2,1,0:T(8,128)(2,1)S(1)} collective-permute-done((bf16[4,360,128]{2,1,0:T(8,128)(2,1)S(1)}, bf16[4,360,128]{2,1,0:T(8,128)(2,1)S(1)}, u32[]{:S(2)}, u32[]{:S(2)}) %collective-permute-start.6) | collective-permute-done | bytes 368672 | tf_op jit(solution)/shard_map/ppermute | solution.py:19
  269.7 6.9 %fusion.65 = bf16[3,4,360,128]{3,2,1,0:T(8,128)(2,1)} fusion(bf16[3,4,360,128]{3,2,1,0:T(8,128)(2,1)S(1)} %copy-done.3, pred[3]{0:T(512)(128)(4,1)S(1)} %get-tuple-element.576, bf16[3,4,360,128]{3,2,1,0:T(8,128)(2,1)S(1)} %maximum_select_fusion.1, bf16[2,4,360,128]{3,2,1,0:T(8,128)(2,1)S(1)} %get-tuple-element.559, ...), kind=kOutput, calls=%fused_computation.179 | convolution fusion | flops 475545600 | bytes 5628416 | tf_op jit(solution)/shard_map/dot_general | solution.py:87
  (188 shorter events, 57.8 us)
Async XLA Ops:
  2.7 7.1 %copy-start.6 = (s32[256,8]{0,1:T(8,128)S(1)}, s32[256,8]{0,1:T(8,128)}, u32[]{:S(2)}) copy-start(s32[256,8]{0,1:T(8,128)} %param.14) | copy-start | bytes 24580
  2.7 7.3 %copy-start.7 = (s32[256,8]{0,1:T(8,128)S(1)}, s32[256,8]{0,1:T(8,128)}, u32[]{:S(2)}) copy-start(s32[256,8]{0,1:T(8,128)} %param.15) | copy-start | bytes 24580
  2.7 8.0 %copy-start.5 = (f32[256,8,4]{0,2,1:T(4,128)S(1)}, f32[256,8,4]{0,2,1:T(4,128)}, u32[]{:S(2)}) copy-start(f32[256,8,4]{0,2,1:T(4,128)} %param.16) | copy-start | bytes 98308
  4.6 6.7 %copy-start.10 = (s32[4]{0:T(128)S(1)}, s32[4]{0:T(128)}, u32[]{:S(2)}) copy-start(s32[4]{0:T(128)} %param.13) | copy-start | bytes 52
  4.7 12.3 %collective-permute-start = (bf16[3,2,360,128]{3,2,1,0:T(8,128)(2,1)S(1)}, bf16[3,2,360,128]{3,2,1,0:T(8,128)(2,1)}, u32[]{:S(2)}, u32[]{:S(2)}) collective-permute-start(bf16[3,2,360,128]{3,2,1,0:T(8,128)(2,1)S(1)} %get-tuple-element.565), channel_id=1, source_target_pairs={{0,1},{1,2},{2,3},{3,4},{4,5},{5,6},{6,7},{7,8},{8,9},{9,10},{10,1... | collective-permute-start | bytes 1658888 | tf_op jit(solution)/shard_map/ppermute | solution.py:30
  7.9 14.5 %collective-permute-start.1 = (bf16[3,2,360,128]{3,2,1,0:T(8,128)(2,1)S(1)}, bf16[3,2,360,128]{3,2,1,0:T(8,128)(2,1)}, u32[]{:S(2)}, u32[]{:S(2)}) collective-permute-start(bf16[3,2,360,128]{3,2,1,0:T(8,128)(2,1)S(1)} %get-tuple-element.566), channel_id=1, source_target_pairs={{1,0},{2,1},{3,2},{4,3},{5,4},{6,5},{7,6},{8,7},{9,8},{10,9},{11,1... | collective-permute-start | bytes 1658888 | tf_op jit(solution)/shard_map/ppermute | solution.py:32
  44.6 1.1 copy-start
  65.8 1.1 copy-start
  87.0 1.1 copy-start
  108.2 1.1 copy-start
  111.1 12.3 %collective-permute-start.3 = (bf16[4,360,128]{2,1,0:T(8,128)(2,1)S(1)}, bf16[4,360,128]{2,1,0:T(8,128)(2,1)S(1)}, u32[]{:S(2)}, u32[]{:S(2)}) collective-permute-start(bf16[4,360,128]{2,1,0:T(8,128)(2,1)S(1)} %slice_bitcast_fusion.1), channel_id=1, source_target_pairs={{64,0},{128,64},{192,128},{65,1},{129,65},{193,129},{66,2},{130,66... | collective-permute-start | bytes 1105928 | tf_op jit(solution)/shard_map/ppermute | solution.py:19
  112.4 20.7 %copy-start.1 = (bf16[3,4,360,128]{3,2,1,0:T(8,128)(2,1)S(1)}, bf16[3,4,360,128]{3,2,1,0:T(8,128)(2,1)}, u32[]{:S(2)}) copy-start(bf16[3,4,360,128]{3,2,1,0:T(8,128)(2,1)} %param.12) | copy-start | bytes 3317764
  112.4 20.7 %copy-start.8 = (bf16[2,384,128]{2,1,0:T(8,128)(2,1)S(1)}, bf16[2,384,128]{2,1,0:T(8,128)(2,1)}, u32[]{:S(2)}) copy-start(bf16[2,384,128]{2,1,0:T(8,128)(2,1)} %param.19) | copy-start | bytes 589828
  112.4 20.7 %collective-permute-start.2 = (bf16[4,360,128]{2,1,0:T(8,128)(2,1)S(1)}, bf16[4,360,128]{2,1,0:T(8,128)(2,1)S(1)}, u32[]{:S(2)}, u32[]{:S(2)}) collective-permute-start(bf16[4,360,128]{2,1,0:T(8,128)(2,1)S(1)} %dynamic-slice_bitcast_fusion.1), channel_id=1, source_target_pairs={{0,64},{64,128},{128,192},{1,65},{65,129},{129,193},{2,66},{66,130... | collective-permute-start | bytes 1105928 | tf_op jit(solution)/shard_map/ppermute | solution.py:19
  140.2 1.0 copy-start.2
  141.2 11.0 %collective-permute-start.4 = (bf16[3,2,360,128]{3,2,1,0:T(8,128)(2,1)S(1)}, bf16[3,2,360,128]{3,2,1,0:T(8,128)(2,1)S(1)}, u32[]{:S(2)}, u32[]{:S(2)}) collective-permute-start(bf16[3,2,360,128]{3,2,1,0:T(8,128)(2,1)S(1)} %get-tuple-element.561), channel_id=1, source_target_pairs={{0,1},{1,2},{2,3},{3,4},{4,5},{5,6},{6,7},{7,8},{8,9},{9,10},{10,1... | collective-permute-start | bytes 1658888 | tf_op jit(solution)/shard_map/ppermute | solution.py:30
  143.1 15.0 %collective-permute-start.5 = (bf16[3,2,360,128]{3,2,1,0:T(8,128)(2,1)S(1)}, bf16[3,2,360,128]{3,2,1,0:T(8,128)(2,1)}, u32[]{:S(2)}, u32[]{:S(2)}) collective-permute-start(bf16[3,2,360,128]{3,2,1,0:T(8,128)(2,1)S(1)} %get-tuple-element.562), channel_id=1, source_target_pairs={{1,0},{2,1},{3,2},{4,3},{5,4},{6,5},{7,6},{8,7},{9,8},{10,9},{11,1... | collective-permute-start | bytes 1658888 | tf_op jit(solution)/shard_map/ppermute | solution.py:32
  152.2 0.8 copy-start.4
  246.7 13.3 %collective-permute-start.7 = (bf16[4,360,128]{2,1,0:T(8,128)(2,1)S(1)}, bf16[4,360,128]{2,1,0:T(8,128)(2,1)S(1)}, u32[]{:S(2)}, u32[]{:S(2)}) collective-permute-start(bf16[4,360,128]{2,1,0:T(8,128)(2,1)S(1)} %slice_bitcast_fusion), channel_id=1, source_target_pairs={{64,0},{128,64},{192,128},{65,1},{129,65},{193,129},{66,2},{130,66... | collective-permute-start | bytes 1105928 | tf_op jit(solution)/shard_map/ppermute | solution.py:19
  248.0 21.7 %copy-start.3 = (bf16[3,4,360,128]{3,2,1,0:T(8,128)(2,1)S(1)}, bf16[3,4,360,128]{3,2,1,0:T(8,128)(2,1)}, u32[]{:S(2)}) copy-start(bf16[3,4,360,128]{3,2,1,0:T(8,128)(2,1)} %copy-done.2) | copy-start | bytes 3317764
  248.1 21.7 %copy-start.9 = (bf16[2,384,128]{2,1,0:T(8,128)(2,1)S(1)}, bf16[2,384,128]{2,1,0:T(8,128)(2,1)}, u32[]{:S(2)}) copy-start(bf16[2,384,128]{2,1,0:T(8,128)(2,1)} %param.19) | copy-start | bytes 589828
  248.1 21.7 %collective-permute-start.6 = (bf16[4,360,128]{2,1,0:T(8,128)(2,1)S(1)}, bf16[4,360,128]{2,1,0:T(8,128)(2,1)S(1)}, u32[]{:S(2)}, u32[]{:S(2)}) collective-permute-start(bf16[4,360,128]{2,1,0:T(8,128)(2,1)S(1)} %dynamic-slice_bitcast_fusion), channel_id=1, source_target_pairs={{0,64},{64,128},{128,192},{1,65},{65,129},{129,193},{2,66},{66,130... | collective-permute-start | bytes 1105928 | tf_op jit(solution)/shard_map/ppermute | solution.py:19
where the time goes:
time: 282 us; the launch traced here: 277 us
  loops' own time  119 us (42%)
  waiting for transfers between devices  47.9 us (17%)
  local copies, waits for them, and re-layouts  39.7 us (14%)
  matrix products  27.5 us (10%)
  starting transfers between devices  23.8 us (8%)
  other arithmetic  17.3 us (6%)
    another operation x2, loops' own time, filter_band(): return lax.fori_loop(0, row_count, one_row, output)  119 us
    ppermute x4, waiting for transfers between devices, from_behind(): return lax.ppermute(block, axis, route)  30.1 us
    mul x104, local copies, waits for them, and re-layouts, one_row(): factors[None, None, :, None]  26.7 us
    ppermute x4, starting transfers between devices, from_behind(): return lax.ppermute(block, axis, route)  14.1 us
    dot_general x2, matrix products, mix_levels(): jnp.dot(stacked.reshape(-1, 3 * channels), vertical_weight, preferred_ele...  14 us
    dot_general x8, matrix products, one_row(): mixed = jnp.dot(filtered, weight, preferred_element_type=jnp.float32)  13.5 us
    ppermute x2, waiting for transfers between devices, with_halo(): lax.ppermute(head, axis, [((i + 1) % count, i) for i in range(ends)])  10.5 us
    ppermute x2, waiting for transfers between devices, with_halo(): lax.ppermute(tail, axis, [(i, (i + 1) % count) for i in range(ends)])  7.26 us
  transfers between devices with their start and end apart: 8, of which 8 were waited for; matrix products, arithmetic and copies ran while one was open for 2% of the time, Pallas kernels for 0%

commit v1 on v0

v1 whole, which is shorter than its diff:
```python
import jax
import jax.numpy as jnp
from jax import lax
from jax.experimental import pallas as pl
from jax.experimental.pallas import tpu as pltpu
from jax.sharding import PartitionSpec as P

K = 4
TAPS = 8
H = 2
PASSES = 2
PAD = 8
EPSILON = 1e-06

BF16 = jnp.bfloat16
F32 = jnp.float32
VMEM = pl.BlockSpec(memory_space=pltpu.VMEM)
SMEM = pl.BlockSpec(memory_space=pltpu.SMEM)
LIMIT = 24 * 1024 * 1024


def call(kernel, out_shape, in_specs, scratch=(), flops=0, nbytes=0):
    many = isinstance(out_shape, (tuple, list))
    return pl.pallas_call(
        kernel,
        out_shape=out_shape,
        in_specs=in_specs,
        out_specs=[VMEM] * len(out_shape) if many else VMEM,
        scratch_shapes=list(scratch),
        compiler_params=pltpu.CompilerParams(vmem_limit_bytes=LIMIT),
        cost_estimate=pl.CostEstimate(flops=flops, bytes_accessed=nbytes, transcendentals=0),
    )


def normed(widened, gain):
    mean_square = jnp.mean(widened * widened, axis=-1, keepdims=True)
    return widened * lax.rsqrt(mean_square + EPSILON) * gain


def norm_kernel(field, gain, head, tail):
    slots, rows = field.shape[:2]
    for slot in range(slots):
        for row in range(rows):
            value = normed(field[slot, row].astype(F32), gain[0:1, :]).astype(BF16)
            if row < H:
                head[slot, row] = value
            else:
                tail[slot, row - H] = value


def tap_map_kernel(values, weight, *outs):
    channels = weight.shape[-1]
    rows = values.shape[0]
    for p in range(PASSES):

        def one(index, carry, p=p):
            row = index // TAPS
            tap = index % TAPS
            total = None
            for k in range(K):
                part = values[row, tap * K + k] * weight[p, k * channels : (k + 1) * channels, :].astype(F32)
                total = part if total is None else total + part
            outs[p][row, pl.ds(pl.multiple_of(tap * channels, channels), channels), :] = total.astype(BF16)
            return carry

        lax.fori_loop(0, rows * TAPS, one, 0)


def stage(scratch, place, slot, head, tail, low, high):
    lons = head.shape[2]
    for row, (ref, at) in enumerate(
        [(low, 0), (low, 1), (head, 0), (head, 1), (tail, 0), (tail, 1), (high, 0), (high, 1)]
    ):
        value = ref[slot, at].astype(F32)
        scratch[place, row, pl.ds(PAD, lons), :] = value
        scratch[place, row, pl.ds(0, PAD), :] = value[lons - PAD :]
        scratch[place, row, pl.ds(PAD + lons, PAD), :] = value[:PAD]


def disco_rows(scratch, place, row_table, lon_table, weights, out):
    rows, lons = out.shape[0], out.shape[1]

    def one(row, carry):
        parts = []
        for tap in range(TAPS):
            source = row + row_table[row, tap] + H
            start = lon_table[row, tap] + PAD
            parts.append(scratch[place, source, pl.ds(start, lons), :].astype(BF16))
        lhs = jnp.concatenate(parts, axis=1)
        total = jnp.dot(lhs, weights[row], preferred_element_type=F32)
        out[row] = total.astype(BF16)
        return carry

    lax.fori_loop(0, rows, one, 0)


def ends_kernel(count, row_table, lon_table, head, tail, low, high, weights, bottom, top, scratch):
    last = count[0] - 1
    stage(scratch, 0, 0, head, tail, low, high)
    stage(scratch, 1, last, head, tail, low, high)
    disco_rows(scratch, 0, row_table, lon_table, weights, bottom)
    disco_rows(scratch, 1, row_table, lon_table, weights, top)


def middle_kernel(row_table, lon_table, head, tail, low, high, weights, middle, scratch):
    stage(scratch, 0, 1, head, tail, low, high)
    disco_rows(scratch, 0, row_table, lon_table, weights, middle)


def erf(x):
    return lax.erf(x)


def gelu(v):
    return 0.5 * v * (1.0 + erf(v * 0.7071067811865476))


def mix(below, disco, above, weight):
    stacked = jnp.concatenate([below, disco, above], axis=1)
    return gelu(jnp.dot(stacked, weight[...], preferred_element_type=F32))


def mix_rows(count, current, bottom, middle, top, from_below, from_above, weight, put):
    rows = current.shape[1]
    own = count[0]

    def one(row, carry):
        b, m, t = bottom[row], middle[row], top[row]
        lo, hi = from_below[row], from_above[row]
        three, two, single = own == 3, own == 2, own == 1
        first = mix(lo, b, jnp.where(single, hi, jnp.where(two, t, m)), weight)
        last = mix(jnp.where(single, lo, jnp.where(two, b, m)), t, hi, weight)
        inner = mix(b, m, t, weight)
        x0 = current[0, row].astype(F32) + first
        x1 = current[1, row].astype(F32) + jnp.where(three, inner, last)
        x2 = current[2, row].astype(F32) + last
        put(0, row, x0.astype(BF16))
        put(1, row, jnp.where(own >= 2, x1, 0.0).astype(BF16))
        put(2, row, jnp.where(three, x2, 0.0).astype(BF16))
        return carry

    lax.fori_loop(0, rows, one, 0)


def inner_mix_kernel(count, current, bottom, middle, top, from_below, from_above, weight, gain, out, head, tail):
    rows = current.shape[1]

    def put(slot, row, value):
        out[slot, row] = value

    mix_rows(count, current, bottom, middle, top, from_below, from_above, weight, put)
    for slot in range(current.shape[0]):
        for row in range(rows):
            value = normed(out[slot, row].astype(F32), gain[0:1, :]).astype(BF16)
            if row < H:
                head[slot, row] = value
            else:
                tail[slot, row - H] = value


def last_mix_kernel(count, current, bottom, middle, top, from_below, from_above, weight, out):
    def put(slot, row, value):
        out[slot, row] = value

    mix_rows(count, current, bottom, middle, top, from_below, from_above, weight, put)


def on_device(field, level_count, tap_rows, tap_lons, tap_values, norm_gain, disco_weight, vert_weight):
    slots, rows, lons, channels = field.shape
    first_row = lax.axis_index("lat") * rows
    count = lax.dynamic_slice_in_dim(level_count, lax.axis_index("lev"), 1, 0)
    row_part = lax.dynamic_slice_in_dim(tap_rows, first_row, rows, 0)
    lon_part = lax.dynamic_slice_in_dim(tap_lons, first_row, rows, 0)
    value_part = lax.dynamic_slice_in_dim(tap_values, first_row, rows, 0).reshape(rows, TAPS * K)
    lats = lax.axis_size("lat")
    levs = lax.axis_size("lev")
    up = [(i, i + 1) for i in range(lats - 1)]
    down = [(i + 1, i) for i in range(lats - 1)]
    level_up = [(i, i + 1) for i in range(levs - 1)]
    level_down = [(i + 1, i) for i in range(levs - 1)]

    edge = jax.ShapeDtypeStruct((slots, H, lons, channels), BF16)
    plane = jax.ShapeDtypeStruct((rows, lons, channels), BF16)
    whole = jax.ShapeDtypeStruct(field.shape, BF16)
    padded = lons + 2 * PAD

    head, tail = call(norm_kernel, [edge, edge], [VMEM, VMEM], nbytes=2 * field.size * 2)(field, norm_gain[0:1])
    maps = call(
        tap_map_kernel,
        [jax.ShapeDtypeStruct((rows, TAPS * channels, channels), BF16)] * PASSES,
        [SMEM, VMEM],
        flops=8 * PASSES * rows * TAPS * channels * channels,
        nbytes=1 << 21,
    )(value_part, disco_weight)
    current = field
    for p in range(PASSES):
        low = lax.ppermute(tail, "lat", up)
        high = lax.ppermute(head, "lat", down)
        dots = 2 * rows * lons * TAPS * channels * channels
        bottom, top = call(
            ends_kernel,
            [plane, plane],
            [SMEM, SMEM, SMEM, VMEM, VMEM, VMEM, VMEM, VMEM],
            [pltpu.VMEM((2, rows + 2 * H, padded, channels), F32)],
            flops=2 * dots,
            nbytes=1 << 22,
        )(count, row_part, lon_part, head, tail, low, high, maps[p])
        from_below = lax.ppermute(top, "lev", level_up)
        from_above = lax.ppermute(bottom, "lev", level_down)
        middle = call(
            middle_kernel,
            plane,
            [SMEM, SMEM, VMEM, VMEM, VMEM, VMEM, VMEM],
            [pltpu.VMEM((1, rows + 2 * H, padded, channels), F32)],
            flops=dots,
            nbytes=1 << 22,
        )(row_part, lon_part, head, tail, low, high, maps[p])
        operands = (count, current, bottom, middle, top, from_below, from_above, vert_weight[p])
        specs = [SMEM] + [VMEM] * 7
        if p + 1 < PASSES:
            current, head, tail = call(inner_mix_kernel, [whole, edge, edge], specs + [VMEM], flops=dots, nbytes=1 << 22)(
                *operands, norm_gain[p + 1 : p + 2]
            )
        else:
            current = call(last_mix_kernel, whole, specs, flops=dots, nbytes=1 << 22)(*operands)
    return current


def solution(mesh):
    return jax.shard_map(
        on_device,
        mesh=mesh,
        in_specs=(P("lev", "lat", None, None), P(), P(), P(), P(), P(), P(), P()),
        out_specs=P("lev", "lat", None, None),
        check_vma=False,
    )
```

time: 282 us -> 106 us (0.38); the launches traced: 277 us -> 105 us
  loops' own time: 119 us -> 0 us
  local copies, waits for them, and re-layouts: 39.7 us -> 3.1 us
  matrix products: 27.5 us -> 0 us
  Pallas kernels: 0 us -> 23.7 us
  other arithmetic: 17.3 us -> 0 us
  starting transfers between devices: 23.8 us -> 29.7 us
    another operation x2 -> x0, loops' own time: 119 us -> none  [filter_band(): return lax.fori_loop(0, row_count, one_row, output)]
    dot_general x10 -> x0, matrix products: 27.5 us -> none  [the longest x2 14 us: mix_levels(): jnp.dot(stacked.reshape(-1, 3 * channels), vertical_weight, preferred_ele...]
    mul x105 -> x0, local copies, waits for them, and re-layouts: 27.5 us -> none  [the longest x104 26.7 us: one_row(): factors[None, None, :, None]]
    pallas_call x0 -> x8, Pallas kernels: none -> 23.7 us  [the longest x2 8.98 us: on_device(): call(ends_kernel, [plane, plane], [SMEM, SMEM, SMEM, VMEM, VMEM, VMEM, VM...]
    concatenate x2 -> x0, other arithmetic: 7.25 us -> none  [filter_band(): jnp.concatenate([padded[:, :, lon_count - WLON:], padded, padded[:, :, :W...]
    convert_element_type x10 -> x0, other arithmetic: 7.03 us -> none  [the longest x8 4.45 us: one_row(): picked[:, 0].astype(jnp.float32)[:, :, None, :]]
    dynamic_slice x11 -> x3, local copies, waits for them, and re-layouts: 7.03 us -> 0.81 us  [the longest x1 0.66 us: on_device(): count = lax.dynamic_slice_in_dim(level_count, lax.axis_index('lev'), 1, 0)]
    ppermute x8, starting transfers between devices: 23.8 us -> 29.7 us  [the longest x2 11.7 us: on_device(): low = lax.ppermute(tail, 'lat', up)]
  transfers between devices with their start and end apart: 8 -> 8, of which waited for: 8 -> 7; matrix products, arithmetic and copies ran while one was open for 2% -> 1% of each run, Pallas kernels for 0% -> 7%
where the time goes in v1:
time: 106 us; the launch traced here: 105 us
  waiting for transfers between devices  48.3 us (46%)
  starting transfers between devices  29.7 us (28%)
  Pallas kernels  23.7 us (22%)
  local copies, waits for them, and re-layouts  3.1 us (3%)
    ppermute x2, waiting for transfers between devices, on_device(): from_below = lax.ppermute(top, 'lev', level_up)  23.3 us
    ppermute x2, starting transfers between devices, on_device(): low = lax.ppermute(tail, 'lat', up)  11.7 us
    ppermute x2, starting transfers between devices, on_device(): from_below = lax.ppermute(top, 'lev', level_up)  11.5 us
    ppermute x2, waiting for transfers between devices, on_device(): low = lax.ppermute(tail, 'lat', up)  10 us
    ppermute x2, waiting for transfers between devices, on_device(): high = lax.ppermute(head, 'lat', down)  10 us
    pallas_call x2, Pallas kernels, on_device(): call(ends_kernel, [plane, plane], [SMEM, SMEM, SMEM, VMEM, VMEM, VMEM, VM...  8.98 us
    ppermute x2, waiting for transfers between devices, on_device(): from_above = lax.ppermute(bottom, 'lev', level_down)  4.98 us
    pallas_call x2, Pallas kernels, on_device(): call(middle_kernel, plane, [SMEM, SMEM, VMEM, VMEM, VMEM, VMEM, VMEM], [p...  4.44 us
  transfers between devices with their start and end apart: 8, of which 7 were waited for; matrix products, arithmetic and copies ran while one was open for 1% of the time, Pallas kernels for 7%

profile of v1, /device:TPU:49, one launch (start us, length us, event | category | flops | bytes accessed | tf_op | source)
XLA Modules:
  0.0 105.0 jit_solution(970541505573365024)
XLA Ops:
  0.0 0.8 fusion
  0.8 1.2 %copy-done.1 = bf16[3,4,360,128]{3,2,1,0:T(8,128)(2,1)S(1)} copy-done((bf16[3,4,360,128]{3,2,1,0:T(8,128)(2,1)S(1)}, bf16[3,4,360,128]{3,2,1,0:T(8,128)(2,1)}, u32[]{:S(2)}) %copy-start.1) | copy-done | bytes 1105944
  2.7 3.2 %collective-permute-start = (bf16[3,2,360,128]{3,2,1,0:T(8,128)(2,1)S(1)}, bf16[3,2,360,128]{3,2,1,0:T(8,128)(2,1)S(1)}, u32[]{:S(2)}, u32[]{:S(2)}) collective-permute-start(bf16[3,2,360,128]{3,2,1,0:T(8,128)(2,1)S(1)} %get-tuple-element.17.tail), channel_id=1, source_target_pairs={{0,1},{1,2},{2,3},{3,4},{4,5},{5,6},{6,7},{7,8},{8,9},{9,10},{10,1... | collective-permute-start | bytes 1658888 | tf_op jit(solution)/shard_map/ppermute | solution.py:197
  5.9 1.9 %collective-permute-start.1 = (bf16[3,2,360,128]{3,2,1,0:T(8,128)(2,1)S(1)}, bf16[3,2,360,128]{3,2,1,0:T(8,128)(2,1)S(1)}, u32[]{:S(2)}, u32[]{:S(2)}) collective-permute-start(bf16[3,2,360,128]{3,2,1,0:T(8,128)(2,1)S(1)} %get-tuple-element.16.head), channel_id=1, source_target_pairs={{1,0},{2,1},{3,2},{4,3},{5,4},{6,5},{7,6},{8,7},{9,8},{10,9},{11,1... | collective-permute-start | bytes 1658888 | tf_op jit(solution)/shard_map/ppermute | solution.py:198
  8.9 2.9 %shard_map.83 = (bf16[4,1024,128]{2,1,0:T(8,128)(2,1)S(1)}, bf16[4,1024,128]{2,1,0:T(8,128)(2,1)S(1)}) custom-call(f32[4,32]{1,0:T(4,128)S(1)} %copy.15.values, bf16[2,512,128]{2,1,0:T(8,128)(2,1)S(1)} %copy-done.3), custom_call_target="tpu_custom_call" | custom-call | flops 8388608 | bytes 2097152 | tf_op jit(solution)/shard_map/pallas_call | solution.py:188
  11.8 3.2 %collective-permute-done.low = bf16[3,2,360,128]{3,2,1,0:T(8,128)(2,1)S(1)} collective-permute-done((bf16[3,2,360,128]{3,2,1,0:T(8,128)(2,1)S(1)}, bf16[3,2,360,128]{3,2,1,0:T(8,128)(2,1)S(1)}, u32[]{:S(2)}, u32[]{:S(2)}) %collective-permute-start) | collective-permute-done | bytes 552992 | tf_op jit(solution)/shard_map/ppermute | solution.py:197
  15.0 5.3 %collective-permute-done.1.high = bf16[3,2,360,128]{3,2,1,0:T(8,128)(2,1)S(1)} collective-permute-done((bf16[3,2,360,128]{3,2,1,0:T(8,128)(2,1)S(1)}, bf16[3,2,360,128]{3,2,1,0:T(8,128)(2,1)S(1)}, u32[]{:S(2)}, u32[]{:S(2)}) %collective-permute-start.1) | collective-permute-done | bytes 552992 | tf_op jit(solution)/shard_map/ppermute | solution.py:198
  20.3 4.5 %shard_map.84 = (bf16[4,360,128]{2,1,0:T(8,128)(2,1)S(1)}, bf16[4,360,128]{2,1,0:T(8,128)(2,1)S(1)}) custom-call(s32[1]{0:T(128)} %dynamic_slice.12.count, s32[4,8]{1,0:T(4,128)S(1)} %copy.16.row_table, s32[4,8]{1,0:T(4,128)S(1)} %copy.17.lon_table, bf16[3,2,360,128]{3,2,1,0:T(8,128)(2,1)S(1)} %get-tuple-element.16.head, ...), custom_call_target="tpu_custom_call" | custom-call | flops 754974720 | bytes 4194304 | tf_op jit(solution)/shard_map/pallas_call | solution.py:200
  24.8 4.9 %collective-permute-start.2 = (bf16[4,360,128]{2,1,0:T(8,128)(2,1)S(1)}, bf16[4,360,128]{2,1,0:T(8,128)(2,1)S(1)}, u32[]{:S(2)}, u32[]{:S(2)}) collective-permute-start(bf16[4,360,128]{2,1,0:T(8,128)(2,1)S(1)} %get-tuple-element.20.top), channel_id=1, source_target_pairs={{0,64},{64,128},{128,192},{1,65},{65,129},{129,193},{2,66},{66,130... | collective-permute-start | bytes 1105928 | tf_op jit(solution)/shard_map/ppermute | solution.py:208
  29.8 1.3 %collective-permute-start.3 = (bf16[4,360,128]{2,1,0:T(8,128)(2,1)S(1)}, bf16[4,360,128]{2,1,0:T(8,128)(2,1)S(1)}, u32[]{:S(2)}, u32[]{:S(2)}) collective-permute-start(bf16[4,360,128]{2,1,0:T(8,128)(2,1)S(1)} %get-tuple-element.19.bottom), channel_id=1, source_target_pairs={{64,0},{128,64},{192,128},{65,1},{129,65},{193,129},{66,2},{130,66... | collective-permute-start | bytes 1105928 | tf_op jit(solution)/shard_map/ppermute | solution.py:209
  31.1 2.2 %shard_map.85.middle = bf16[4,360,128]{2,1,0:T(8,128)(2,1)S(1)} custom-call(s32[4,8]{1,0:T(4,128)S(1)} %copy.16.row_table, s32[4,8]{1,0:T(4,128)S(1)} %copy.17.lon_table, bf16[3,2,360,128]{3,2,1,0:T(8,128)(2,1)S(1)} %get-tuple-element.16.head, bf16[3,2,360,128]{3,2,1,0:T(8,128)(2,1)S(1)} %get-tuple-element.17.tail, ...), custom_call_target="tpu_custom_call" | custom-call | flops 377487360 | bytes 4194304 | tf_op jit(solution)/shard_map/pallas_call | solution.py:210
  33.3 11.5 %collective-permute-done.2.from_below = bf16[4,360,128]{2,1,0:T(8,128)(2,1)S(1)} collective-permute-done((bf16[4,360,128]{2,1,0:T(8,128)(2,1)S(1)}, bf16[4,360,128]{2,1,0:T(8,128)(2,1)S(1)}, u32[]{:S(2)}, u32[]{:S(2)}) %collective-permute-start.2) | collective-permute-done | bytes 368672 | tf_op jit(solution)/shard_map/ppermute | solution.py:208
  44.8 3.2 %shard_map.86 = (bf16[3,4,360,128]{3,2,1,0:T(8,128)(2,1)S(1)}, bf16[3,2,360,128]{3,2,1,0:T(8,128)(2,1)S(1)}, bf16[3,2,360,128]{3,2,1,0:T(8,128)(2,1)S(1)}) custom-call(s32[1]{0:T(128)} %dynamic_slice.12.count, bf16[3,4,360,128]{3,2,1,0:T(8,128)(2,1)S(1)} %copy-done.2, bf16[4,360,128]{2,1,0:T(8,128)(2,1)S(1)} %get-tuple-element.19.bottom, ...), custom_call_target="tpu_custom_call" | custom-call | flops 377487360 | bytes 4194304 | tf_op jit(solution)/shard_map/pallas_call | solution.py:221
  48.0 8.5 %collective-permute-start.4 = (bf16[3,2,360,128]{3,2,1,0:T(8,128)(2,1)S(1)}, bf16[3,2,360,128]{3,2,1,0:T(8,128)(2,1)S(1)}, u32[]{:S(2)}, u32[]{:S(2)}) collective-permute-start(bf16[3,2,360,128]{3,2,1,0:T(8,128)(2,1)S(1)} %get-tuple-element.23.tail), channel_id=1, source_target_pairs={{0,1},{1,2},{2,3},{3,4},{4,5},{5,6},{6,7},{7,8},{8,9},{9,10},{10,1... | collective-permute-start | bytes 1658888 | tf_op jit(solution)/shard_map/ppermute | solution.py:197
  56.6 1.9 %collective-permute-start.5 = (bf16[3,2,360,128]{3,2,1,0:T(8,128)(2,1)S(1)}, bf16[3,2,360,128]{3,2,1,0:T(8,128)(2,1)S(1)}, u32[]{:S(2)}, u32[]{:S(2)}) collective-permute-start(bf16[3,2,360,128]{3,2,1,0:T(8,128)(2,1)S(1)} %get-tuple-element.22.head), channel_id=1, source_target_pairs={{1,0},{2,1},{3,2},{4,3},{5,4},{6,5},{7,6},{8,7},{9,8},{10,9},{11,1... | collective-permute-start | bytes 1658888 | tf_op jit(solution)/shard_map/ppermute | solution.py:198
  58.5 6.9 %collective-permute-done.4.low = bf16[3,2,360,128]{3,2,1,0:T(8,128)(2,1)S(1)} collective-permute-done((bf16[3,2,360,128]{3,2,1,0:T(8,128)(2,1)S(1)}, bf16[3,2,360,128]{3,2,1,0:T(8,128)(2,1)S(1)}, u32[]{:S(2)}, u32[]{:S(2)}) %collective-permute-start.4) | collective-permute-done | bytes 552992 | tf_op jit(solution)/shard_map/ppermute | solution.py:197
  65.4 4.7 %collective-permute-done.5.high = bf16[3,2,360,128]{3,2,1,0:T(8,128)(2,1)S(1)} collective-permute-done((bf16[3,2,360,128]{3,2,1,0:T(8,128)(2,1)S(1)}, bf16[3,2,360,128]{3,2,1,0:T(8,128)(2,1)S(1)}, u32[]{:S(2)}, u32[]{:S(2)}) %collective-permute-start.5) | collective-permute-done | bytes 552992 | tf_op jit(solution)/shard_map/ppermute | solution.py:198
  70.0 4.5 %shard_map.87 = (bf16[4,360,128]{2,1,0:T(8,128)(2,1)S(1)}, bf16[4,360,128]{2,1,0:T(8,128)(2,1)S(1)}) custom-call(s32[1]{0:T(128)} %dynamic_slice.12.count, s32[4,8]{1,0:T(4,128)S(1)} %copy.16.row_table, s32[4,8]{1,0:T(4,128)S(1)} %copy.17.lon_table, bf16[3,2,360,128]{3,2,1,0:T(8,128)(2,1)S(1)} %get-tuple-element.22.head, ...), custom_call_target="tpu_custom_call" | custom-call | flops 754974720 | bytes 4194304 | tf_op jit(solution)/shard_map/pallas_call | solution.py:200
  74.5 6.6 %collective-permute-start.6 = (bf16[4,360,128]{2,1,0:T(8,128)(2,1)S(1)}, bf16[4,360,128]{2,1,0:T(8,128)(2,1)S(1)}, u32[]{:S(2)}, u32[]{:S(2)}) collective-permute-start(bf16[4,360,128]{2,1,0:T(8,128)(2,1)S(1)} %get-tuple-element.26.top), channel_id=1, source_target_pairs={{0,64},{64,128},{128,192},{1,65},{65,129},{129,193},{2,66},{66,130... | collective-permute-start | bytes 1105928 | tf_op jit(solution)/shard_map/ppermute | solution.py:208
  81.1 1.3 %collective-permute-start.7 = (bf16[4,360,128]{2,1,0:T(8,128)(2,1)S(1)}, bf16[4,360,128]{2,1,0:T(8,128)(2,1)S(1)}, u32[]{:S(2)}, u32[]{:S(2)}) collective-permute-start(bf16[4,360,128]{2,1,0:T(8,128)(2,1)S(1)} %get-tuple-element.25.bottom), channel_id=1, source_target_pairs={{64,0},{128,64},{192,128},{65,1},{129,65},{193,129},{66,2},{130,66... | collective-permute-start | bytes 1105928 | tf_op jit(solution)/shard_map/ppermute | solution.py:209
  82.4 2.2 %shard_map.88.middle = bf16[4,360,128]{2,1,0:T(8,128)(2,1)S(1)} custom-call(s32[4,8]{1,0:T(4,128)S(1)} %copy.16.row_table, s32[4,8]{1,0:T(4,128)S(1)} %copy.17.lon_table, bf16[3,2,360,128]{3,2,1,0:T(8,128)(2,1)S(1)} %get-tuple-element.22.head, bf16[3,2,360,128]{3,2,1,0:T(8,128)(2,1)S(1)} %get-tuple-element.23.tail, ...), custom_call_target="tpu_custom_call" | custom-call | flops 377487360 | bytes 4194304 | tf_op jit(solution)/shard_map/pallas_call | solution.py:210
  84.6 11.9 %collective-permute-done.6.from_below = bf16[4,360,128]{2,1,0:T(8,128)(2,1)S(1)} collective-permute-done((bf16[4,360,128]{2,1,0:T(8,128)(2,1)S(1)}, bf16[4,360,128]{2,1,0:T(8,128)(2,1)S(1)}, u32[]{:S(2)}, u32[]{:S(2)}) %collective-permute-start.6) | collective-permute-done | bytes 368672 | tf_op jit(solution)/shard_map/ppermute | solution.py:208
  96.5 5.0 %collective-permute-done.7.from_above = bf16[4,360,128]{2,1,0:T(8,128)(2,1)S(1)} collective-permute-done((bf16[4,360,128]{2,1,0:T(8,128)(2,1)S(1)}, bf16[4,360,128]{2,1,0:T(8,128)(2,1)S(1)}, u32[]{:S(2)}, u32[]{:S(2)}) %collective-permute-start.7) | collective-permute-done | bytes 368672 | tf_op jit(solution)/shard_map/ppermute | solution.py:209
  101.5 3.5 %shard_map.89 = bf16[3,4,360,128]{3,2,1,0:T(8,128)(2,1)} custom-call(s32[1]{0:T(128)} %dynamic_slice.12.count, bf16[3,4,360,128]{3,2,1,0:T(8,128)(2,1)S(1)} %get-tuple-element.21.current, bf16[4,360,128]{2,1,0:T(8,128)(2,1)S(1)} %get-tuple-element.25.bottom, bf16[4,360,128]{2,1,0:T(8,128)(2,1)S(1)} %shard_map.88.middle, ...), custom_call_target="tpu_custom_call" | custom-call | flops 377487360 | bytes 4194304 | tf_op jit(solution)/shard_map/pallas_call | solution.py:225
  (24 shorter events, 1.8 us)
Async XLA Ops:
  0.0 8.1 %copy-start = (f32[256,8,4]{0,2,1:T(4,128)S(1)}, f32[256,8,4]{0,2,1:T(4,128)}, u32[]{:S(2)}) copy-start(f32[256,8,4]{0,2,1:T(4,128)} %param.12) | copy-start | bytes 98308
  0.0 8.3 %copy-start.7 = (s32[4]{0:T(128)S(1)}, s32[4]{0:T(128)}, u32[]{:S(2)}) copy-start(s32[4]{0:T(128)} %param.9) | copy-start | bytes 52
  0.8 1.2 %copy-start.1 = (bf16[3,4,360,128]{3,2,1,0:T(8,128)(2,1)S(1)}, bf16[3,4,360,128]{3,2,1,0:T(8,128)(2,1)}, u32[]{:S(2)}) copy-start(bf16[3,4,360,128]{3,2,1,0:T(8,128)(2,1)} %current.1) | copy-start | bytes 3317764
  2.0 5.8 %copy-start.5 = (s32[256,8]{0,1:T(8,128)S(1)}, s32[256,8]{0,1:T(8,128)}, u32[]{:S(2)}) copy-start(s32[256,8]{0,1:T(8,128)} %param.11) | copy-start | bytes 24580
  2.0 5.8 %copy-start.6 = (s32[256,8]{0,1:T(8,128)S(1)}, s32[256,8]{0,1:T(8,128)}, u32[]{:S(2)}) copy-start(s32[256,8]{0,1:T(8,128)} %param.10) | copy-start | bytes 24580
  2.0 6.9 %copy-start.3 = (bf16[2,512,128]{2,1,0:T(8,128)(2,1)S(1)}, bf16[2,512,128]{2,1,0:T(8,128)(2,1)}, u32[]{:S(2)}) copy-start(bf16[2,512,128]{2,1,0:T(8,128)(2,1)} %weight.1) | copy-start | bytes 786436
  2.7 12.3 %collective-permute-start = (bf16[3,2,360,128]{3,2,1,0:T(8,128)(2,1)S(1)}, bf16[3,2,360,128]{3,2,1,0:T(8,128)(2,1)S(1)}, u32[]{:S(2)}, u32[]{:S(2)}) collective-permute-start(bf16[3,2,360,128]{3,2,1,0:T(8,128)(2,1)S(1)} %get-tuple-element.17.tail), channel_id=1, source_target_pairs={{0,1},{1,2},{2,3},{3,4},{4,5},{5,6},{6,7},{7,8},{8,9},{9,10},{10,1... | collective-permute-start | bytes 1658888 | tf_op jit(solution)/shard_map/ppermute | solution.py:197
  5.9 14.4 %collective-permute-start.1 = (bf16[3,2,360,128]{3,2,1,0:T(8,128)(2,1)S(1)}, bf16[3,2,360,128]{3,2,1,0:T(8,128)(2,1)S(1)}, u32[]{:S(2)}, u32[]{:S(2)}) collective-permute-start(bf16[3,2,360,128]{3,2,1,0:T(8,128)(2,1)S(1)} %get-tuple-element.16.head), channel_id=1, source_target_pairs={{1,0},{2,1},{3,2},{4,3},{5,4},{6,5},{7,6},{8,7},{9,8},{10,9},{11,1... | collective-permute-start | bytes 1658888 | tf_op jit(solution)/shard_map/ppermute | solution.py:198
  20.3 10.8 %copy-start.4 = (bf16[2,384,128]{2,1,0:T(8,128)(2,1)S(1)}, bf16[2,384,128]{2,1,0:T(8,128)(2,1)}, u32[]{:S(2)}) copy-start(bf16[2,384,128]{2,1,0:T(8,128)(2,1)} %param.15) | copy-start | bytes 589828
  24.8 20.0 %collective-permute-start.2 = (bf16[4,360,128]{2,1,0:T(8,128)(2,1)S(1)}, bf16[4,360,128]{2,1,0:T(8,128)(2,1)S(1)}, u32[]{:S(2)}, u32[]{:S(2)}) collective-permute-start(bf16[4,360,128]{2,1,0:T(8,128)(2,1)S(1)} %get-tuple-element.20.top), channel_id=1, source_target_pairs={{0,64},{64,128},{128,192},{1,65},{65,129},{129,193},{2,66},{66,130... | collective-permute-start | bytes 1105928 | tf_op jit(solution)/shard_map/ppermute | solution.py:208
  29.8 15.1 %collective-permute-start.3 = (bf16[4,360,128]{2,1,0:T(8,128)(2,1)S(1)}, bf16[4,360,128]{2,1,0:T(8,128)(2,1)S(1)}, u32[]{:S(2)}, u32[]{:S(2)}) collective-permute-start(bf16[4,360,128]{2,1,0:T(8,128)(2,1)S(1)} %get-tuple-element.19.bottom), channel_id=1, source_target_pairs={{64,0},{128,64},{192,128},{65,1},{129,65},{193,129},{66,2},{130,66... | collective-permute-start | bytes 1105928 | tf_op jit(solution)/shard_map/ppermute | solution.py:209
  31.1 13.7 %copy-start.2 = (bf16[3,4,360,128]{3,2,1,0:T(8,128)(2,1)S(1)}, bf16[3,4,360,128]{3,2,1,0:T(8,128)(2,1)}, u32[]{:S(2)}) copy-start(bf16[3,4,360,128]{3,2,1,0:T(8,128)(2,1)} %current.1) | copy-start | bytes 3317764
  48.0 17.3 %collective-permute-start.4 = (bf16[3,2,360,128]{3,2,1,0:T(8,128)(2,1)S(1)}, bf16[3,2,360,128]{3,2,1,0:T(8,128)(2,1)S(1)}, u32[]{:S(2)}, u32[]{:S(2)}) collective-permute-start(bf16[3,2,360,128]{3,2,1,0:T(8,128)(2,1)S(1)} %get-tuple-element.23.tail), channel_id=1, source_target_pairs={{0,1},{1,2},{2,3},{3,4},{4,5},{5,6},{6,7},{7,8},{8,9},{9,10},{10,1... | collective-permute-start | bytes 1658888 | tf_op jit(solution)/shard_map/ppermute | solution.py:197
  56.6 13.5 %collective-permute-start.5 = (bf16[3,2,360,128]{3,2,1,0:T(8,128)(2,1)S(1)}, bf16[3,2,360,128]{3,2,1,0:T(8,128)(2,1)S(1)}, u32[]{:S(2)}, u32[]{:S(2)}) collective-permute-start(bf16[3,2,360,128]{3,2,1,0:T(8,128)(2,1)S(1)} %get-tuple-element.22.head), channel_id=1, source_target_pairs={{1,0},{2,1},{3,2},{4,3},{5,4},{6,5},{7,6},{8,7},{9,8},{10,9},{11,1... | collective-permute-start | bytes 1658888 | tf_op jit(solution)/shard_map/ppermute | solution.py:198
  74.5 22.0 %collective-permute-start.6 = (bf16[4,360,128]{2,1,0:T(8,128)(2,1)S(1)}, bf16[4,360,128]{2,1,0:T(8,128)(2,1)S(1)}, u32[]{:S(2)}, u32[]{:S(2)}) collective-permute-start(bf16[4,360,128]{2,1,0:T(8,128)(2,1)S(1)} %get-tuple-element.26.top), channel_id=1, source_target_pairs={{0,64},{64,128},{128,192},{1,65},{65,129},{129,193},{2,66},{66,130... | collective-permute-start | bytes 1105928 | tf_op jit(solution)/shard_map/ppermute | solution.py:208
  81.1 20.4 %collective-permute-start.7 = (bf16[4,360,128]{2,1,0:T(8,128)(2,1)S(1)}, bf16[4,360,128]{2,1,0:T(8,128)(2,1)S(1)}, u32[]{:S(2)}, u32[]{:S(2)}) collective-permute-start(bf16[4,360,128]{2,1,0:T(8,128)(2,1)S(1)} %get-tuple-element.25.bottom), channel_id=1, source_target_pairs={{64,0},{128,64},{192,128},{65,1},{129,65},{193,129},{66,2},{130,66... | collective-permute-start | bytes 1105928 | tf_op jit(solution)/shard_map/ppermute | solution.py:209

commit v2 on v0

v2 whole, which is shorter than its diff:
```python
import functools

import jax
import jax.numpy as jnp
from jax import lax
from jax.experimental import pallas as pl
from jax.experimental.pallas import tpu as pltpu
from jax.sharding import PartitionSpec as P

K = 4
TAPS = 8
H = 2
PASSES = 2
PAD = 8
EPSILON = 1e-06

BF16 = jnp.bfloat16
F32 = jnp.float32
VMEM = pl.BlockSpec(memory_space=pltpu.VMEM)
SMEM = pl.BlockSpec(memory_space=pltpu.SMEM)
LIMIT = 24 * 1024 * 1024


def call(kernel, out_shape, in_specs, scratch=(), flops=0, nbytes=0, after=()):
    many = isinstance(out_shape, (tuple, list))
    count, late = len(in_specs), len(after)

    def body(*refs):
        kernel(*refs[:count], *refs[count + late :])

    made = pl.pallas_call(
        body,
        out_shape=out_shape,
        in_specs=list(in_specs) + [pl.BlockSpec(memory_space=pl.ANY)] * late,
        out_specs=[VMEM] * len(out_shape) if many else VMEM,
        scratch_shapes=list(scratch),
        compiler_params=pltpu.CompilerParams(vmem_limit_bytes=LIMIT),
        cost_estimate=pl.CostEstimate(flops=flops, bytes_accessed=nbytes, transcendentals=0),
    )
    return lambda *operands: made(*operands, *after)


def here(level_count):
    group = lax.axis_index("lev")
    own = level_count[group]
    return own, group % 2 == 1, lax.axis_index("lat") % 2


def plane_slots(own, group_odd):
    return jnp.where(group_odd, 0, own - 1), jnp.where(group_odd, own - 1, 0), 1


def far_row(lat_odd):
    return H * lat_odd


def near_row(lat_odd):
    return H * (1 - lat_odd)


def normed(widened, gain):
    mean_square = jnp.mean(widened * widened, axis=-1, keepdims=True)
    return (widened * lax.rsqrt(mean_square + EPSILON) * gain).astype(BF16)


def norm_kernel(level_count, field, gain, far, near):
    own, group_odd, lat_odd = here(level_count)
    for plane, slot in enumerate(plane_slots(own, group_odd)):
        for h in range(H):
            far[plane, h] = normed(field[slot, far_row(lat_odd) + h].astype(F32), gain[0:1, :])
            near[plane, h] = normed(field[slot, near_row(lat_odd) + h].astype(F32), gain[0:1, :])


def tap_map_kernel(values, weight, out):
    channels = weight.shape[-1]
    rows = values.shape[0]

    def one(index, carry):
        row = index // TAPS
        tap = index % TAPS
        total = None
        for k in range(K):
            part = values[row, tap * K + k] * weight[k * channels : (k + 1) * channels, :].astype(F32)
            total = part if total is None else total + part
        out[row, pl.ds(pl.multiple_of(tap * channels, channels), channels), :] = total.astype(BF16)
        return carry

    lax.fori_loop(0, rows * TAPS, one, 0)


def stage(scratch, place, refs, plane, firsts):
    for ref, first in zip(refs, firsts):
        lons = ref.shape[2]
        for h in range(H):
            value = ref[plane, h].astype(F32)
            scratch[place, first + h, pl.ds(PAD, lons), :] = value
            scratch[place, first + h, pl.ds(0, PAD), :] = value[lons - PAD :]
            scratch[place, first + h, pl.ds(PAD + lons, PAD), :] = value[:PAD]


def disco_kernel(planes, is_far, row_table, lon_table, far, near, got, weights, *rest):
    outs, scratch = rest[:-1], rest[-1]
    lat_odd = lax.axis_index("lat") % 2
    lons = far.shape[2]
    first = far_row(lat_odd) if is_far else near_row(lat_odd)
    got_first = 3 * H * lat_odd if is_far else 3 * H * (1 - lat_odd)
    for place, plane in enumerate(planes):
        stage(scratch, place, (far, near, got), plane, (H + far_row(lat_odd), H + near_row(lat_odd), got_first))

    def one(h, carry):
        row = first + h
        taps = [(row + row_table[row, tap] + H, lon_table[row, tap] + PAD) for tap in range(TAPS)]
        for place, out in enumerate(outs):
            parts = [scratch[place, source, pl.ds(start, lons), :].astype(BF16) for source, start in taps]
            total = jnp.dot(jnp.concatenate(parts, axis=1), weights[row], preferred_element_type=F32)
            out[h] = total.astype(BF16)
        return carry

    lax.fori_loop(0, H, one, 0)


def gelu(v):
    return 0.5 * v * (1.0 + lax.erf(v * 0.7071067811865476))


def mix(below, disco, above, weight):
    stacked = jnp.concatenate([below, disco, above], axis=1)
    return gelu(jnp.dot(stacked, weight[...], preferred_element_type=F32))


def mixed(h, own, group_odd, one, two, middle, got_one, got_two, weight):
    a, b, m = one[h], two[h], middle[h]
    for_one, for_two = got_one[h], got_two[h]
    three, single = own == 3, own == 1
    bottom, top = jnp.where(group_odd, a, b), jnp.where(group_odd, b, a)
    below, above = jnp.where(group_odd, for_one, for_two), jnp.where(group_odd, for_two, for_one)
    low = mix(below, bottom, jnp.where(single, above, jnp.where(three, m, top)), weight)
    high = mix(jnp.where(single, below, jnp.where(three, m, bottom)), top, above, weight)
    return low, high, mix(bottom, m, top, weight)


def mix_kernel(is_far, level_count, current, one, two, middle, got_one, got_two, weight, gain, new, edge):
    own, group_odd, lat_odd = here(level_count)
    first = far_row(lat_odd) if is_far else near_row(lat_odd)
    slots = (0, own - 1, 1)

    def each(h, carry):
        values = mixed(h, own, group_odd, one, two, middle, got_one, got_two, weight)
        for plane, value in enumerate(values):
            x = (current[slots[plane], first + h].astype(F32) + value).astype(BF16)
            new[plane, h] = x
            place = jnp.where(group_odd, plane, 1 - plane) if plane < 2 else plane
            edge[place, h] = normed(x.astype(F32), gain[0:1, :])
        return carry

    lax.fori_loop(0, H, each, 0)


def last_kernel(level_count, current, one, two, middle, got_one, got_two, weight, out):
    own, group_odd, _ = here(level_count)

    def each(h, carry):
        values = mixed(h, own, group_odd, one, two, middle, got_one, got_two, weight)
        bottom, top, m = [(current[p, h].astype(F32) + value).astype(BF16) for p, value in enumerate(values)]
        zero = jnp.zeros_like(top)
        out[0, h] = bottom
        out[1, h] = jnp.where(own == 3, m, jnp.where(own == 2, top, zero))
        out[2, h] = jnp.where(own == 3, top, zero)
        return carry

    lax.fori_loop(0, H, each, 0)


def final_kernel(level_count, current, one, two, middle, got_one, got_two, weight, near_rows, out):
    own, group_odd, lat_odd = here(level_count)
    for slot in range(out.shape[0]):
        for h in range(H):
            out[slot, near_row(lat_odd) + h] = near_rows[slot, h]

    def each(h, carry):
        row = far_row(lat_odd) + h
        values = mixed(h, own, group_odd, one, two, middle, got_one, got_two, weight)
        bottom, top, m = [(current[p, h].astype(F32) + value).astype(BF16) for p, value in enumerate(values)]
        zero = jnp.zeros_like(top)
        out[0, row] = bottom
        out[1, row] = jnp.where(own == 3, m, jnp.where(own == 2, top, zero))
        out[2, row] = jnp.where(own == 3, top, zero)
        return carry

    lax.fori_loop(0, H, each, 0)


def pairs(count, first):
    found = [(i, i + 1) for i in range(first, count - 1, 2)]
    return found + [(j, i) for i, j in found]


def on_device(field, level_count, tap_rows, tap_lons, tap_values, norm_gain, disco_weight, vert_weight):
    slots, rows, lons, channels = field.shape
    lats, levs = lax.axis_size("lat"), lax.axis_size("lev")
    near_pairs, far_pairs = pairs(lats, 0), pairs(lats, 1)
    one_pairs, two_pairs = pairs(levs, 0), pairs(levs, 1)
    edge = jax.ShapeDtypeStruct((slots, H, lons, channels), BF16)
    plane = jax.ShapeDtypeStruct((H, lons, channels), BF16)
    work = 12 * H * lons * TAPS * channels * channels

    first_row = lax.axis_index("lat") * rows
    row_part = lax.dynamic_slice_in_dim(tap_rows, first_row, rows, 0)
    lon_part = lax.dynamic_slice_in_dim(tap_lons, first_row, rows, 0)
    value_part = lax.dynamic_slice_in_dim(tap_values, first_row, rows, 0).reshape(rows, TAPS * K)

    def maps_of(p, after=()):
        shape = jax.ShapeDtypeStruct((rows, TAPS * channels, channels), BF16)
        return call(tap_map_kernel, shape, [SMEM, VMEM], flops=work, after=after)(value_part, disco_weight[p])

    def disco(planes, is_far, far, near, got, maps, after):
        scratch = pltpu.VMEM((len(planes), rows + 2 * H, lons + 2 * PAD, channels), F32)
        return call(
            functools.partial(disco_kernel, planes, is_far),
            [plane] * len(planes),
            [SMEM] * 2 + [VMEM] * 4,
            [scratch],
            flops=work * len(planes),
            nbytes=1 << 20,
            after=after,
        )(row_part, lon_part, far, near, got, maps)

    far, near = call(norm_kernel, [edge, edge], [SMEM, VMEM, VMEM], nbytes=1 << 21)(level_count, field, norm_gain[0:1])
    maps = maps_of(0)
    for p in range(PASSES):
        far_got = lax.ppermute(far, "lat", far_pairs)
        near_got = lax.ppermute(near, "lat", near_pairs)
        ends, after = [], []
        for is_far, got in ((False, near_got), (True, far_got)):
            one, two = disco((0, 1), is_far, far, near, got, maps, after)
            got_one = lax.ppermute(one, "lev", one_pairs)
            got_two = lax.ppermute(two, "lev", two_pairs)
            (middle,) = disco((2,), is_far, far, near, got, maps, [one])
            after = [middle]
            ends.append((one, two, middle, got_one, got_two, vert_weight[p]))
        if p + 1 < PASSES:
            maps = maps_of(p + 1, after)
            after = [maps]
            made = []
            for is_far in (False, True):
                new, edges = call(
                    functools.partial(mix_kernel, is_far),
                    [edge, edge],
                    [SMEM] + [VMEM] * 8,
                    flops=work * 2,
                    nbytes=1 << 20,
                    after=after,
                )(level_count, field, *ends[is_far], norm_gain[p + 1 : p + 2])
                made.append((new, edges))
                after = [new]
            (near_new, near), (far_new, far) = made
        else:
            near_rows = call(last_kernel, edge, [SMEM] + [VMEM] * 7, flops=work * 2, nbytes=1 << 20, after=after)(
                level_count, near_new, *ends[0]
            )
            return call(
                final_kernel, jax.ShapeDtypeStruct(field.shape, BF16), [SMEM] + [VMEM] * 8, flops=work * 2, nbytes=1 << 20
            )(level_count, far_new, *ends[1], near_rows)


def solution(mesh):
    return jax.shard_map(
        on_device,
        mesh=mesh,
        in_specs=(P("lev", "lat", None, None), P(), P(), P(), P(), P(), P(), P()),
        out_specs=P("lev", "lat", None, None),
        check_vma=False,
    )
```

time: 282 us -> 95.6 us (0.34)
  the two profiles are of different devices: /device:TPU:49 before, /device:TPU:189 now
where the time goes in v2:
time: 95.6 us; the launch traced here: 95.3 us
  waiting for transfers between devices  41.7 us (44%)
  Pallas kernels  25.5 us (27%)
  starting transfers between devices  23.7 us (25%)
  local copies, waits for them, and re-layouts  4.06 us (4%)
    pallas_call x15, Pallas kernels, call(): return lambda *operands: made(*operands, *after)  25.5 us
    ppermute x2, waiting for transfers between devices, on_device(): far_got = lax.ppermute(far, 'lat', far_pairs)  24.1 us
    ppermute x4, waiting for transfers between devices, on_device(): got_two = lax.ppermute(two, 'lev', two_pairs)  16.5 us
    ppermute x4, starting transfers between devices, on_device(): got_two = lax.ppermute(two, 'lev', two_pairs)  11.2 us
    ppermute x4, starting transfers between devices, on_device(): got_one = lax.ppermute(one, 'lev', one_pairs)  6.51 us
    ppermute x2, starting transfers between devices, on_device(): far_got = lax.ppermute(far, 'lat', far_pairs)  5.75 us
    unnamed x18, local copies, waits for them, and re-layouts  2.09 us
  transfers between devices with their start and end apart: 12, of which 5 were waited for; matrix products, arithmetic and copies ran while one was open for 1% of the time, Pallas kernels for 23%

profile of v2, /device:TPU:189, one launch (start us, length us, event | category | flops | bytes accessed | tf_op | source)
XLA Modules:
  0.0 95.3 jit_solution(16423086900820036459)
XLA Ops:
  3.9 3.8 %collective-permute-start = (bf16[3,2,360,128]{3,2,1,0:T(8,128)(2,1)S(1)}, bf16[3,2,360,128]{3,2,1,0:T(8,128)(2,1)S(1)}, u32[]{:S(2)}, u32[]{:S(2)}) collective-permute-start(bf16[3,2,360,128]{3,2,1,0:T(8,128)(2,1)S(1)} %get-tuple-element.19.refs_2_), channel_id=1, source_target_pairs={{1,2},{3,4},{5,6},{7,8},{9,10},{11,12},{13,14},{15,16},{17,18},{19... | collective-permute-start | bytes 1658888 | tf_op jit(solution)/shard_map/ppermute | solution.py:231
  8.1 1.7 %shard_map.83.refs_5_ = bf16[4,1024,128]{2,1,0:T(8,128)(2,1)S(1)} custom-call(f32[4,32]{1,0:T(4,128)S(1)} %copy.15.refs_0_, bf16[512,128]{1,0:T(8,128)(2,1)S(1)} %get-tuple-element.34.refs_1_), custom_call_target="tpu_custom_call" | custom-call | flops 1132462080 | tf_op jit(solution)/shard_map/pallas_call | solution.py:40
  11.0 1.9 %shard_map.84 = (bf16[2,360,128]{2,1,0:T(8,128)(2,1)S(1)}, bf16[2,360,128]{2,1,0:T(8,128)(2,1)S(1)}) custom-call(s32[4,8]{1,0:T(4,128)S(1)} %copy.16.refs_0_, s32[4,8]{1,0:T(4,128)S(1)} %copy.17.refs_1_, bf16[3,2,360,128]{3,2,1,0:T(8,128)(2,1)S(1)} %get-tuple-element.19.refs_2_, bf16[3,2,360,128]{3,2,1,0:T(8,128)(2,1)S(1)} %get-tuple-element.20.refs_3_, ...), custom_call_target="tpu_custom_call" | custom-call | flops 2264924160 | bytes 1048576 | tf_op jit(solution)/shard_map/pallas_call | solution.py:40
  15.6 7.8 %collective-permute-done.refs_4_ = bf16[3,2,360,128]{3,2,1,0:T(8,128)(2,1)S(1)} collective-permute-done((bf16[3,2,360,128]{3,2,1,0:T(8,128)(2,1)S(1)}, bf16[3,2,360,128]{3,2,1,0:T(8,128)(2,1)S(1)}, u32[]{:S(2)}, u32[]{:S(2)}) %collective-permute-start) | collective-permute-done | bytes 552992 | tf_op jit(solution)/shard_map/ppermute | solution.py:231
  23.4 1.9 %shard_map.86 = (bf16[2,360,128]{2,1,0:T(8,128)(2,1)S(1)}, bf16[2,360,128]{2,1,0:T(8,128)(2,1)S(1)}) custom-call(s32[4,8]{1,0:T(4,128)S(1)} %copy.16.refs_0_, s32[4,8]{1,0:T(4,128)S(1)} %copy.17.refs_1_, bf16[3,2,360,128]{3,2,1,0:T(8,128)(2,1)S(1)} %get-tuple-element.19.refs_2_, bf16[3,2,360,128]{3,2,1,0:T(8,128)(2,1)S(1)} %get-tuple-element.20.refs_3_, ...), custom_call_target="tpu_custom_call" | custom-call | flops 2264924160 | bytes 1048576 | tf_op jit(solution)/shard_map/pallas_call | solution.py:40
  25.3 5.0 %collective-permute-start.2 = (bf16[2,360,128]{2,1,0:T(8,128)(2,1)S(1)}, bf16[2,360,128]{2,1,0:T(8,128)(2,1)S(1)}, u32[]{:S(2)}, u32[]{:S(2)}) collective-permute-start(bf16[2,360,128]{2,1,0:T(8,128)(2,1)S(1)} %get-tuple-element.22.refs_6_.refs_2_), channel_id=1, source_target_pairs={{0,64},{128,192},{64,0},{192,128},{1,65},{129,193},{65,1},{193,129... | collective-permute-start | bytes 552968 | tf_op jit(solution)/shard_map/ppermute | solution.py:236
  30.3 1.9 %collective-permute-start.3 = (bf16[2,360,128]{2,1,0:T(8,128)(2,1)S(1)}, bf16[2,360,128]{2,1,0:T(8,128)(2,1)S(1)}, u32[]{:S(2)}, u32[]{:S(2)}) collective-permute-start(bf16[2,360,128]{2,1,0:T(8,128)(2,1)S(1)} %get-tuple-element.23.refs_3_), channel_id=1, source_target_pairs={{64,128},{128,64},{65,129},{129,65},{66,130},{130,66},{67,131},{13... | collective-permute-start | bytes 552968 | tf_op jit(solution)/shard_map/ppermute | solution.py:237
  32.3 5.5 %collective-permute-start.5 = (bf16[2,360,128]{2,1,0:T(8,128)(2,1)S(1)}, bf16[2,360,128]{2,1,0:T(8,128)(2,1)S(1)}, u32[]{:S(2)}, u32[]{:S(2)}) collective-permute-start(bf16[2,360,128]{2,1,0:T(8,128)(2,1)S(1)} %get-tuple-element.24.refs_3_), channel_id=1, source_target_pairs={{64,128},{128,64},{65,129},{129,65},{66,130},{130,66},{67,131},{13... | collective-permute-start | bytes 552968 | tf_op jit(solution)/shard_map/ppermute | solution.py:237
  37.7 1.4 %shard_map.87.refs_2_.refs_4_ = bf16[2,360,128]{2,1,0:T(8,128)(2,1)S(1)} custom-call(s32[4,8]{1,0:T(4,128)S(1)} %copy.16.refs_0_, s32[4,8]{1,0:T(4,128)S(1)} %copy.17.refs_1_, bf16[3,2,360,128]{3,2,1,0:T(8,128)(2,1)S(1)} %get-tuple-element.19.refs_2_, bf16[3,2,360,128]{3,2,1,0:T(8,128)(2,1)S(1)} %get-tuple-element.20.refs_3_, ...), custom_call_target="tpu_custom_call" | custom-call | flops 1132462080 | bytes 1048576 | tf_op jit(solution)/shard_map/pallas_call | solution.py:40
  39.2 1.7 %shard_map.88.refs_9_.refs_5_ = bf16[4,1024,128]{2,1,0:T(8,128)(2,1)S(1)} custom-call(f32[4,32]{1,0:T(4,128)S(1)} %copy.15.refs_0_, bf16[512,128]{1,0:T(8,128)(2,1)S(1)} %get-tuple-element.33.refs_1_, bf16[2,360,128]{2,1,0:T(8,128)(2,1)S(1)} %shard_map.87.refs_2_.refs_4_), custom_call_target="tpu_custom_call" | custom-call | flops 1132462080 | tf_op jit(solution)/shard_map/pallas_call | solution.py:40
  41.0 10.3 %collective-permute-done.5.refs_6_ = bf16[2,360,128]{2,1,0:T(8,128)(2,1)S(1)} collective-permute-done((bf16[2,360,128]{2,1,0:T(8,128)(2,1)S(1)}, bf16[2,360,128]{2,1,0:T(8,128)(2,1)S(1)}, u32[]{:S(2)}, u32[]{:S(2)}) %collective-permute-start.5) | collective-permute-done | bytes 184352 | tf_op jit(solution)/shard_map/ppermute | solution.py:237
  51.2 1.7 %shard_map.89 = (bf16[3,2,360,128]{3,2,1,0:T(8,128)(2,1)S(1)}, bf16[3,2,360,128]{3,2,1,0:T(8,128)(2,1)S(1)}) custom-call(s32[4]{0:T(128)S(1)} %copy-done.4, bf16[3,4,360,128]{3,2,1,0:T(8,128)(2,1)S(1)} %copy-done.2, bf16[2,360,128]{2,1,0:T(8,128)(2,1)S(1)} %get-tuple-element.21.refs_6_.refs_2_, bf16[2,360,128]{2,1,0:T(8,128)(2,1)S(1)} %get-tuple-element.24.refs_3_, ...), custom_call_target="tpu_custom_call" | custom-call | flops 2264924160 | bytes 1048576 | tf_op jit(solution)/shard_map/pallas_call | solution.py:40
  53.1 1.7 %shard_map.90 = (bf16[3,2,360,128]{3,2,1,0:T(8,128)(2,1)S(1)}, bf16[3,2,360,128]{3,2,1,0:T(8,128)(2,1)S(1)}) custom-call(s32[4]{0:T(128)S(1)} %copy-done.4, bf16[3,4,360,128]{3,2,1,0:T(8,128)(2,1)S(1)} %copy-done.2, bf16[2,360,128]{2,1,0:T(8,128)(2,1)S(1)} %get-tuple-element.22.refs_6_.refs_2_, bf16[2,360,128]{2,1,0:T(8,128)(2,1)S(1)} %get-tuple-element.23.refs_3_, ...), custom_call_target="tpu_custom_call" | custom-call | flops 2264924160 | bytes 1048576 | tf_op jit(solution)/shard_map/pallas_call | solution.py:40
  54.9 1.9 %collective-permute-start.6 = (bf16[3,2,360,128]{3,2,1,0:T(8,128)(2,1)S(1)}, bf16[3,2,360,128]{3,2,1,0:T(8,128)(2,1)S(1)}, u32[]{:S(2)}, u32[]{:S(2)}) collective-permute-start(bf16[3,2,360,128]{3,2,1,0:T(8,128)(2,1)S(1)} %get-tuple-element.27.refs_2_), channel_id=1, source_target_pairs={{1,2},{3,4},{5,6},{7,8},{9,10},{11,12},{13,14},{15,16},{17,18},{19... | collective-permute-start | bytes 1658888 | tf_op jit(solution)/shard_map/ppermute | solution.py:231
  56.8 1.9 %shard_map.91 = (bf16[2,360,128]{2,1,0:T(8,128)(2,1)S(1)}, bf16[2,360,128]{2,1,0:T(8,128)(2,1)S(1)}) custom-call(s32[4,8]{1,0:T(4,128)S(1)} %copy.16.refs_0_, s32[4,8]{1,0:T(4,128)S(1)} %copy.17.refs_1_, bf16[3,2,360,128]{3,2,1,0:T(8,128)(2,1)S(1)} %get-tuple-element.27.refs_2_, bf16[3,2,360,128]{3,2,1,0:T(8,128)(2,1)S(1)} %get-tuple-element.28.refs_3_, ...), custom_call_target="tpu_custom_call" | custom-call | flops 2264924160 | bytes 1048576 | tf_op jit(solution)/shard_map/pallas_call | solution.py:40
  58.8 1.9 %collective-permute-start.11 = (bf16[2,360,128]{2,1,0:T(8,128)(2,1)S(1)}, bf16[2,360,128]{2,1,0:T(8,128)(2,1)S(1)}, u32[]{:S(2)}, u32[]{:S(2)}) collective-permute-start(bf16[2,360,128]{2,1,0:T(8,128)(2,1)S(1)} %get-tuple-element.32.refs_3_), channel_id=1, source_target_pairs={{64,128},{128,64},{65,129},{129,65},{66,130},{130,66},{67,131},{13... | collective-permute-start | bytes 552968 | tf_op jit(solution)/shard_map/ppermute | solution.py:237
  60.7 1.4 %shard_map.92.refs_6_.refs_4_ = bf16[2,360,128]{2,1,0:T(8,128)(2,1)S(1)} custom-call(s32[4,8]{1,0:T(4,128)S(1)} %copy.16.refs_0_, s32[4,8]{1,0:T(4,128)S(1)} %copy.17.refs_1_, bf16[3,2,360,128]{3,2,1,0:T(8,128)(2,1)S(1)} %get-tuple-element.27.refs_2_, bf16[3,2,360,128]{3,2,1,0:T(8,128)(2,1)S(1)} %get-tuple-element.28.refs_3_, ...), custom_call_target="tpu_custom_call" | custom-call | flops 1132462080 | bytes 1048576 | tf_op jit(solution)/shard_map/pallas_call | solution.py:40
  62.2 16.3 %collective-permute-done.6.refs_4_ = bf16[3,2,360,128]{3,2,1,0:T(8,128)(2,1)S(1)} collective-permute-done((bf16[3,2,360,128]{3,2,1,0:T(8,128)(2,1)S(1)}, bf16[3,2,360,128]{3,2,1,0:T(8,128)(2,1)S(1)}, u32[]{:S(2)}, u32[]{:S(2)}) %collective-permute-start.6) | collective-permute-done | bytes 552992 | tf_op jit(solution)/shard_map/ppermute | solution.py:231
  78.5 1.9 %shard_map.93 = (bf16[2,360,128]{2,1,0:T(8,128)(2,1)S(1)}, bf16[2,360,128]{2,1,0:T(8,128)(2,1)S(1)}) custom-call(s32[4,8]{1,0:T(4,128)S(1)} %copy.16.refs_0_, s32[4,8]{1,0:T(4,128)S(1)} %copy.17.refs_1_, bf16[3,2,360,128]{3,2,1,0:T(8,128)(2,1)S(1)} %get-tuple-element.27.refs_2_, bf16[3,2,360,128]{3,2,1,0:T(8,128)(2,1)S(1)} %get-tuple-element.28.refs_3_, ...), custom_call_target="tpu_custom_call" | custom-call | flops 2264924160 | bytes 1048576 | tf_op jit(solution)/shard_map/pallas_call | solution.py:40
  80.5 1.9 %collective-permute-start.9 = (bf16[2,360,128]{2,1,0:T(8,128)(2,1)S(1)}, bf16[2,360,128]{2,1,0:T(8,128)(2,1)S(1)}, u32[]{:S(2)}, u32[]{:S(2)}) collective-permute-start(bf16[2,360,128]{2,1,0:T(8,128)(2,1)S(1)} %get-tuple-element.31.refs_3_), channel_id=1, source_target_pairs={{64,128},{128,64},{65,129},{129,65},{66,130},{130,66},{67,131},{13... | collective-permute-start | bytes 552968 | tf_op jit(solution)/shard_map/ppermute | solution.py:237
  82.4 1.4 %shard_map.94.refs_8_.refs_4_ = bf16[2,360,128]{2,1,0:T(8,128)(2,1)S(1)} custom-call(s32[4,8]{1,0:T(4,128)S(1)} %copy.16.refs_0_, s32[4,8]{1,0:T(4,128)S(1)} %copy.17.refs_1_, bf16[3,2,360,128]{3,2,1,0:T(8,128)(2,1)S(1)} %get-tuple-element.27.refs_2_, bf16[3,2,360,128]{3,2,1,0:T(8,128)(2,1)S(1)} %get-tuple-element.28.refs_3_, ...), custom_call_target="tpu_custom_call" | custom-call | flops 1132462080 | bytes 1048576 | tf_op jit(solution)/shard_map/pallas_call | solution.py:40
  83.9 1.5 %shard_map.95.refs_8_ = bf16[3,2,360,128]{3,2,1,0:T(8,128)(2,1)S(1)} custom-call(s32[4]{0:T(128)S(1)} %copy-done.4, bf16[3,2,360,128]{3,2,1,0:T(8,128)(2,1)S(1)} %get-tuple-element.25.refs_9_.refs_1_, bf16[2,360,128]{2,1,0:T(8,128)(2,1)S(1)} %get-tuple-element.29.refs_6_.refs_2_, bf16[2,360,128]{2,1,0:T(8,128)(2,1)S(1)} %get-tuple-element.32.refs_3_, ...), custom_call_target="tpu_custom_call" | custom-call | flops 2264924160 | bytes 1048576 | tf_op jit(solution)/shard_map/pallas_call | solution.py:40
  86.5 6.2 %collective-permute-done.9.refs_6_ = bf16[2,360,128]{2,1,0:T(8,128)(2,1)S(1)} collective-permute-done((bf16[2,360,128]{2,1,0:T(8,128)(2,1)S(1)}, bf16[2,360,128]{2,1,0:T(8,128)(2,1)S(1)}, u32[]{:S(2)}, u32[]{:S(2)}) %collective-permute-start.9) | collective-permute-done | bytes 184352 | tf_op jit(solution)/shard_map/ppermute | solution.py:237
  92.7 2.5 %shard_map.96 = bf16[3,4,360,128]{3,2,1,0:T(8,128)(2,1)} custom-call(s32[4]{0:T(128)S(1)} %copy-done.4, bf16[3,2,360,128]{3,2,1,0:T(8,128)(2,1)S(1)} %get-tuple-element.26.refs_1_, bf16[2,360,128]{2,1,0:T(8,128)(2,1)S(1)} %get-tuple-element.30.refs_6_.refs_2_, bf16[2,360,128]{2,1,0:T(8,128)(2,1)S(1)} %get-tuple-element.31.refs_3_, ...), custom_call_target="tpu_custom_call" | custom-call | flops 2264924160 | bytes 1048576 | tf_op jit(solution)/shard_map/pallas_call | solution.py:40
  (39 shorter events, 9.5 us)
Async XLA Ops:
  0.0 7.8 %copy-start = (f32[256,8,4]{0,2,1:T(4,128)S(1)}, f32[256,8,4]{0,2,1:T(4,128)}, u32[]{:S(2)}) copy-start(f32[256,8,4]{0,2,1:T(4,128)} %param.12) | copy-start | bytes 98308
  0.8 1.2 %copy-start.1 = (bf16[3,4,360,128]{3,2,1,0:T(8,128)(2,1)S(1)}, bf16[3,4,360,128]{3,2,1,0:T(8,128)(2,1)}, u32[]{:S(2)}) copy-start(bf16[3,4,360,128]{3,2,1,0:T(8,128)(2,1)} %refs_1_.5) | copy-start | bytes 3317764
  2.0 0.7 copy-start.3
  2.7 5.3 %copy-start.6 = (s32[256,8]{0,1:T(8,128)S(1)}, s32[256,8]{0,1:T(8,128)}, u32[]{:S(2)}) copy-start(s32[256,8]{0,1:T(8,128)} %param.11) | copy-start | bytes 24580
  2.7 5.3 %copy-start.7 = (s32[256,8]{0,1:T(8,128)S(1)}, s32[256,8]{0,1:T(8,128)}, u32[]{:S(2)}) copy-start(s32[256,8]{0,1:T(8,128)} %param.10) | copy-start | bytes 24580
  2.7 5.4 %copy-start.5 = (bf16[2,512,128]{2,1,0:T(8,128)(2,1)S(1)}, bf16[2,512,128]{2,1,0:T(8,128)(2,1)}, u32[]{:S(2)}) copy-start(bf16[2,512,128]{2,1,0:T(8,128)(2,1)} %param.14) | copy-start | bytes 786436
  3.9 19.5 %collective-permute-start = (bf16[3,2,360,128]{3,2,1,0:T(8,128)(2,1)S(1)}, bf16[3,2,360,128]{3,2,1,0:T(8,128)(2,1)S(1)}, u32[]{:S(2)}, u32[]{:S(2)}) collective-permute-start(bf16[3,2,360,128]{3,2,1,0:T(8,128)(2,1)S(1)} %get-tuple-element.19.refs_2_), channel_id=1, source_target_pairs={{1,2},{3,4},{5,6},{7,8},{9,10},{11,12},{13,14},{15,16},{17,18},{19... | collective-permute-start | bytes 1658888 | tf_op jit(solution)/shard_map/ppermute | solution.py:231
  7.7 3.2 %collective-permute-start.1 = (bf16[3,2,360,128]{3,2,1,0:T(8,128)(2,1)S(1)}, bf16[3,2,360,128]{3,2,1,0:T(8,128)(2,1)S(1)}, u32[]{:S(2)}, u32[]{:S(2)}) collective-permute-start(bf16[3,2,360,128]{3,2,1,0:T(8,128)(2,1)S(1)} %get-tuple-element.20.refs_3_), channel_id=1, source_target_pairs={{0,1},{2,3},{4,5},{6,7},{8,9},{10,11},{12,13},{14,15},{16,17},{18,... | collective-permute-start | bytes 1658888 | tf_op jit(solution)/shard_map/ppermute | solution.py:232
  12.9 28.1 %collective-permute-start.4 = (bf16[2,360,128]{2,1,0:T(8,128)(2,1)S(1)}, bf16[2,360,128]{2,1,0:T(8,128)(2,1)S(1)}, u32[]{:S(2)}, u32[]{:S(2)}) collective-permute-start(bf16[2,360,128]{2,1,0:T(8,128)(2,1)S(1)} %get-tuple-element.21.refs_6_.refs_2_), channel_id=1, source_target_pairs={{0,64},{128,192},{64,0},{192,128},{1,65},{129,193},{65,1},{193,129... | collective-permute-start | bytes 552968 | tf_op jit(solution)/shard_map/ppermute | solution.py:236
  25.3 27.8 %collective-permute-start.2 = (bf16[2,360,128]{2,1,0:T(8,128)(2,1)S(1)}, bf16[2,360,128]{2,1,0:T(8,128)(2,1)S(1)}, u32[]{:S(2)}, u32[]{:S(2)}) collective-permute-start(bf16[2,360,128]{2,1,0:T(8,128)(2,1)S(1)} %get-tuple-element.22.refs_6_.refs_2_), channel_id=1, source_target_pairs={{0,64},{128,192},{64,0},{192,128},{1,65},{129,193},{65,1},{193,129... | collective-permute-start | bytes 552968 | tf_op jit(solution)/shard_map/ppermute | solution.py:236
  30.3 22.8 %collective-permute-start.3 = (bf16[2,360,128]{2,1,0:T(8,128)(2,1)S(1)}, bf16[2,360,128]{2,1,0:T(8,128)(2,1)S(1)}, u32[]{:S(2)}, u32[]{:S(2)}) collective-permute-start(bf16[2,360,128]{2,1,0:T(8,128)(2,1)S(1)} %get-tuple-element.23.refs_3_), channel_id=1, source_target_pairs={{64,128},{128,64},{65,129},{129,65},{66,130},{130,66},{67,131},{13... | collective-permute-start | bytes 552968 | tf_op jit(solution)/shard_map/ppermute | solution.py:237
  32.3 19.0 %collective-permute-start.5 = (bf16[2,360,128]{2,1,0:T(8,128)(2,1)S(1)}, bf16[2,360,128]{2,1,0:T(8,128)(2,1)S(1)}, u32[]{:S(2)}, u32[]{:S(2)}) collective-permute-start(bf16[2,360,128]{2,1,0:T(8,128)(2,1)S(1)} %get-tuple-element.24.refs_3_), channel_id=1, source_target_pairs={{64,128},{128,64},{65,129},{129,65},{66,130},{130,66},{67,131},{13... | collective-permute-start | bytes 552968 | tf_op jit(solution)/shard_map/ppermute | solution.py:237
  39.2 12.1 %copy-start.2 = (bf16[3,4,360,128]{3,2,1,0:T(8,128)(2,1)S(1)}, bf16[3,4,360,128]{3,2,1,0:T(8,128)(2,1)}, u32[]{:S(2)}) copy-start(bf16[3,4,360,128]{3,2,1,0:T(8,128)(2,1)} %refs_1_.5) | copy-start | bytes 3317764
  39.2 12.1 %copy-start.4 = (s32[4]{0:T(128)S(1)}, s32[4]{0:T(128)}, u32[]{:S(2)}) copy-start(s32[4]{0:T(128)} %refs_0_.9) | copy-start | bytes 52
  53.0 3.8 %collective-permute-start.7 = (bf16[3,2,360,128]{3,2,1,0:T(8,128)(2,1)S(1)}, bf16[3,2,360,128]{3,2,1,0:T(8,128)(2,1)S(1)}, u32[]{:S(2)}, u32[]{:S(2)}) collective-permute-start(bf16[3,2,360,128]{3,2,1,0:T(8,128)(2,1)S(1)} %get-tuple-element.28.refs_3_), channel_id=1, source_target_pairs={{0,1},{2,3},{4,5},{6,7},{8,9},{10,11},{12,13},{14,15},{16,17},{18,... | collective-permute-start | bytes 1658888 | tf_op jit(solution)/shard_map/ppermute | solution.py:232
  54.9 23.6 %collective-permute-start.6 = (bf16[3,2,360,128]{3,2,1,0:T(8,128)(2,1)S(1)}, bf16[3,2,360,128]{3,2,1,0:T(8,128)(2,1)S(1)}, u32[]{:S(2)}, u32[]{:S(2)}) collective-permute-start(bf16[3,2,360,128]{3,2,1,0:T(8,128)(2,1)S(1)} %get-tuple-element.27.refs_2_), channel_id=1, source_target_pairs={{1,2},{3,4},{5,6},{7,8},{9,10},{11,12},{13,14},{15,16},{17,18},{19... | collective-permute-start | bytes 1658888 | tf_op jit(solution)/shard_map/ppermute | solution.py:231
  58.7 25.2 %collective-permute-start.10 = (bf16[2,360,128]{2,1,0:T(8,128)(2,1)S(1)}, bf16[2,360,128]{2,1,0:T(8,128)(2,1)S(1)}, u32[]{:S(2)}, u32[]{:S(2)}) collective-permute-start(bf16[2,360,128]{2,1,0:T(8,128)(2,1)S(1)} %get-tuple-element.29.refs_6_.refs_2_), channel_id=1, source_target_pairs={{0,64},{128,192},{64,0},{192,128},{1,65},{129,193},{65,1},{193,129... | collective-permute-start | bytes 552968 | tf_op jit(solution)/shard_map/ppermute | solution.py:236
  58.8 25.1 %collective-permute-start.11 = (bf16[2,360,128]{2,1,0:T(8,128)(2,1)S(1)}, bf16[2,360,128]{2,1,0:T(8,128)(2,1)S(1)}, u32[]{:S(2)}, u32[]{:S(2)}) collective-permute-start(bf16[2,360,128]{2,1,0:T(8,128)(2,1)S(1)} %get-tuple-element.32.refs_3_), channel_id=1, source_target_pairs={{64,128},{128,64},{65,129},{129,65},{66,130},{130,66},{67,131},{13... | collective-permute-start | bytes 552968 | tf_op jit(solution)/shard_map/ppermute | solution.py:237
  80.4 6.2 %collective-permute-start.8 = (bf16[2,360,128]{2,1,0:T(8,128)(2,1)S(1)}, bf16[2,360,128]{2,1,0:T(8,128)(2,1)S(1)}, u32[]{:S(2)}, u32[]{:S(2)}) collective-permute-start(bf16[2,360,128]{2,1,0:T(8,128)(2,1)S(1)} %get-tuple-element.30.refs_6_.refs_2_), channel_id=1, source_target_pairs={{0,64},{128,192},{64,0},{192,128},{1,65},{129,193},{65,1},{193,129... | collective-permute-start | bytes 552968 | tf_op jit(solution)/shard_map/ppermute | solution.py:236
  80.5 12.2 %collective-permute-start.9 = (bf16[2,360,128]{2,1,0:T(8,128)(2,1)S(1)}, bf16[2,360,128]{2,1,0:T(8,128)(2,1)S(1)}, u32[]{:S(2)}, u32[]{:S(2)}) collective-permute-start(bf16[2,360,128]{2,1,0:T(8,128)(2,1)S(1)} %get-tuple-element.31.refs_3_), channel_id=1, source_target_pairs={{64,128},{128,64},{65,129},{129,65},{66,130},{130,66},{67,131},{13... | collective-permute-start | bytes 552968 | tf_op jit(solution)/shard_map/ppermute | solution.py:237

commit v3 on v2

v3 whole, which is shorter than its diff:
```python
import functools

import jax
import jax.numpy as jnp
from jax import lax
from jax.experimental import pallas as pl
from jax.experimental.pallas import tpu as pltpu
from jax.sharding import PartitionSpec as P

K = 4
TAPS = 8
H = 2
PASSES = 2
PAD = 8
EPSILON = 1e-06

BF16 = jnp.bfloat16
F32 = jnp.float32
VMEM = pl.BlockSpec(memory_space=pltpu.VMEM)
SMEM = pl.BlockSpec(memory_space=pltpu.SMEM)
LIMIT = 24 * 1024 * 1024


def call(kernel, out_shape, in_specs, scratch=(), after=(), cost=1, out_specs=None):
    many = isinstance(out_shape, (tuple, list))
    count, late = len(in_specs), len(after)

    def body(*refs):
        kernel(*refs[:count], *refs[count + late :])

    made = pl.pallas_call(
        body,
        out_shape=out_shape,
        in_specs=list(in_specs) + [pl.BlockSpec(memory_space=pl.ANY)] * late,
        out_specs=out_specs or ([VMEM] * len(out_shape) if many else VMEM),
        scratch_shapes=list(scratch),
        compiler_params=pltpu.CompilerParams(vmem_limit_bytes=LIMIT),
        cost_estimate=pl.CostEstimate(flops=cost, bytes_accessed=1, transcendentals=0),
    )
    return lambda *operands: made(*operands, *after)


def here(level_count):
    group = lax.axis_index("lev")
    own = level_count[group]
    return own, group % 2 == 1, lax.axis_index("lat") % 2


def plane_slots(own, group_odd):
    return jnp.where(group_odd, 0, own - 1), jnp.where(group_odd, own - 1, 0), 1


def far_row(lat_odd):
    return H * lat_odd


def near_row(lat_odd):
    return H * (1 - lat_odd)


def normed(widened, gain):
    mean_square = jnp.mean(widened * widened, axis=-1, keepdims=True)
    return (widened * lax.rsqrt(mean_square + EPSILON) * gain).astype(BF16)


def norm_kernel(is_far, field, gain, out, rows, sems):
    lat_odd = lax.axis_index("lat") % 2
    first = far_row(lat_odd) if is_far else near_row(lat_odd)
    slots = out.shape[0]
    copies = [pltpu.make_async_copy(field.at[slot, pl.ds(first, H)], rows.at[slot], sems.at[slot]) for slot in range(slots)]
    for copy in copies:
        copy.start()
    for slot, copy in enumerate(copies):
        copy.wait()
        for h in range(H):
            out[slot, h] = normed(rows[slot, h].astype(F32), gain[0:1, :])


def tap_map_kernel(values, weight, out):
    channels = weight.shape[-1]
    rows = values.shape[0]

    def one(index, carry):
        row = index // TAPS
        tap = index % TAPS
        total = None
        for k in range(K):
            part = values[row, tap * K + k] * weight[k * channels : (k + 1) * channels, :].astype(F32)
            total = part if total is None else total + part
        out[row, pl.ds(pl.multiple_of(tap * channels, channels), channels), :] = total.astype(BF16)
        return carry

    lax.fori_loop(0, rows * TAPS, one, 0)


def stage(scratch, place, refs, planes, firsts):
    for ref, plane, first in zip(refs, planes, firsts):
        lons = ref.shape[2]
        for h in range(H):
            value = ref[plane, h].astype(F32)
            scratch[place, first + h, pl.ds(PAD, lons), :] = value
            scratch[place, first + h, pl.ds(0, PAD), :] = value[lons - PAD :]
            scratch[place, first + h, pl.ds(PAD + lons, PAD), :] = value[:PAD]


def disco_rows(scratch, places, row, row_table, lon_table, weights, lons):
    taps = [(row + row_table[row, tap] + H, lon_table[row, tap] + PAD) for tap in range(TAPS)]
    for place in places:
        parts = [scratch[place, source, pl.ds(start, lons), :].astype(BF16) for source, start in taps]
        total = jnp.dot(jnp.concatenate(parts, axis=1), weights[row], preferred_element_type=F32)
        yield total.astype(BF16)


def places_of(level_count, is_far):
    own, group_odd, lat_odd = here(level_count)
    beyond = 3 * H * lat_odd if is_far else 3 * H * (1 - lat_odd)
    first = far_row(lat_odd) if is_far else near_row(lat_odd)
    return own, group_odd, first, (H + far_row(lat_odd), H + near_row(lat_odd), beyond)


def ends_kernel(is_far, slotted, level_count, row_table, lon_table, far, near, got, weights, one, two, scratch):
    own, group_odd, first, at = places_of(level_count, is_far)
    for place, slot in enumerate(plane_slots(own, group_odd)[:2]):
        plane = slot if slotted else place
        stage(scratch, place, (far, near, got), (plane,) * 3, at)

    def each(h, carry):
        one[h], two[h] = disco_rows(scratch, (0, 1), first + h, row_table, lon_table, weights, far.shape[2])
        return carry

    lax.fori_loop(0, H, each, 0)


def middle_kernel(is_far, planes, level_count, row_table, lon_table, far, near, got, weights, one, two, current, mixing, gain, *rest):
    middle, new, scratch = rest[0], rest[1], rest[-1]
    _, group_odd, first, at = places_of(level_count, is_far)
    stage(scratch, 0, (far, near, got), planes, at)

    def each(h, carry):
        (m,) = disco_rows(scratch, (0,), first + h, row_table, lon_table, weights, far.shape[2])
        middle[h] = m
        below, above = jnp.where(group_odd, one[h], two[h]), jnp.where(group_odd, two[h], one[h])
        old = current[1, first + h] if len(current.shape) == 4 else current[h]
        x = (old.astype(F32) + mix(below, m, above, mixing[...])).astype(BF16)
        new[h] = x
        if len(rest) == 4:
            rest[2][0, h] = normed(x.astype(F32), gain[1:2, :])
        return carry

    lax.fori_loop(0, H, each, 0)


def gelu(v):
    return 0.5 * v * (1.0 + lax.erf(v * 0.7071067811865476))


def mix(below, disco, above, weight):
    stacked = jnp.concatenate([below, disco, above], axis=1)
    return gelu(jnp.dot(stacked, weight, preferred_element_type=F32))


def ends_mixed(h, own, group_odd, one, two, middle, got_one, got_two, weight):
    channels = weight.shape[1]

    def block(upper):
        return weight[pl.ds(pl.multiple_of(jnp.where(upper, 2 * channels, 0), channels), channels), :]

    low, centre, high = block(group_odd), weight[channels : 2 * channels, :], block(jnp.logical_not(group_odd))
    three, single = own == 3, own == 1
    a, b, m, outer_a, outer_b = one[h], two[h], middle[h], got_one[h], got_two[h]
    inside_a = jnp.where(single, outer_b, jnp.where(three, m, b))
    inside_b = jnp.where(single, outer_a, jnp.where(three, m, a))
    value_a = mix(outer_a, a, inside_a, jnp.concatenate([high, centre, low], axis=0))
    value_b = mix(outer_b, b, inside_b, jnp.concatenate([low, centre, high], axis=0))
    return value_a, value_b


def mix_kernel(is_far, level_count, current, one, two, middle, got_one, got_two, weight, gain, middle_edge, new, edge):
    own, group_odd, lat_odd = here(level_count)
    first = far_row(lat_odd) if is_far else near_row(lat_odd)
    slots = plane_slots(own, group_odd)

    def each(h, carry):
        values = ends_mixed(h, own, group_odd, one, two, middle, got_one, got_two, weight)
        for plane, value in enumerate(values):
            x = (current[slots[plane], first + h].astype(F32) + value).astype(BF16)
            new[plane, h] = x
            edge[plane, h] = normed(x.astype(F32), gain[1:2, :])
        if not is_far:
            edge[2, h] = middle_edge[0, h]
        return carry

    lax.fori_loop(0, H, each, 0)


def last_kernel(level_count, current, one, two, middle, got_one, got_two, weight, out):
    own, group_odd, _ = here(level_count)

    def each(h, carry):
        for plane, value in enumerate(ends_mixed(h, own, group_odd, one, two, middle, got_one, got_two, weight)):
            out[plane, h] = (current[plane, h].astype(F32) + value).astype(BF16)
        return carry

    lax.fori_loop(0, H, each, 0)


def final_kernel(
    level_count, current, one, two, middle, got_one, got_two, weight, new_middle, near_ends, near_middle, out, rows, sems
):
    own, group_odd, lat_odd = here(level_count)
    slots = plane_slots(own, group_odd)
    zero = jnp.zeros(new_middle.shape[1:], BF16)

    def send(first, part):
        copies = [
            pltpu.make_async_copy(rows.at[slot, pl.ds(first, H)], out.at[slot, pl.ds(first, H)], sems.at[part, slot])
            for slot in range(out.shape[0])
        ]
        for copy in copies:
            copy.start()
        return copies

    near, far = near_row(lat_odd), far_row(lat_odd)
    for h in range(H):
        rows[1, near + h] = jnp.where(own == 3, near_middle[h], zero)
        rows[2, near + h] = zero
        rows[1, far + h] = jnp.where(own == 3, new_middle[h], zero)
        rows[2, far + h] = zero
        for plane in range(2):
            rows[slots[plane], near + h] = near_ends[plane, h]
    copies = send(near, 0)

    def each(h, carry):
        for plane, value in enumerate(ends_mixed(h, own, group_odd, one, two, middle, got_one, got_two, weight)):
            rows[slots[plane], far + h] = (current[plane, h].astype(F32) + value).astype(BF16)
        return carry

    lax.fori_loop(0, H, each, 0)
    for copy in copies + send(far, 1):
        copy.wait()


def pairs(count, first):
    found = [(i, i + 1) for i in range(first, count - 1, 2)]
    return found + [(j, i) for i, j in found]


def on_device(field, level_count, tap_rows, tap_lons, tap_values, norm_gain, disco_weight, vert_weight):
    slots, rows, lons, channels = field.shape
    lats, levs = lax.axis_size("lat"), lax.axis_size("lev")
    near_pairs, far_pairs = pairs(lats, 0), pairs(lats, 1)
    one_pairs, two_pairs = pairs(levs, 0), pairs(levs, 1)
    plane = jax.ShapeDtypeStruct((H, lons, channels), BF16)

    def edge(planes):
        return jax.ShapeDtypeStruct((planes, H, lons, channels), BF16)

    first_row = lax.axis_index("lat") * rows
    row_part = lax.dynamic_slice_in_dim(tap_rows, first_row, rows, 0)
    lon_part = lax.dynamic_slice_in_dim(tap_lons, first_row, rows, 0)
    value_part = lax.dynamic_slice_in_dim(tap_values, first_row, rows, 0).reshape(rows, TAPS * K)

    def maps_of(p, after=()):
        shape = jax.ShapeDtypeStruct((rows, TAPS * channels, channels), BF16)
        return call(tap_map_kernel, shape, [SMEM, VMEM], after=after, cost=10**10 if p == 0 else 1)(value_part, disco_weight[p])

    def padded(planes):
        return pltpu.VMEM((planes, rows + 2 * H, lons + 2 * PAD, channels), F32)

    hbm = pl.BlockSpec(memory_space=pltpu.HBM)
    scratch = [pltpu.VMEM((slots, H, lons, channels), BF16), pltpu.SemaphoreType.DMA((slots,))]

    def first_norm(is_far, after=()):
        kernel = functools.partial(norm_kernel, is_far)
        return call(kernel, edge(slots), [hbm, VMEM], scratch, after=after)(field, norm_gain)

    far = first_norm(True)
    near = first_norm(False, [far])
    near_got = lax.ppermute(near, "lat", near_pairs)
    far_got = lax.ppermute(far, "lat", far_pairs)
    maps = maps_of(0, [near])

    ends_edges = middle_edges = (far, near, far_got, near_got)
    middle_at = ((1, 1, 1), (1, 1, 1))
    ends_now, middle_now = (field, field), (field, field)
    for p in range(PASSES):
        last = p + 1 == PASSES
        done, after = [], []
        for is_far in (False, True):
            far, near, far_got, near_got = ends_edges
            one, two = call(
                functools.partial(ends_kernel, is_far, p == 0),
                [plane] * 2,
                [SMEM] * 3 + [VMEM] * 4,
                [padded(2)],
                after=after,
            )(level_count, row_part, lon_part, far, near, far_got if is_far else near_got, maps)
            got_one = lax.ppermute(one, "lev", one_pairs)
            got_two = lax.ppermute(two, "lev", two_pairs)
            far, near, far_got, near_got = middle_edges
            made = call(
                functools.partial(middle_kernel, is_far, middle_at[is_far]),
                [plane] * 2 + [edge(1)] * (not last),
                [SMEM] * 3 + [VMEM] * 9,
                [padded(1)],
            )(
                level_count, row_part, lon_part, far, near, far_got if is_far else near_got, maps,
                one, two, middle_now[is_far], vert_weight[p], norm_gain,
            )
            after = [made[0], one, two]
            done.append(((one, two, made[0], got_one, got_two, vert_weight[p]), made[1:]))
        (near_ends, near_made), (far_ends, far_made) = done
        if last:
            near_rows = call(last_kernel, edge(2), [SMEM] + [VMEM] * 7, after=after)(level_count, ends_now[0], *near_ends)
            return call(
                final_kernel,
                jax.ShapeDtypeStruct(field.shape, BF16),
                [SMEM] + [VMEM] * 10,
                [pltpu.VMEM(field.shape, BF16), pltpu.SemaphoreType.DMA((2, slots))],
                out_specs=hbm,
            )(level_count, ends_now[1], *far_ends, far_made[0], near_rows, near_made[0])
        middle_far = far_made[1]
        middle_far_got = lax.ppermute(middle_far, "lat", far_pairs)
        maps = maps_of(p + 1, after)
        new_near, near = call(functools.partial(mix_kernel, False), [edge(2), edge(3)], [SMEM] + [VMEM] * 9, after=[maps])(
            level_count, field, *near_ends, norm_gain, near_made[1]
        )
        near_got = lax.ppermute(near, "lat", near_pairs)
        new_far, far = call(functools.partial(mix_kernel, True), [edge(2), edge(2)], [SMEM] + [VMEM] * 9, after=[near], cost=10**10)(
            level_count, field, *far_ends, norm_gain, middle_far
        )
        far_got = lax.ppermute(far, "lat", far_pairs)
        ends_edges = (far, near, far_got, near_got)
        middle_edges = (middle_far, near, middle_far_got, near_got)
        middle_at = ((0, 2, 2), (0, 2, 0))
        ends_now, middle_now = (new_near, new_far), (near_made[0], far_made[0])


def solution(mesh):
    return jax.shard_map(
        on_device,
        mesh=mesh,
        in_specs=(P("lev", "lat", None, None), P(), P(), P(), P(), P(), P(), P()),
        out_specs=P("lev", "lat", None, None),
        check_vma=False,
    )
```

time: 95.6 us -> 81.4 us (0.85)
  the two profiles are of different devices: /device:TPU:189 before, /device:TPU:23 now
where the time goes in v3:
time: 81.4 us; the launch traced here: 81.1 us
  starting transfers between devices  34.2 us (42%)
  Pallas kernels  28.8 us (35%)
  waiting for transfers between devices  14.4 us (18%)
  local copies, waits for them, and re-layouts  3.35 us (4%)
    pallas_call x16, Pallas kernels, call(): return lambda *operands: made(*operands, *after)  28.8 us
    ppermute x4, starting transfers between devices, on_device(): got_one = lax.ppermute(one, 'lev', one_pairs)  20.2 us
    ppermute x4, waiting for transfers between devices, on_device(): got_one = lax.ppermute(one, 'lev', one_pairs)  9.8 us
    ppermute x2, starting transfers between devices, on_device(): far_got = lax.ppermute(far, 'lat', far_pairs)  6.16 us
    ppermute x2, waiting for transfers between devices, on_device(): far_got = lax.ppermute(far, 'lat', far_pairs)  4.54 us
    ppermute x1, starting transfers between devices, on_device(): middle_far_got = lax.ppermute(middle_far, 'lat', far_pairs)  3.64 us
    ppermute x4, starting transfers between devices, on_device(): got_two = lax.ppermute(two, 'lev', two_pairs)  2.65 us
    unnamed x20, local copies, waits for them, and re-layouts  2.14 us
  transfers between devices with their start and end apart: 13, of which 3 were waited for; matrix products, arithmetic and copies ran while one was open for 2% of the time, Pallas kernels for 31%

profile of v3, /device:TPU:23, one launch (start us, length us, event | category | flops | bytes accessed | tf_op | source)
XLA Modules:
  0.0 81.1 jit_solution(15683416799646250404)
XLA Ops:
  3.2 4.2 %collective-permute-start = (bf16[3,2,360,128]{3,2,1,0:T(8,128)(2,1)S(1)}, bf16[3,2,360,128]{3,2,1,0:T(8,128)(2,1)S(1)}, u32[]{:S(2)}, u32[]{:S(2)}) collective-permute-start(bf16[3,2,360,128]{3,2,1,0:T(8,128)(2,1)S(1)} %shard_map.82.refs_2_.refs_3_), channel_id=1, source_target_pairs={{1,2},{3,4},{5,6},{7,8},{9,10},{11,12},{13,14},{15,16},{17,18},{19... | collective-permute-start | bytes 1658888 | tf_op jit(solution)/shard_map/ppermute | solution.py:280
  9.2 1.7 %shard_map.84.refs_6_ = bf16[4,1024,128]{2,1,0:T(8,128)(2,1)S(1)} custom-call(f32[4,32]{1,0:T(4,128)S(1)} %copy.15.refs_0_, bf16[512,128]{1,0:T(8,128)(2,1)S(1)} %get-tuple-element.50.refs_1_, bf16[3,2,360,128]{3,2,1,0:T(8,128)(2,1)S(1)} %shard_map.83.refs_2_.refs_4_), custom_call_target="tpu_custom_call" | custom-call | flops 10000000000 | bytes 1 | tf_op jit(solution)/shard_map/pallas_call | solution.py:40
  12.2 1.9 %shard_map.85 = (bf16[2,360,128]{2,1,0:T(8,128)(2,1)S(1)}, bf16[2,360,128]{2,1,0:T(8,128)(2,1)S(1)}) custom-call(s32[4]{0:T(128)S(1)} %copy-done.3, s32[4,8]{1,0:T(4,128)S(1)} %copy.16.refs_1_, s32[4,8]{1,0:T(4,128)S(1)} %copy.17.refs_2_, bf16[3,2,360,128]{3,2,1,0:T(8,128)(2,1)S(1)} %shard_map.82.refs_2_.refs_3_, ...), custom_call_target="tpu_custom_call" | custom-call | flops 1 | bytes 1 | tf_op jit(solution)/shard_map/pallas_call | solution.py:40
  14.1 3.1 %collective-permute-start.4 = (bf16[2,360,128]{2,1,0:T(8,128)(2,1)S(1)}, bf16[2,360,128]{2,1,0:T(8,128)(2,1)S(1)}, u32[]{:S(2)}, u32[]{:S(2)}) collective-permute-start(bf16[2,360,128]{2,1,0:T(8,128)(2,1)S(1)} %get-tuple-element.27.refs_7_.refs_8_.refs_2_), channel_id=1, source_target_pairs={{0,64},{128,192},{64,0},{192,128},{1,65},{129,193},{65,1},{193,129... | collective-permute-start | bytes 552968 | tf_op jit(solution)/shard_map/ppermute | solution.py:298
  17.9 2.2 %shard_map.86 = (bf16[2,360,128]{2,1,0:T(8,128)(2,1)S(1)}, bf16[2,360,128]{2,1,0:T(8,128)(2,1)S(1)}, bf16[1,2,360,128]{3,2,1,0:T(8,128)(2,1)S(1)}) custom-call(s32[4]{0:T(128)S(1)} %copy-done.3, s32[4,8]{1,0:T(4,128)S(1)} %copy.16.refs_1_, s32[4,8]{1,0:T(4,128)S(1)} %copy.17.refs_2_, bf16[3,2,360,128]{3,2,1,0:T(8,128)(2,1)S(1)} %shard_map.82.refs_2_.refs_3_, ...), custom_call_target="tpu_custom_call" | custom-call | flops 1 | bytes 1 | tf_op jit(solution)/shard_map/pallas_call | solution.py:40
  20.1 4.5 %collective-permute-done.refs_5_ = bf16[3,2,360,128]{3,2,1,0:T(8,128)(2,1)S(1)} collective-permute-done((bf16[3,2,360,128]{3,2,1,0:T(8,128)(2,1)S(1)}, bf16[3,2,360,128]{3,2,1,0:T(8,128)(2,1)S(1)}, u32[]{:S(2)}, u32[]{:S(2)}) %collective-permute-start) | collective-permute-done | bytes 552992 | tf_op jit(solution)/shard_map/ppermute | solution.py:280
  24.6 1.9 %shard_map.87 = (bf16[2,360,128]{2,1,0:T(8,128)(2,1)S(1)}, bf16[2,360,128]{2,1,0:T(8,128)(2,1)S(1)}) custom-call(s32[4]{0:T(128)S(1)} %copy-done.3, s32[4,8]{1,0:T(4,128)S(1)} %copy.16.refs_1_, s32[4,8]{1,0:T(4,128)S(1)} %copy.17.refs_2_, bf16[3,2,360,128]{3,2,1,0:T(8,128)(2,1)S(1)} %shard_map.82.refs_2_.refs_3_, ...), custom_call_target="tpu_custom_call" | custom-call | flops 1 | bytes 1 | tf_op jit(solution)/shard_map/pallas_call | solution.py:40
  28.5 2.2 %shard_map.88 = (bf16[2,360,128]{2,1,0:T(8,128)(2,1)S(1)}, bf16[2,360,128]{2,1,0:T(8,128)(2,1)S(1)}, bf16[1,2,360,128]{3,2,1,0:T(8,128)(2,1)S(1)}) custom-call(s32[4]{0:T(128)S(1)} %copy-done.3, s32[4,8]{1,0:T(4,128)S(1)} %copy.16.refs_1_, s32[4,8]{1,0:T(4,128)S(1)} %copy.17.refs_2_, bf16[3,2,360,128]{3,2,1,0:T(8,128)(2,1)S(1)} %shard_map.82.refs_2_.refs_3_, ...), custom_call_target="tpu_custom_call" | custom-call | flops 1 | bytes 1 | tf_op jit(solution)/shard_map/pallas_call | solution.py:40
  30.7 1.7 %shard_map.89.refs_10_.refs_6_ = bf16[4,1024,128]{2,1,0:T(8,128)(2,1)S(1)} custom-call(f32[4,32]{1,0:T(4,128)S(1)} %copy.15.refs_0_, bf16[512,128]{1,0:T(8,128)(2,1)S(1)} %get-tuple-element.49.refs_1_, bf16[2,360,128]{2,1,0:T(8,128)(2,1)S(1)} %get-tuple-element.32.refs_2_.refs_4_, bf16[2,360,128]{2,1,0:T(8,128)(2,1)S(1)} %get-tuple-element.30.refs_7_.refs_3_.refs_2_, ...), custom_call_target="tpu_custom_call" | custom-call | flops 1 | bytes 1 | tf_op jit(solution)/shard_map/pallas_call | solution.py:40
  32.5 1.5 %shard_map.90 = (bf16[2,2,360,128]{3,2,1,0:T(8,128)(2,1)S(1)}, bf16[3,2,360,128]{3,2,1,0:T(8,128)(2,1)S(1)}) custom-call(s32[4]{0:T(128)S(1)} %copy-done.3, bf16[3,4,360,128]{3,2,1,0:T(8,128)(2,1)S(1)} %copy-done.2, bf16[2,360,128]{2,1,0:T(8,128)(2,1)S(1)} %get-tuple-element.27.refs_7_.refs_8_.refs_2_, ...), custom_call_target="tpu_custom_call" | custom-call | flops 1 | bytes 1 | tf_op jit(solution)/shard_map/pallas_call | solution.py:40
  34.0 1.3 %collective-permute-start.7 = (bf16[3,2,360,128]{3,2,1,0:T(8,128)(2,1)S(1)}, bf16[3,2,360,128]{3,2,1,0:T(8,128)(2,1)S(1)}, u32[]{:S(2)}, u32[]{:S(2)}) collective-permute-start(bf16[3,2,360,128]{3,2,1,0:T(8,128)(2,1)S(1)} %get-tuple-element.35.refs_10_.refs_4_), channel_id=1, source_target_pairs={{0,1},{2,3},{4,5},{6,7},{8,9},{10,11},{12,13},{14,15},{16,17},{18,... | collective-permute-start | bytes 1658888 | tf_op jit(solution)/shard_map/ppermute | solution.py:328
  35.4 3.9 %collective-permute-done.2.refs_5_ = bf16[2,360,128]{2,1,0:T(8,128)(2,1)S(1)} collective-permute-done((bf16[2,360,128]{2,1,0:T(8,128)(2,1)S(1)}, bf16[2,360,128]{2,1,0:T(8,128)(2,1)S(1)}, u32[]{:S(2)}, u32[]{:S(2)}) %collective-permute-start.2) | collective-permute-done | bytes 184352 | tf_op jit(solution)/shard_map/ppermute | solution.py:298
  39.2 1.5 %shard_map.91 = (bf16[2,2,360,128]{3,2,1,0:T(8,128)(2,1)S(1)}, bf16[2,2,360,128]{3,2,1,0:T(8,128)(2,1)S(1)}) custom-call(s32[4]{0:T(128)S(1)} %copy-done.3, bf16[3,4,360,128]{3,2,1,0:T(8,128)(2,1)S(1)} %copy-done.2, bf16[2,360,128]{2,1,0:T(8,128)(2,1)S(1)} %get-tuple-element.30.refs_7_.refs_3_.refs_2_, ...), custom_call_target="tpu_custom_call" | custom-call | flops 10000000000 | bytes 1 | tf_op jit(solution)/shard_map/pallas_call | solution.py:40
  40.8 1.9 %collective-permute-start.6 = (bf16[2,2,360,128]{3,2,1,0:T(8,128)(2,1)S(1)}, bf16[2,2,360,128]{3,2,1,0:T(8,128)(2,1)S(1)}, u32[]{:S(2)}, u32[]{:S(2)}) collective-permute-start(bf16[2,2,360,128]{3,2,1,0:T(8,128)(2,1)S(1)} %get-tuple-element.37.refs_3_), channel_id=1, source_target_pairs={{1,2},{3,4},{5,6},{7,8},{9,10},{11,12},{13,14},{15,16},{17,18},{19... | collective-permute-start | bytes 1105928 | tf_op jit(solution)/shard_map/ppermute | solution.py:332
  42.7 3.6 %collective-permute-start.8 = (bf16[1,2,360,128]{3,2,1,0:T(8,128)(2,1)S(1)}, bf16[1,2,360,128]{3,2,1,0:T(8,128)(2,1)S(1)}, u32[]{:S(2)}, u32[]{:S(2)}) collective-permute-start(bf16[1,2,360,128]{3,2,1,0:T(8,128)(2,1)S(1)} %get-tuple-element.33.refs_9_.refs_3_), channel_id=1, source_target_pairs={{1,2},{3,4},{5,6},{7,8},{9,10},{11,12},{13,14},{15,16},{17,18},{19... | collective-permute-start | bytes 552968 | tf_op jit(solution)/shard_map/ppermute | solution.py:323
  46.4 1.9 %shard_map.92 = (bf16[2,360,128]{2,1,0:T(8,128)(2,1)S(1)}, bf16[2,360,128]{2,1,0:T(8,128)(2,1)S(1)}) custom-call(s32[4]{0:T(128)S(1)} %copy-done.3, s32[4,8]{1,0:T(4,128)S(1)} %copy.16.refs_1_, s32[4,8]{1,0:T(4,128)S(1)} %copy.17.refs_2_, bf16[2,2,360,128]{3,2,1,0:T(8,128)(2,1)S(1)} %get-tuple-element.37.refs_3_, ...), custom_call_target="tpu_custom_call" | custom-call | flops 1 | bytes 1 | tf_op jit(solution)/shard_map/pallas_call | solution.py:40
  48.3 6.0 %collective-permute-start.11 = (bf16[2,360,128]{2,1,0:T(8,128)(2,1)S(1)}, bf16[2,360,128]{2,1,0:T(8,128)(2,1)S(1)}, u32[]{:S(2)}, u32[]{:S(2)}) collective-permute-start(bf16[2,360,128]{2,1,0:T(8,128)(2,1)S(1)} %get-tuple-element.38.refs_7_.refs_8_.refs_2_), channel_id=1, source_target_pairs={{0,64},{128,192},{64,0},{192,128},{1,65},{129,193},{65,1},{193,129... | collective-permute-start | bytes 552968 | tf_op jit(solution)/shard_map/ppermute | solution.py:298
  54.9 2.1 %shard_map.93 = (bf16[2,360,128]{2,1,0:T(8,128)(2,1)S(1)}, bf16[2,360,128]{2,1,0:T(8,128)(2,1)S(1)}) custom-call(s32[4]{0:T(128)S(1)} %copy-done.3, s32[4,8]{1,0:T(4,128)S(1)} %copy.16.refs_1_, s32[4,8]{1,0:T(4,128)S(1)} %copy.17.refs_2_, bf16[1,2,360,128]{3,2,1,0:T(8,128)(2,1)S(1)} %get-tuple-element.33.refs_9_.refs_3_, ...), custom_call_target="tpu_custom_call" | custom-call | flops 1 | bytes 1 | tf_op jit(solution)/shard_map/pallas_call | solution.py:40
  57.0 1.9 %shard_map.94 = (bf16[2,360,128]{2,1,0:T(8,128)(2,1)S(1)}, bf16[2,360,128]{2,1,0:T(8,128)(2,1)S(1)}) custom-call(s32[4]{0:T(128)S(1)} %copy-done.3, s32[4,8]{1,0:T(4,128)S(1)} %copy.16.refs_1_, s32[4,8]{1,0:T(4,128)S(1)} %copy.17.refs_2_, bf16[2,2,360,128]{3,2,1,0:T(8,128)(2,1)S(1)} %get-tuple-element.37.refs_3_, ...), custom_call_target="tpu_custom_call" | custom-call | flops 1 | bytes 1 | tf_op jit(solution)/shard_map/pallas_call | solution.py:40
  59.6 9.8 %collective-permute-start.9 = (bf16[2,360,128]{2,1,0:T(8,128)(2,1)S(1)}, bf16[2,360,128]{2,1,0:T(8,128)(2,1)S(1)}, u32[]{:S(2)}, u32[]{:S(2)}) collective-permute-start(bf16[2,360,128]{2,1,0:T(8,128)(2,1)S(1)} %get-tuple-element.42.refs_7_.refs_9_.refs_2_), channel_id=1, source_target_pairs={{0,64},{128,192},{64,0},{192,128},{1,65},{129,193},{65,1},{193,129... | collective-permute-start | bytes 552968 | tf_op jit(solution)/shard_map/ppermute | solution.py:298
  69.4 2.0 %shard_map.95 = (bf16[2,360,128]{2,1,0:T(8,128)(2,1)S(1)}, bf16[2,360,128]{2,1,0:T(8,128)(2,1)S(1)}) custom-call(s32[4]{0:T(128)S(1)} %copy-done.3, s32[4,8]{1,0:T(4,128)S(1)} %copy.16.refs_1_, s32[4,8]{1,0:T(4,128)S(1)} %copy.17.refs_2_, bf16[1,2,360,128]{3,2,1,0:T(8,128)(2,1)S(1)} %get-tuple-element.33.refs_9_.refs_3_, ...), custom_call_target="tpu_custom_call" | custom-call | flops 1 | bytes 1 | tf_op jit(solution)/shard_map/pallas_call | solution.py:40
  71.5 1.3 %shard_map.96.refs_9_ = bf16[2,2,360,128]{3,2,1,0:T(8,128)(2,1)S(1)} custom-call(s32[4]{0:T(128)S(1)} %copy-done.3, bf16[2,2,360,128]{3,2,1,0:T(8,128)(2,1)S(1)} %get-tuple-element.47.refs_1_, bf16[2,360,128]{2,1,0:T(8,128)(2,1)S(1)} %get-tuple-element.38.refs_7_.refs_8_.refs_2_, bf16[2,360,128]{2,1,0:T(8,128)(2,1)S(1)} %get-tuple-element.39.refs_8_.refs_9_.refs_3_, ...), custom_call_target="tpu_custom_call" | custom-call | flops 1 | bytes 1 | tf_op jit(solution)/shard_map/pallas_call | solution.py:40
  72.8 5.9 %collective-permute-done.9.refs_5_ = bf16[2,360,128]{2,1,0:T(8,128)(2,1)S(1)} collective-permute-done((bf16[2,360,128]{2,1,0:T(8,128)(2,1)S(1)}, bf16[2,360,128]{2,1,0:T(8,128)(2,1)S(1)}, u32[]{:S(2)}, u32[]{:S(2)}) %collective-permute-start.9) | collective-permute-done | bytes 184352 | tf_op jit(solution)/shard_map/ppermute | solution.py:298
  78.7 2.3 %shard_map.97 = bf16[3,4,360,128]{3,2,1,0:T(8,128)(2,1)} custom-call(s32[4]{0:T(128)S(1)} %copy-done.3, bf16[2,2,360,128]{3,2,1,0:T(8,128)(2,1)S(1)} %get-tuple-element.36.refs_1_, bf16[2,360,128]{2,1,0:T(8,128)(2,1)S(1)} %get-tuple-element.42.refs_7_.refs_9_.refs_2_, bf16[2,360,128]{2,1,0:T(8,128)(2,1)S(1)} %get-tuple-element.43.refs_8_.refs_10_.refs_3_, ...), custom_call_target="tpu_custom_call" | custom-call | flops 1 | bytes 1 | tf_op jit(solution)/shard_map/pallas_call | solution.py:40
  (43 shorter events, 10.1 us)
Async XLA Ops:
  0.0 9.0 %copy-start = (f32[256,8,4]{0,2,1:T(4,128)S(1)}, f32[256,8,4]{0,2,1:T(4,128)}, u32[]{:S(2)}) copy-start(f32[256,8,4]{0,2,1:T(4,128)} %param.12) | copy-start | bytes 98308
  0.0 1.3 %copy-start.1 = (bf16[3,4,360,128]{3,2,1,0:T(8,128)(2,1)S(1)}, bf16[3,4,360,128]{3,2,1,0:T(8,128)(2,1)}, u32[]{:S(2)}) copy-start(bf16[3,4,360,128]{3,2,1,0:T(8,128)(2,1)} %refs_1_.7) | copy-start | bytes 3317764
  1.3 0.7 copy-start.4
  3.2 5.9 %copy-start.6 = (bf16[2,512,128]{2,1,0:T(8,128)(2,1)S(1)}, bf16[2,512,128]{2,1,0:T(8,128)(2,1)}, u32[]{:S(2)}) copy-start(bf16[2,512,128]{2,1,0:T(8,128)(2,1)} %param.14) | copy-start | bytes 786436
  3.2 21.4 %collective-permute-start = (bf16[3,2,360,128]{3,2,1,0:T(8,128)(2,1)S(1)}, bf16[3,2,360,128]{3,2,1,0:T(8,128)(2,1)S(1)}, u32[]{:S(2)}, u32[]{:S(2)}) collective-permute-start(bf16[3,2,360,128]{3,2,1,0:T(8,128)(2,1)S(1)} %shard_map.82.refs_2_.refs_3_), channel_id=1, source_target_pairs={{1,2},{3,4},{5,6},{7,8},{9,10},{11,12},{13,14},{15,16},{17,18},{19... | collective-permute-start | bytes 1658888 | tf_op jit(solution)/shard_map/ppermute | solution.py:280
  8.8 3.4 %collective-permute-start.1 = (bf16[3,2,360,128]{3,2,1,0:T(8,128)(2,1)S(1)}, bf16[3,2,360,128]{3,2,1,0:T(8,128)(2,1)S(1)}, u32[]{:S(2)}, u32[]{:S(2)}) collective-permute-start(bf16[3,2,360,128]{3,2,1,0:T(8,128)(2,1)S(1)} %shard_map.83.refs_2_.refs_4_), channel_id=1, source_target_pairs={{0,1},{2,3},{4,5},{6,7},{8,9},{10,11},{12,13},{14,15},{16,17},{18,... | collective-permute-start | bytes 1658888 | tf_op jit(solution)/shard_map/ppermute | solution.py:279
  9.1 1.8 %copy-start.7 = (s32[256,8]{0,1:T(8,128)S(1)}, s32[256,8]{0,1:T(8,128)}, u32[]{:S(2)}) copy-start(s32[256,8]{0,1:T(8,128)} %param.11) | copy-start | bytes 24580
  9.2 1.8 %copy-start.8 = (s32[256,8]{0,1:T(8,128)S(1)}, s32[256,8]{0,1:T(8,128)}, u32[]{:S(2)}) copy-start(s32[256,8]{0,1:T(8,128)} %param.10) | copy-start | bytes 24580
  9.2 3.0 %copy-start.3 = (s32[4]{0:T(128)S(1)}, s32[4]{0:T(128)}, u32[]{:S(2)}) copy-start(s32[4]{0:T(128)} %refs_0_.27) | copy-start | bytes 52
  12.1 5.7 %copy-start.2 = (bf16[3,4,360,128]{3,2,1,0:T(8,128)(2,1)S(1)}, bf16[3,4,360,128]{3,2,1,0:T(8,128)(2,1)}, u32[]{:S(2)}) copy-start(bf16[3,4,360,128]{3,2,1,0:T(8,128)(2,1)} %refs_1_.7) | copy-start | bytes 3317764
  12.2 5.7 %copy-start.5 = (f32[2,128]{1,0:T(2,128)S(1)}, f32[2,128]{1,0:T(2,128)}, u32[]{:S(2)}) copy-start(f32[2,128]{1,0:T(2,128)} %refs_11_.7) | copy-start | bytes 3076
  14.1 18.4 %collective-permute-start.4 = (bf16[2,360,128]{2,1,0:T(8,128)(2,1)S(1)}, bf16[2,360,128]{2,1,0:T(8,128)(2,1)S(1)}, u32[]{:S(2)}, u32[]{:S(2)}) collective-permute-start(bf16[2,360,128]{2,1,0:T(8,128)(2,1)S(1)} %get-tuple-element.27.refs_7_.refs_8_.refs_2_), channel_id=1, source_target_pairs={{0,64},{128,192},{64,0},{192,128},{1,65},{129,193},{65,1},{193,129... | collective-permute-start | bytes 552968 | tf_op jit(solution)/shard_map/ppermute | solution.py:298
  17.2 15.3 %collective-permute-start.5 = (bf16[2,360,128]{2,1,0:T(8,128)(2,1)S(1)}, bf16[2,360,128]{2,1,0:T(8,128)(2,1)S(1)}, u32[]{:S(2)}, u32[]{:S(2)}) collective-permute-start(bf16[2,360,128]{2,1,0:T(8,128)(2,1)S(1)} %get-tuple-element.28.refs_8_.refs_9_.refs_3_), channel_id=1, source_target_pairs={{64,128},{128,64},{65,129},{129,65},{66,130},{130,66},{67,131},{13... | collective-permute-start | bytes 552968 | tf_op jit(solution)/shard_map/ppermute | solution.py:299
  26.5 12.7 %collective-permute-start.2 = (bf16[2,360,128]{2,1,0:T(8,128)(2,1)S(1)}, bf16[2,360,128]{2,1,0:T(8,128)(2,1)S(1)}, u32[]{:S(2)}, u32[]{:S(2)}) collective-permute-start(bf16[2,360,128]{2,1,0:T(8,128)(2,1)S(1)} %get-tuple-element.30.refs_7_.refs_3_.refs_2_), channel_id=1, source_target_pairs={{0,64},{128,192},{64,0},{192,128},{1,65},{129,193},{65,1},{193,129... | collective-permute-start | bytes 552968 | tf_op jit(solution)/shard_map/ppermute | solution.py:298
  27.8 11.4 %collective-permute-start.3 = (bf16[2,360,128]{2,1,0:T(8,128)(2,1)S(1)}, bf16[2,360,128]{2,1,0:T(8,128)(2,1)S(1)}, u32[]{:S(2)}, u32[]{:S(2)}) collective-permute-start(bf16[2,360,128]{2,1,0:T(8,128)(2,1)S(1)} %get-tuple-element.31.refs_8_.refs_4_.refs_3_), channel_id=1, source_target_pairs={{64,128},{128,64},{65,129},{129,65},{66,130},{130,66},{67,131},{13... | collective-permute-start | bytes 552968 | tf_op jit(solution)/shard_map/ppermute | solution.py:299
  34.0 12.3 %collective-permute-start.7 = (bf16[3,2,360,128]{3,2,1,0:T(8,128)(2,1)S(1)}, bf16[3,2,360,128]{3,2,1,0:T(8,128)(2,1)S(1)}, u32[]{:S(2)}, u32[]{:S(2)}) collective-permute-start(bf16[3,2,360,128]{3,2,1,0:T(8,128)(2,1)S(1)} %get-tuple-element.35.refs_10_.refs_4_), channel_id=1, source_target_pairs={{0,1},{2,3},{4,5},{6,7},{8,9},{10,11},{12,13},{14,15},{16,17},{18,... | collective-permute-start | bytes 1658888 | tf_op jit(solution)/shard_map/ppermute | solution.py:328
  40.8 16.2 %collective-permute-start.6 = (bf16[2,2,360,128]{3,2,1,0:T(8,128)(2,1)S(1)}, bf16[2,2,360,128]{3,2,1,0:T(8,128)(2,1)S(1)}, u32[]{:S(2)}, u32[]{:S(2)}) collective-permute-start(bf16[2,2,360,128]{3,2,1,0:T(8,128)(2,1)S(1)} %get-tuple-element.37.refs_3_), channel_id=1, source_target_pairs={{1,2},{3,4},{5,6},{7,8},{9,10},{11,12},{13,14},{15,16},{17,18},{19... | collective-permute-start | bytes 1105928 | tf_op jit(solution)/shard_map/ppermute | solution.py:332
  42.7 26.7 %collective-permute-start.8 = (bf16[1,2,360,128]{3,2,1,0:T(8,128)(2,1)S(1)}, bf16[1,2,360,128]{3,2,1,0:T(8,128)(2,1)S(1)}, u32[]{:S(2)}, u32[]{:S(2)}) collective-permute-start(bf16[1,2,360,128]{3,2,1,0:T(8,128)(2,1)S(1)} %get-tuple-element.33.refs_9_.refs_3_), channel_id=1, source_target_pairs={{1,2},{3,4},{5,6},{7,8},{9,10},{11,12},{13,14},{15,16},{17,18},{19... | collective-permute-start | bytes 552968 | tf_op jit(solution)/shard_map/ppermute | solution.py:323
  48.3 23.2 %collective-permute-start.11 = (bf16[2,360,128]{2,1,0:T(8,128)(2,1)S(1)}, bf16[2,360,128]{2,1,0:T(8,128)(2,1)S(1)}, u32[]{:S(2)}, u32[]{:S(2)}) collective-permute-start(bf16[2,360,128]{2,1,0:T(8,128)(2,1)S(1)} %get-tuple-element.38.refs_7_.refs_8_.refs_2_), channel_id=1, source_target_pairs={{0,64},{128,192},{64,0},{192,128},{1,65},{129,193},{65,1},{193,129... | collective-permute-start | bytes 552968 | tf_op jit(solution)/shard_map/ppermute | solution.py:298
  54.3 17.2 %collective-permute-start.12 = (bf16[2,360,128]{2,1,0:T(8,128)(2,1)S(1)}, bf16[2,360,128]{2,1,0:T(8,128)(2,1)S(1)}, u32[]{:S(2)}, u32[]{:S(2)}) collective-permute-start(bf16[2,360,128]{2,1,0:T(8,128)(2,1)S(1)} %get-tuple-element.39.refs_8_.refs_9_.refs_3_), channel_id=1, source_target_pairs={{64,128},{128,64},{65,129},{129,65},{66,130},{130,66},{67,131},{13... | collective-permute-start | bytes 552968 | tf_op jit(solution)/shard_map/ppermute | solution.py:299
  58.9 13.9 %collective-permute-start.10 = (bf16[2,360,128]{2,1,0:T(8,128)(2,1)S(1)}, bf16[2,360,128]{2,1,0:T(8,128)(2,1)S(1)}, u32[]{:S(2)}, u32[]{:S(2)}) collective-permute-start(bf16[2,360,128]{2,1,0:T(8,128)(2,1)S(1)} %get-tuple-element.43.refs_8_.refs_10_.refs_3_), channel_id=1, source_target_pairs={{64,128},{128,64},{65,129},{129,65},{66,130},{130,66},{67,131},{13... | collective-permute-start | bytes 552968 | tf_op jit(solution)/shard_map/ppermute | solution.py:299
  59.6 19.2 %collective-permute-start.9 = (bf16[2,360,128]{2,1,0:T(8,128)(2,1)S(1)}, bf16[2,360,128]{2,1,0:T(8,128)(2,1)S(1)}, u32[]{:S(2)}, u32[]{:S(2)}) collective-permute-start(bf16[2,360,128]{2,1,0:T(8,128)(2,1)S(1)} %get-tuple-element.42.refs_7_.refs_9_.refs_2_), channel_id=1, source_target_pairs={{0,64},{128,192},{64,0},{192,128},{1,65},{129,193},{65,1},{193,129... | collective-permute-start | bytes 552968 | tf_op jit(solution)/shard_map/ppermute | solution.py:298

commit v4 on v3

v4 whole, which is shorter than its diff:
```python
import functools

import jax
import jax.numpy as jnp
from jax import lax
from jax.experimental import pallas as pl
from jax.experimental.pallas import tpu as pltpu
from jax.sharding import PartitionSpec as P

K = 4
TAPS = 8
H = 2
PASSES = 2
PAD = 8
EPSILON = 1e-06

BF16 = jnp.bfloat16
F32 = jnp.float32
VMEM = pl.BlockSpec(memory_space=pltpu.VMEM)
SMEM = pl.BlockSpec(memory_space=pltpu.SMEM)
LIMIT = 24 * 1024 * 1024


def call(kernel, out_shape, in_specs, scratch=(), after=(), cost=1, out_specs=None):
    many = isinstance(out_shape, (tuple, list))
    count, late = len(in_specs), len(after)

    def body(*refs):
        kernel(*refs[:count], *refs[count + late :])

    made = pl.pallas_call(
        body,
        out_shape=out_shape,
        in_specs=list(in_specs) + [pl.BlockSpec(memory_space=pl.ANY)] * late,
        out_specs=out_specs or ([VMEM] * len(out_shape) if many else VMEM),
        scratch_shapes=list(scratch),
        compiler_params=pltpu.CompilerParams(vmem_limit_bytes=LIMIT),
        cost_estimate=pl.CostEstimate(flops=cost, bytes_accessed=1, transcendentals=0),
    )
    return lambda *operands: made(*operands, *after)


def here():
    lat_odd = lax.axis_index("lat") % 2
    return (lax.axis_index("lev") + lat_odd) % 2 == 1, lat_odd


def own_levels(level_count):
    lanes = lax.broadcasted_iota(jnp.int32, level_count.shape, 1)
    return jnp.sum(jnp.where(lanes == lax.axis_index("lev"), level_count[...], 0), axis=1, keepdims=True)


def plane_slots(own, one_low):
    return jnp.where(one_low, 0, own - 1), jnp.where(one_low, own - 1, 0)


def choose(flag, yes, no):
    return jnp.where(jnp.broadcast_to(flag, yes.shape), yes, no)


def far_row(lat_odd):
    return H * lat_odd


def near_row(lat_odd):
    return H * (1 - lat_odd)


def normed(widened, gain):
    mean_square = jnp.mean(widened * widened, axis=-1, keepdims=True)
    return (widened * lax.rsqrt(mean_square + EPSILON) * gain).astype(BF16)


def norm_kernel(is_far, field, gain, out):
    _, lat_odd = here()
    first = far_row(lat_odd) if is_far else near_row(lat_odd)
    for slot in range(out.shape[0]):
        for h in range(H):
            out[slot, h] = normed(field[slot, first + h].astype(F32), gain[0:1, :])


def tap_map_kernel(values, weight, out):
    channels = weight.shape[-1]
    rows = values.shape[0]

    def one(index, carry):
        row = index // TAPS
        tap = index % TAPS
        total = None
        for k in range(K):
            part = values[row, tap * K + k] * weight[k * channels : (k + 1) * channels, :].astype(F32)
            total = part if total is None else total + part
        out[row, pl.ds(pl.multiple_of(tap * channels, channels), channels), :] = total.astype(BF16)
        return carry

    lax.fori_loop(0, rows * TAPS, one, 0)


def stage(scratch, place, refs, planes, firsts):
    for ref, plane, first in zip(refs, planes, firsts):
        lons = ref.shape[2]
        for h in range(H):
            value = ref[plane, h].astype(F32)
            scratch[place, first + h, pl.ds(PAD, lons), :] = value
            scratch[place, first + h, pl.ds(0, PAD), :] = value[lons - PAD :]
            scratch[place, first + h, pl.ds(PAD + lons, PAD), :] = value[:PAD]


def disco_rows(scratch, places, row, table, weights, lons):
    entries = table[pl.ds(row, 1), :]
    taps = [(row + entries[0, tap] + H, entries[0, TAPS + tap] + PAD) for tap in range(TAPS)]
    for place in places:
        parts = [scratch[place, source, pl.ds(start, lons), :].astype(BF16) for source, start in taps]
        total = jnp.dot(jnp.concatenate(parts, axis=1), weights[row], preferred_element_type=F32)
        yield total.astype(BF16)


def places_of(is_far):
    one_low, lat_odd = here()
    beyond = 3 * H * lat_odd if is_far else 3 * H * (1 - lat_odd)
    first = far_row(lat_odd) if is_far else near_row(lat_odd)
    return one_low, first, (H + far_row(lat_odd), H + near_row(lat_odd), beyond)


def ends_kernel(is_far, slotted, level_count, table, far, near, got, weights, one, two, scratch):
    one_low, first, at = places_of(is_far)
    for place in range(scratch.shape[0]):
        stage(scratch, place, (far, near, got), (place,) * 3, at)
    places = plane_slots(own_levels(level_count)[0, 0], one_low) if slotted else plane_slots(2, one_low)

    def each(h, carry):
        one[h], two[h] = disco_rows(scratch, places, first + h, table, weights, far.shape[2])
        return carry

    lax.fori_loop(0, H, each, 0, unroll=True)


def middle_kernel(is_far, planes, table, far, near, got, weights, one, two, current, mixing, gain, *rest):
    middle, new = rest[:2]
    scratch = rest[-1]
    one_low, first, at = places_of(is_far)
    stage(scratch, 0, (far, near, got), planes, at)

    def each(h, carry):
        (m,) = disco_rows(scratch, (0,), first + h, table, weights, far.shape[2])
        middle[h] = m
        below, above = jnp.where(one_low, one[h], two[h]), jnp.where(one_low, two[h], one[h])
        old = current[1, first + h] if len(current.shape) == 4 else current[h]
        x = (old.astype(F32) + mix(below, m, above, mixing[...])).astype(BF16)
        new[h] = x
        if len(rest) == 4:
            rest[2][0, h] = normed(x.astype(F32), gain[1:2, :])
        return carry

    lax.fori_loop(0, H, each, 0, unroll=True)


def gelu(v):
    return 0.5 * v * (1.0 + lax.erf(v * 0.7071067811865476))


def mix(below, disco, above, weight):
    stacked = jnp.concatenate([below, disco, above], axis=1)
    return gelu(jnp.dot(stacked, weight, preferred_element_type=F32))


def ends_mixed(h, own, one_low, one, two, middle, got_one, got_two, weight):
    channels = weight.shape[1]

    def block(upper):
        return weight[pl.ds(pl.multiple_of(jnp.where(upper, 2 * channels, 0), channels), channels), :]

    low, centre, high = block(one_low), weight[channels : 2 * channels, :], block(jnp.logical_not(one_low))
    a, b, m, outer_a, outer_b = one[h], two[h], middle[h], got_one[h], got_two[h]
    inside_a = choose(own == 1, outer_b, choose(own == 3, m, b))
    inside_b = choose(own == 1, outer_a, choose(own == 3, m, a))
    value_a = mix(outer_a, a, inside_a, jnp.concatenate([high, centre, low], axis=0))
    value_b = mix(outer_b, b, inside_b, jnp.concatenate([low, centre, high], axis=0))
    return value_a, value_b


def mix_kernel(is_far, level_count, current, one, two, middle, got_one, got_two, weight, gain, middle_edge, new, edge):
    own = own_levels(level_count)
    one_low, lat_odd = here()
    first = far_row(lat_odd) if is_far else near_row(lat_odd)

    def each(h, carry):
        low, centre, high = [current[slot, first + h] for slot in range(3)]
        top = choose(own == 3, high, choose(own == 2, centre, low))
        old = jnp.where(one_low, low, top), jnp.where(one_low, top, low)
        values = ends_mixed(h, own, one_low, one, two, middle, got_one, got_two, weight)
        for plane, value in enumerate(values):
            x = (old[plane].astype(F32) + value).astype(BF16)
            new[plane, h] = x
            edge[jnp.where(one_low, plane, 1 - plane), h] = normed(x.astype(F32), gain[1:2, :])
        if not is_far:
            edge[2, h] = middle_edge[0, h]
        return carry

    lax.fori_loop(0, H, each, 0, unroll=True)


def last_kernel(level_count, current, one, two, middle, got_one, got_two, weight, out):
    own = own_levels(level_count)
    one_low, _ = here()

    def each(h, carry):
        for plane, value in enumerate(ends_mixed(h, own, one_low, one, two, middle, got_one, got_two, weight)):
            out[plane, h] = (current[plane, h].astype(F32) + value).astype(BF16)
        return carry

    lax.fori_loop(0, H, each, 0, unroll=True)


def final_kernel(
    level_count, current, one, two, middle, got_one, got_two, weight, new_middle, near_ends, near_middle, out, rows, sems
):
    own = own_levels(level_count)
    one_low, lat_odd = here()
    near, far = near_row(lat_odd), far_row(lat_odd)

    copies = []

    def send(row, part):
        for slot in range(out.shape[0]):
            copies.append(pltpu.make_async_copy(rows.at[slot, row], out.at[slot, row], sems.at[part, slot]))
            copies[-1].start()

    def put(row, a, b, m):
        bottom, top = jnp.where(one_low, a, b), jnp.where(one_low, b, a)
        zero = jnp.zeros_like(m)
        rows[0, row] = bottom
        rows[1, row] = choose(own == 3, m, choose(own == 2, top, zero))
        rows[2, row] = choose(own == 3, top, zero)

    for h in range(H):
        put(near + h, near_ends[0, h], near_ends[1, h], near_middle[h])
        send(near + h, h)
    for h in range(H):
        values = ends_mixed(h, own, one_low, one, two, middle, got_one, got_two, weight)
        a, b = [(current[plane, h].astype(F32) + value).astype(BF16) for plane, value in enumerate(values)]
        put(far + h, a, b, new_middle[h])
        send(far + h, H + h)
    for copy in copies:
        copy.wait()


def pairs(count, first):
    found = [(i, i + 1) for i in range(first, count - 1, 2)]
    return found + [(j, i) for i, j in found]


def on_device(field, level_count, tap_rows, tap_lons, tap_values, norm_gain, disco_weight, vert_weight):
    slots, rows, lons, channels = field.shape
    lats, levs = lax.axis_size("lat"), lax.axis_size("lev")
    near_pairs, far_pairs = pairs(lats, 0), pairs(lats, 1)
    one_pairs, two_pairs = [
        [(a * lats + lat, b * lats + lat) for lat in range(lats) for a, b in pairs(levs, (lat + turn) % 2)] for turn in (0, 1)
    ]
    plane = jax.ShapeDtypeStruct((H, lons, channels), BF16)

    def edge(planes):
        return jax.ShapeDtypeStruct((planes, H, lons, channels), BF16)

    first_row = lax.axis_index("lat") * rows
    row_part = lax.dynamic_slice_in_dim(tap_rows, first_row, rows, 0)
    lon_part = lax.dynamic_slice_in_dim(tap_lons, first_row, rows, 0)
    table = jnp.concatenate([row_part, lon_part], axis=1)
    counts = level_count.reshape(1, -1)
    value_part = lax.dynamic_slice_in_dim(tap_values, first_row, rows, 0).reshape(rows, TAPS * K)

    def maps_of(p, after=()):
        shape = jax.ShapeDtypeStruct((rows, TAPS * channels, channels), BF16)
        return call(tap_map_kernel, shape, [SMEM, VMEM], after=after, cost=10**10 if p == 0 else 1)(value_part, disco_weight[p])

    def staged(planes):
        scratch = pltpu.VMEM((planes, rows + 2 * H, lons + 2 * PAD, channels), F32)
        return [scratch]

    hbm = pl.BlockSpec(memory_space=pltpu.HBM)

    def first_norm(is_far, after=()):
        kernel = functools.partial(norm_kernel, is_far)
        return call(kernel, edge(slots), [VMEM, VMEM], after=after)(field, norm_gain)

    far = first_norm(True)
    near = first_norm(False, [far])
    near_got = lax.ppermute(near, "lat", near_pairs)
    far_got = lax.ppermute(far, "lat", far_pairs)
    maps = maps_of(0, [near])

    ends_edges = middle_edges = (far, near, far_got, near_got)
    middle_at = ((1, 1, 1), (1, 1, 1))
    ends_now, middle_now = (field, field), (field, field)
    for p in range(PASSES):
        last = p + 1 == PASSES
        done, after = [], []
        for is_far in (False, True):
            far, near, far_got, near_got = ends_edges
            one, two = call(
                functools.partial(ends_kernel, is_far, p == 0),
                [plane] * 2,
                [VMEM] * 6,
                staged(slots if p == 0 else 2),
                after=after,
            )(counts, table, far, near, far_got if is_far else near_got, maps)
            got_one = lax.ppermute(one, ("lev", "lat"), one_pairs)
            got_two = lax.ppermute(two, ("lev", "lat"), two_pairs)
            far, near, far_got, near_got = middle_edges
            made = call(
                functools.partial(middle_kernel, is_far, middle_at[is_far]),
                [plane] * 2 + [edge(1)] * (not last),
                [VMEM] * 10,
                staged(1),
            )(
                table, far, near, far_got if is_far else near_got, maps,
                one, two, middle_now[is_far], vert_weight[p], norm_gain,
            )
            after = [made[0], one, two]
            done.append(((one, two, made[0], got_one, got_two, vert_weight[p]), made[1:]))
        (near_ends, near_made), (far_ends, far_made) = done
        if last:
            near_rows = call(last_kernel, edge(2), [VMEM] * 8, after=after)(counts, ends_now[0], *near_ends)
            return call(
                final_kernel,
                jax.ShapeDtypeStruct(field.shape, BF16),
                [VMEM] * 11,
                [pltpu.VMEM(field.shape, BF16), pltpu.SemaphoreType.DMA((2 * H, slots))],
                out_specs=hbm,
            )(counts, ends_now[1], *far_ends, far_made[0], near_rows, near_made[0])
        middle_far = far_made[1]
        middle_far_got = lax.ppermute(middle_far, "lat", far_pairs)
        maps = maps_of(p + 1, after)
        new_near, near = call(functools.partial(mix_kernel, False), [edge(2), edge(3)], [VMEM] * 10, after=[maps])(
            counts, field, *near_ends, norm_gain, near_made[1]
        )
        near_got = lax.ppermute(near, "lat", near_pairs)
        new_far, far = call(functools.partial(mix_kernel, True), [edge(2), edge(2)], [VMEM] * 10, after=[near], cost=10**10)(
            counts, field, *far_ends, norm_gain, middle_far
        )
        far_got = lax.ppermute(far, "lat", far_pairs)
        ends_edges = (far, near, far_got, near_got)
        middle_edges = (middle_far, near, middle_far_got, near_got)
        middle_at = ((0, 2, 2), (0, 2, 0))
        ends_now, middle_now = (new_near, new_far), (near_made[0], far_made[0])


def solution(mesh):
    return jax.shard_map(
        on_device,
        mesh=mesh,
        in_specs=(P("lev", "lat", None, None), P(), P(), P(), P(), P(), P(), P()),
        out_specs=P("lev", "lat", None, None),
        check_vma=False,
    )
```

time: 81.4 us -> 77.8 us (0.956)
  the two profiles are of different devices: /device:TPU:23 before, /device:TPU:6 now
where the time goes in v4:
time: 77.8 us; the launch traced here: 77.3 us
  starting transfers between devices  43 us (55%)
  Pallas kernels  19.1 us (25%)
  waiting for transfers between devices  11.3 us (15%)
  local copies, waits for them, and re-layouts  3.35 us (4%)
    ppermute x4, starting transfers between devices, on_device(): got_one = lax.ppermute(one, ('lev', 'lat'), one_pairs)  23.9 us
    pallas_call x16, Pallas kernels, call(): return lambda *operands: made(*operands, *after)  19.1 us
    ppermute x2, starting transfers between devices, on_device(): far_got = lax.ppermute(far, 'lat', far_pairs)  9.23 us
    ppermute x4, waiting for transfers between devices, on_device(): got_one = lax.ppermute(one, ('lev', 'lat'), one_pairs)  8.37 us
    ppermute x2, starting transfers between devices, on_device(): near_got = lax.ppermute(near, 'lat', near_pairs)  5.35 us
    ppermute x2, waiting for transfers between devices, on_device(): far_got = lax.ppermute(far, 'lat', far_pairs)  2.96 us
    ppermute x4, starting transfers between devices, on_device(): got_two = lax.ppermute(two, ('lev', 'lat'), two_pairs)  2.69 us
    unnamed x20, local copies, waits for them, and re-layouts  2.14 us
  transfers between devices with their start and end apart: 13, of which 2 were waited for; matrix products, arithmetic and copies ran while one was open for 2% of the time, Pallas kernels for 22%

profile of v4, /device:TPU:6, one launch (start us, length us, event | category | flops | bytes accessed | tf_op | source)
XLA Modules:
  0.0 77.3 jit_solution(15127003601471640319)
XLA Ops:
  0.0 1.2 %copy-done.1 = bf16[3,4,360,128]{3,2,1,0:T(8,128)(2,1)S(1)} copy-done((bf16[3,4,360,128]{3,2,1,0:T(8,128)(2,1)S(1)}, bf16[3,4,360,128]{3,2,1,0:T(8,128)(2,1)}, u32[]{:S(2)}) %copy-start.1) | copy-done | bytes 1105944
  2.3 3.7 %collective-permute-start = (bf16[3,2,360,128]{3,2,1,0:T(8,128)(2,1)S(1)}, bf16[3,2,360,128]{3,2,1,0:T(8,128)(2,1)S(1)}, u32[]{:S(2)}, u32[]{:S(2)}) collective-permute-start(bf16[3,2,360,128]{3,2,1,0:T(8,128)(2,1)S(1)} %shard_map.82.refs_2_.refs_1_), channel_id=1, source_target_pairs={{1,2},{3,4},{5,6},{7,8},{9,10},{11,12},{13,14},{15,16},{17,18},{19... | collective-permute-start | bytes 1658888 | tf_op jit(solution)/shard_map/ppermute | solution.py:289
  7.1 1.7 %shard_map.84.refs_5_.refs_4_ = bf16[4,1024,128]{2,1,0:T(8,128)(2,1)S(1)} custom-call(f32[4,32]{1,0:T(4,128)S(1)} %copy.15.refs_0_, bf16[512,128]{1,0:T(8,128)(2,1)S(1)} %get-tuple-element.50.refs_1_, bf16[3,2,360,128]{3,2,1,0:T(8,128)(2,1)S(1)} %shard_map.83.refs_2_.refs_3_), custom_call_target="tpu_custom_call" | custom-call | flops 10000000000 | bytes 1 | tf_op jit(solution)/shard_map/pallas_call | solution.py:40
  9.2 1.0 %slice_bitcast_fusion.2 = (bf16[384,128]{1,0:T(8,128)(2,1)S(1)}, bf16[384,128]{1,0:T(8,128)(2,1)S(1)}) fusion(bf16[2,384,128]{2,1,0:T(8,128)(2,1)} %param.15), kind=kLoop, calls=%fused_computation.2 | loop fusion | bytes 393216 | tf_op jit(solution)/shard_map/squeeze | solution.py:317
  10.2 1.2 %shard_map.85 = (bf16[2,360,128]{2,1,0:T(8,128)(2,1)S(1)}, bf16[2,360,128]{2,1,0:T(8,128)(2,1)S(1)}) custom-call(s32[1,4]{1,0:T(1,128)S(1)} %bitcast.10, s32[4,16]{1,0:T(4,128)S(1)} %pad_add_fusion.refs_1_.refs_0_, bf16[3,2,360,128]{3,2,1,0:T(8,128)(2,1)S(1)} %shard_map.82.refs_2_.refs_1_, bf16[3,2,360,128]{3,2,1,0:T(8,128)(2,1)S(1)} %shard_map.83.refs_2_.refs_3_, ...), custom_call_target="tpu_custom_call" | custom-call | flops 1 | bytes 1 | tf_op jit(solution)/shard_map/pallas_call | solution.py:40
  11.4 5.2 %collective-permute-start.4 = (bf16[2,360,128]{2,1,0:T(8,128)(2,1)S(1)}, bf16[2,360,128]{2,1,0:T(8,128)(2,1)S(1)}, u32[]{:S(2)}, u32[]{:S(2)}) collective-permute-start(bf16[2,360,128]{2,1,0:T(8,128)(2,1)S(1)} %get-tuple-element.27.refs_5_.refs_7_.refs_2_), channel_id=1, source_target_pairs={{0,64},{128,192},{64,0},{192,128},{65,129},{129,65},{2,66},{130,19... | collective-permute-start | bytes 552968 | tf_op jit(solution)/shard_map/ppermute | solution.py:307
  17.3 1.6 %shard_map.86 = (bf16[2,360,128]{2,1,0:T(8,128)(2,1)S(1)}, bf16[2,360,128]{2,1,0:T(8,128)(2,1)S(1)}, bf16[1,2,360,128]{3,2,1,0:T(8,128)(2,1)S(1)}) custom-call(s32[4,16]{1,0:T(4,128)S(1)} %pad_add_fusion.refs_1_.refs_0_, bf16[3,2,360,128]{3,2,1,0:T(8,128)(2,1)S(1)} %shard_map.82.refs_2_.refs_1_, bf16[3,2,360,128]{3,2,1,0:T(8,128)(2,1)S(1)} %shard_map.83.refs_2_.refs_3_, ...), custom_call_target="tpu_custom_call" | custom-call | flops 1 | bytes 1 | tf_op jit(solution)/shard_map/pallas_call | solution.py:40
  19.0 3.0 %collective-permute-done.refs_4_.refs_3_ = bf16[3,2,360,128]{3,2,1,0:T(8,128)(2,1)S(1)} collective-permute-done((bf16[3,2,360,128]{3,2,1,0:T(8,128)(2,1)S(1)}, bf16[3,2,360,128]{3,2,1,0:T(8,128)(2,1)S(1)}, u32[]{:S(2)}, u32[]{:S(2)}) %collective-permute-start) | collective-permute-done | bytes 552992 | tf_op jit(solution)/shard_map/ppermute | solution.py:289
  21.9 1.2 %shard_map.87 = (bf16[2,360,128]{2,1,0:T(8,128)(2,1)S(1)}, bf16[2,360,128]{2,1,0:T(8,128)(2,1)S(1)}) custom-call(s32[1,4]{1,0:T(1,128)S(1)} %bitcast.11, s32[4,16]{1,0:T(4,128)S(1)} %pad_add_fusion.refs_1_.refs_0_, bf16[3,2,360,128]{3,2,1,0:T(8,128)(2,1)S(1)} %shard_map.82.refs_2_.refs_1_, bf16[3,2,360,128]{3,2,1,0:T(8,128)(2,1)S(1)} %shard_map.83.refs_2_.refs_3_, ...), custom_call_target="tpu_custom_call" | custom-call | flops 1 | bytes 1 | tf_op jit(solution)/shard_map/pallas_call | solution.py:40
  23.1 5.3 %collective-permute-start.2 = (bf16[2,360,128]{2,1,0:T(8,128)(2,1)S(1)}, bf16[2,360,128]{2,1,0:T(8,128)(2,1)S(1)}, u32[]{:S(2)}, u32[]{:S(2)}) collective-permute-start(bf16[2,360,128]{2,1,0:T(8,128)(2,1)S(1)} %get-tuple-element.30.refs_5_.refs_3_.refs_2_), channel_id=1, source_target_pairs={{0,64},{128,192},{64,0},{192,128},{65,129},{129,65},{2,66},{130,19... | collective-permute-start | bytes 552968 | tf_op jit(solution)/shard_map/ppermute | solution.py:307
  29.2 1.6 %shard_map.88 = (bf16[2,360,128]{2,1,0:T(8,128)(2,1)S(1)}, bf16[2,360,128]{2,1,0:T(8,128)(2,1)S(1)}, bf16[1,2,360,128]{3,2,1,0:T(8,128)(2,1)S(1)}) custom-call(s32[4,16]{1,0:T(4,128)S(1)} %pad_add_fusion.refs_1_.refs_0_, bf16[3,2,360,128]{3,2,1,0:T(8,128)(2,1)S(1)} %shard_map.82.refs_2_.refs_1_, bf16[3,2,360,128]{3,2,1,0:T(8,128)(2,1)S(1)} %shard_map.83.refs_2_.refs_3_, ...), custom_call_target="tpu_custom_call" | custom-call | flops 1 | bytes 1 | tf_op jit(solution)/shard_map/pallas_call | solution.py:40
  30.8 1.7 %shard_map.89.refs_10_.refs_5_.refs_4_ = bf16[4,1024,128]{2,1,0:T(8,128)(2,1)S(1)} custom-call(f32[4,32]{1,0:T(4,128)S(1)} %copy.15.refs_0_, bf16[512,128]{1,0:T(8,128)(2,1)S(1)} %get-tuple-element.49.refs_1_, bf16[2,360,128]{2,1,0:T(8,128)(2,1)S(1)} %get-tuple-element.32.refs_2_.refs_4_, bf16[2,360,128]{2,1,0:T(8,128)(2,1)S(1)} %get-tuple-element.30.refs_5_.refs_3_.refs_2_, ...), custom_call_target="tpu_custom_call" | custom-call | flops 1 | bytes 1 | tf_op jit(solution)/shard_map/pallas_call | solution.py:40
  32.6 0.8 %shard_map.90 = (bf16[2,2,360,128]{3,2,1,0:T(8,128)(2,1)S(1)}, bf16[3,2,360,128]{3,2,1,0:T(8,128)(2,1)S(1)}) custom-call(s32[1,4]{1,0:T(1,128)S(1)} %bitcast.12, bf16[3,4,360,128]{3,2,1,0:T(8,128)(2,1)S(1)} %copy-done.2, bf16[2,360,128]{2,1,0:T(8,128)(2,1)S(1)} %get-tuple-element.27.refs_5_.refs_7_.refs_2_, ...), custom_call_target="tpu_custom_call" | custom-call | flops 1 | bytes 1 | tf_op jit(solution)/shard_map/pallas_call | solution.py:40
  33.4 4.8 %collective-permute-start.7 = (bf16[3,2,360,128]{3,2,1,0:T(8,128)(2,1)S(1)}, bf16[3,2,360,128]{3,2,1,0:T(8,128)(2,1)S(1)}, u32[]{:S(2)}, u32[]{:S(2)}) collective-permute-start(bf16[3,2,360,128]{3,2,1,0:T(8,128)(2,1)S(1)} %get-tuple-element.35.refs_10_.refs_3_.refs_2_), channel_id=1, source_target_pairs={{0,1},{2,3},{4,5},{6,7},{8,9},{10,11},{12,13},{14,15},{16,17},{18,... | collective-permute-start | bytes 1658888 | tf_op jit(solution)/shard_map/ppermute | solution.py:337
  39.0 5.6 %collective-permute-start.6 = (bf16[2,2,360,128]{3,2,1,0:T(8,128)(2,1)S(1)}, bf16[2,2,360,128]{3,2,1,0:T(8,128)(2,1)S(1)}, u32[]{:S(2)}, u32[]{:S(2)}) collective-permute-start(bf16[2,2,360,128]{3,2,1,0:T(8,128)(2,1)S(1)} %get-tuple-element.37.refs_2_), channel_id=1, source_target_pairs={{1,2},{3,4},{5,6},{7,8},{9,10},{11,12},{13,14},{15,16},{17,18},{19... | collective-permute-start | bytes 1105928 | tf_op jit(solution)/shard_map/ppermute | solution.py:341
  44.6 1.9 %collective-permute-start.8 = (bf16[1,2,360,128]{3,2,1,0:T(8,128)(2,1)S(1)}, bf16[1,2,360,128]{3,2,1,0:T(8,128)(2,1)S(1)}, u32[]{:S(2)}, u32[]{:S(2)}) collective-permute-start(bf16[1,2,360,128]{3,2,1,0:T(8,128)(2,1)S(1)} %get-tuple-element.33.refs_9_.refs_1_), channel_id=1, source_target_pairs={{1,2},{3,4},{5,6},{7,8},{9,10},{11,12},{13,14},{15,16},{17,18},{19... | collective-permute-start | bytes 552968 | tf_op jit(solution)/shard_map/ppermute | solution.py:332
  46.5 1.2 %shard_map.92 = (bf16[2,360,128]{2,1,0:T(8,128)(2,1)S(1)}, bf16[2,360,128]{2,1,0:T(8,128)(2,1)S(1)}) custom-call(s32[1,4]{1,0:T(1,128)S(1)} %bitcast.14, s32[4,16]{1,0:T(4,128)S(1)} %pad_add_fusion.refs_1_.refs_0_, bf16[2,2,360,128]{3,2,1,0:T(8,128)(2,1)S(1)} %get-tuple-element.37.refs_2_, ...), custom_call_target="tpu_custom_call" | custom-call | flops 1 | bytes 1 | tf_op jit(solution)/shard_map/pallas_call | solution.py:40
  47.7 3.8 %collective-permute-start.11 = (bf16[2,360,128]{2,1,0:T(8,128)(2,1)S(1)}, bf16[2,360,128]{2,1,0:T(8,128)(2,1)S(1)}, u32[]{:S(2)}, u32[]{:S(2)}) collective-permute-start(bf16[2,360,128]{2,1,0:T(8,128)(2,1)S(1)} %get-tuple-element.38.refs_5_.refs_7_.refs_2_), channel_id=1, source_target_pairs={{0,64},{128,192},{64,0},{192,128},{65,129},{129,65},{2,66},{130,19... | collective-permute-start | bytes 552968 | tf_op jit(solution)/shard_map/ppermute | solution.py:307
  52.2 1.5 %shard_map.93 = (bf16[2,360,128]{2,1,0:T(8,128)(2,1)S(1)}, bf16[2,360,128]{2,1,0:T(8,128)(2,1)S(1)}) custom-call(s32[4,16]{1,0:T(4,128)S(1)} %pad_add_fusion.refs_1_.refs_0_, bf16[1,2,360,128]{3,2,1,0:T(8,128)(2,1)S(1)} %get-tuple-element.33.refs_9_.refs_1_, bf16[3,2,360,128]{3,2,1,0:T(8,128)(2,1)S(1)} %get-tuple-element.35.refs_10_.refs_3_.refs_2_, ...), custom_call_target="tpu_custom_call" | custom-call | flops 1 | bytes 1 | tf_op jit(solution)/shard_map/pallas_call | solution.py:40
  53.8 1.2 %shard_map.94 = (bf16[2,360,128]{2,1,0:T(8,128)(2,1)S(1)}, bf16[2,360,128]{2,1,0:T(8,128)(2,1)S(1)}) custom-call(s32[1,4]{1,0:T(1,128)S(1)} %bitcast.15, s32[4,16]{1,0:T(4,128)S(1)} %pad_add_fusion.refs_1_.refs_0_, bf16[2,2,360,128]{3,2,1,0:T(8,128)(2,1)S(1)} %get-tuple-element.37.refs_2_, ...), custom_call_target="tpu_custom_call" | custom-call | flops 1 | bytes 1 | tf_op jit(solution)/shard_map/pallas_call | solution.py:40
  55.7 9.5 %collective-permute-start.9 = (bf16[2,360,128]{2,1,0:T(8,128)(2,1)S(1)}, bf16[2,360,128]{2,1,0:T(8,128)(2,1)S(1)}, u32[]{:S(2)}, u32[]{:S(2)}) collective-permute-start(bf16[2,360,128]{2,1,0:T(8,128)(2,1)S(1)} %get-tuple-element.42.refs_5_.refs_9_.refs_2_), channel_id=1, source_target_pairs={{0,64},{128,192},{64,0},{192,128},{65,129},{129,65},{2,66},{130,19... | collective-permute-start | bytes 552968 | tf_op jit(solution)/shard_map/ppermute | solution.py:307
  65.2 1.5 %shard_map.95 = (bf16[2,360,128]{2,1,0:T(8,128)(2,1)S(1)}, bf16[2,360,128]{2,1,0:T(8,128)(2,1)S(1)}) custom-call(s32[4,16]{1,0:T(4,128)S(1)} %pad_add_fusion.refs_1_.refs_0_, bf16[1,2,360,128]{3,2,1,0:T(8,128)(2,1)S(1)} %get-tuple-element.33.refs_9_.refs_1_, bf16[3,2,360,128]{3,2,1,0:T(8,128)(2,1)S(1)} %get-tuple-element.35.refs_10_.refs_3_.refs_2_, ...), custom_call_target="tpu_custom_call" | custom-call | flops 1 | bytes 1 | tf_op jit(solution)/shard_map/pallas_call | solution.py:40
  67.4 8.4 %collective-permute-done.9.refs_5_ = bf16[2,360,128]{2,1,0:T(8,128)(2,1)S(1)} collective-permute-done((bf16[2,360,128]{2,1,0:T(8,128)(2,1)S(1)}, bf16[2,360,128]{2,1,0:T(8,128)(2,1)S(1)}, u32[]{:S(2)}, u32[]{:S(2)}) %collective-permute-start.9) | collective-permute-done | bytes 184352 | tf_op jit(solution)/shard_map/ppermute | solution.py:307
  75.7 1.6 %shard_map.97 = bf16[3,4,360,128]{3,2,1,0:T(8,128)(2,1)} custom-call(s32[1,4]{1,0:T(1,128)S(1)} %bitcast.17, bf16[2,2,360,128]{3,2,1,0:T(8,128)(2,1)S(1)} %get-tuple-element.36.refs_1_, bf16[2,360,128]{2,1,0:T(8,128)(2,1)S(1)} %get-tuple-element.42.refs_5_.refs_9_.refs_2_, bf16[2,360,128]{2,1,0:T(8,128)(2,1)S(1)} %get-tuple-element.43.refs_6_.refs_10_.refs_3_, ...), custom_call_target="tpu_custom_call" | custom-call | flops 1 | bytes 1 | tf_op jit(solution)/shard_map/pallas_call | solution.py:40
  (44 shorter events, 6.6 us)
Async XLA Ops:
  0.0 6.9 %copy-start = (f32[256,8,4]{0,2,1:T(4,128)S(1)}, f32[256,8,4]{0,2,1:T(4,128)}, u32[]{:S(2)}) copy-start(f32[256,8,4]{0,2,1:T(4,128)} %param.12) | copy-start | bytes 98308
  0.0 1.3 %copy-start.1 = (bf16[3,4,360,128]{3,2,1,0:T(8,128)(2,1)S(1)}, bf16[3,4,360,128]{3,2,1,0:T(8,128)(2,1)}, u32[]{:S(2)}) copy-start(bf16[3,4,360,128]{3,2,1,0:T(8,128)(2,1)} %refs_1_.7) | copy-start | bytes 3317764
  1.3 0.7 copy-start.3
  2.3 4.7 %copy-start.6 = (bf16[2,512,128]{2,1,0:T(8,128)(2,1)S(1)}, bf16[2,512,128]{2,1,0:T(8,128)(2,1)}, u32[]{:S(2)}) copy-start(bf16[2,512,128]{2,1,0:T(8,128)(2,1)} %param.14) | copy-start | bytes 786436
  2.3 19.6 %collective-permute-start = (bf16[3,2,360,128]{3,2,1,0:T(8,128)(2,1)S(1)}, bf16[3,2,360,128]{3,2,1,0:T(8,128)(2,1)S(1)}, u32[]{:S(2)}, u32[]{:S(2)}) collective-permute-start(bf16[3,2,360,128]{3,2,1,0:T(8,128)(2,1)S(1)} %shard_map.82.refs_2_.refs_1_), channel_id=1, source_target_pairs={{1,2},{3,4},{5,6},{7,8},{9,10},{11,12},{13,14},{15,16},{17,18},{19... | collective-permute-start | bytes 1658888 | tf_op jit(solution)/shard_map/ppermute | solution.py:289
  6.4 3.8 %collective-permute-start.1 = (bf16[3,2,360,128]{3,2,1,0:T(8,128)(2,1)S(1)}, bf16[3,2,360,128]{3,2,1,0:T(8,128)(2,1)S(1)}, u32[]{:S(2)}, u32[]{:S(2)}) collective-permute-start(bf16[3,2,360,128]{3,2,1,0:T(8,128)(2,1)S(1)} %shard_map.83.refs_2_.refs_3_), channel_id=1, source_target_pairs={{0,1},{2,3},{4,5},{6,7},{8,9},{10,11},{12,13},{14,15},{16,17},{18,... | collective-permute-start | bytes 1658888 | tf_op jit(solution)/shard_map/ppermute | solution.py:288
  7.1 1.8 %copy-start.7 = (s32[256,8]{0,1:T(8,128)S(1)}, s32[256,8]{0,1:T(8,128)}, u32[]{:S(2)}) copy-start(s32[256,8]{0,1:T(8,128)} %param.11) | copy-start | bytes 24580
  7.1 1.8 %copy-start.8 = (s32[256,8]{0,1:T(8,128)S(1)}, s32[256,8]{0,1:T(8,128)}, u32[]{:S(2)}) copy-start(s32[256,8]{0,1:T(8,128)} %param.10) | copy-start | bytes 24580
  7.1 3.1 %copy-start.5 = (s32[4]{0:T(128)S(1)}, s32[4]{0:T(128)}, u32[]{:S(2)}) copy-start(s32[4]{0:T(128)} %param.9) | copy-start | bytes 52
  10.2 7.1 %copy-start.2 = (bf16[3,4,360,128]{3,2,1,0:T(8,128)(2,1)S(1)}, bf16[3,4,360,128]{3,2,1,0:T(8,128)(2,1)}, u32[]{:S(2)}) copy-start(bf16[3,4,360,128]{3,2,1,0:T(8,128)(2,1)} %refs_1_.7) | copy-start | bytes 3317764
  10.2 7.1 %copy-start.4 = (f32[2,128]{1,0:T(2,128)S(1)}, f32[2,128]{1,0:T(2,128)}, u32[]{:S(2)}) copy-start(f32[2,128]{1,0:T(2,128)} %refs_9_.7) | copy-start | bytes 3076
  11.4 21.1 %collective-permute-start.4 = (bf16[2,360,128]{2,1,0:T(8,128)(2,1)S(1)}, bf16[2,360,128]{2,1,0:T(8,128)(2,1)S(1)}, u32[]{:S(2)}, u32[]{:S(2)}) collective-permute-start(bf16[2,360,128]{2,1,0:T(8,128)(2,1)S(1)} %get-tuple-element.27.refs_5_.refs_7_.refs_2_), channel_id=1, source_target_pairs={{0,64},{128,192},{64,0},{192,128},{65,129},{129,65},{2,66},{130,19... | collective-permute-start | bytes 552968 | tf_op jit(solution)/shard_map/ppermute | solution.py:307
  16.6 15.9 %collective-permute-start.5 = (bf16[2,360,128]{2,1,0:T(8,128)(2,1)S(1)}, bf16[2,360,128]{2,1,0:T(8,128)(2,1)S(1)}, u32[]{:S(2)}, u32[]{:S(2)}) collective-permute-start(bf16[2,360,128]{2,1,0:T(8,128)(2,1)S(1)} %get-tuple-element.28.refs_6_.refs_8_.refs_3_), channel_id=1, source_target_pairs={{64,128},{128,64},{1,65},{129,193},{65,1},{193,129},{66,130},{130,... | collective-permute-start | bytes 552968 | tf_op jit(solution)/shard_map/ppermute | solution.py:308
  23.1 15.1 %collective-permute-start.2 = (bf16[2,360,128]{2,1,0:T(8,128)(2,1)S(1)}, bf16[2,360,128]{2,1,0:T(8,128)(2,1)S(1)}, u32[]{:S(2)}, u32[]{:S(2)}) collective-permute-start(bf16[2,360,128]{2,1,0:T(8,128)(2,1)S(1)} %get-tuple-element.30.refs_5_.refs_3_.refs_2_), channel_id=1, source_target_pairs={{0,64},{128,192},{64,0},{192,128},{65,129},{129,65},{2,66},{130,19... | collective-permute-start | bytes 552968 | tf_op jit(solution)/shard_map/ppermute | solution.py:307
  28.5 9.7 %collective-permute-start.3 = (bf16[2,360,128]{2,1,0:T(8,128)(2,1)S(1)}, bf16[2,360,128]{2,1,0:T(8,128)(2,1)S(1)}, u32[]{:S(2)}, u32[]{:S(2)}) collective-permute-start(bf16[2,360,128]{2,1,0:T(8,128)(2,1)S(1)} %get-tuple-element.31.refs_6_.refs_4_.refs_3_), channel_id=1, source_target_pairs={{64,128},{128,64},{1,65},{129,193},{65,1},{193,129},{66,130},{130,... | collective-permute-start | bytes 552968 | tf_op jit(solution)/shard_map/ppermute | solution.py:308
  33.4 13.2 %collective-permute-start.7 = (bf16[3,2,360,128]{3,2,1,0:T(8,128)(2,1)S(1)}, bf16[3,2,360,128]{3,2,1,0:T(8,128)(2,1)S(1)}, u32[]{:S(2)}, u32[]{:S(2)}) collective-permute-start(bf16[3,2,360,128]{3,2,1,0:T(8,128)(2,1)S(1)} %get-tuple-element.35.refs_10_.refs_3_.refs_2_), channel_id=1, source_target_pairs={{0,1},{2,3},{4,5},{6,7},{8,9},{10,11},{12,13},{14,15},{16,17},{18,... | collective-permute-start | bytes 1658888 | tf_op jit(solution)/shard_map/ppermute | solution.py:337
  39.0 14.8 %collective-permute-start.6 = (bf16[2,2,360,128]{3,2,1,0:T(8,128)(2,1)S(1)}, bf16[2,2,360,128]{3,2,1,0:T(8,128)(2,1)S(1)}, u32[]{:S(2)}, u32[]{:S(2)}) collective-permute-start(bf16[2,2,360,128]{3,2,1,0:T(8,128)(2,1)S(1)} %get-tuple-element.37.refs_2_), channel_id=1, source_target_pairs={{1,2},{3,4},{5,6},{7,8},{9,10},{11,12},{13,14},{15,16},{17,18},{19... | collective-permute-start | bytes 1105928 | tf_op jit(solution)/shard_map/ppermute | solution.py:341
  44.6 20.6 %collective-permute-start.8 = (bf16[1,2,360,128]{3,2,1,0:T(8,128)(2,1)S(1)}, bf16[1,2,360,128]{3,2,1,0:T(8,128)(2,1)S(1)}, u32[]{:S(2)}, u32[]{:S(2)}) collective-permute-start(bf16[1,2,360,128]{3,2,1,0:T(8,128)(2,1)S(1)} %get-tuple-element.33.refs_9_.refs_1_), channel_id=1, source_target_pairs={{1,2},{3,4},{5,6},{7,8},{9,10},{11,12},{13,14},{15,16},{17,18},{19... | collective-permute-start | bytes 552968 | tf_op jit(solution)/shard_map/ppermute | solution.py:332
  47.7 19.0 %collective-permute-start.11 = (bf16[2,360,128]{2,1,0:T(8,128)(2,1)S(1)}, bf16[2,360,128]{2,1,0:T(8,128)(2,1)S(1)}, u32[]{:S(2)}, u32[]{:S(2)}) collective-permute-start(bf16[2,360,128]{2,1,0:T(8,128)(2,1)S(1)} %get-tuple-element.38.refs_5_.refs_7_.refs_2_), channel_id=1, source_target_pairs={{0,64},{128,192},{64,0},{192,128},{65,129},{129,65},{2,66},{130,19... | collective-permute-start | bytes 552968 | tf_op jit(solution)/shard_map/ppermute | solution.py:307
  51.6 15.2 %collective-permute-start.12 = (bf16[2,360,128]{2,1,0:T(8,128)(2,1)S(1)}, bf16[2,360,128]{2,1,0:T(8,128)(2,1)S(1)}, u32[]{:S(2)}, u32[]{:S(2)}) collective-permute-start(bf16[2,360,128]{2,1,0:T(8,128)(2,1)S(1)} %get-tuple-element.39.refs_6_.refs_8_.refs_3_), channel_id=1, source_target_pairs={{64,128},{128,64},{1,65},{129,193},{65,1},{193,129},{66,130},{130,... | collective-permute-start | bytes 552968 | tf_op jit(solution)/shard_map/ppermute | solution.py:308
  55.0 12.4 %collective-permute-start.10 = (bf16[2,360,128]{2,1,0:T(8,128)(2,1)S(1)}, bf16[2,360,128]{2,1,0:T(8,128)(2,1)S(1)}, u32[]{:S(2)}, u32[]{:S(2)}) collective-permute-start(bf16[2,360,128]{2,1,0:T(8,128)(2,1)S(1)} %get-tuple-element.43.refs_6_.refs_10_.refs_3_), channel_id=1, source_target_pairs={{64,128},{128,64},{1,65},{129,193},{65,1},{193,129},{66,130},{130,... | collective-permute-start | bytes 552968 | tf_op jit(solution)/shard_map/ppermute | solution.py:308
  55.7 20.1 %collective-permute-start.9 = (bf16[2,360,128]{2,1,0:T(8,128)(2,1)S(1)}, bf16[2,360,128]{2,1,0:T(8,128)(2,1)S(1)}, u32[]{:S(2)}, u32[]{:S(2)}) collective-permute-start(bf16[2,360,128]{2,1,0:T(8,128)(2,1)S(1)} %get-tuple-element.42.refs_5_.refs_9_.refs_2_), channel_id=1, source_target_pairs={{0,64},{128,192},{64,0},{192,128},{65,129},{129,65},{2,66},{130,19... | collective-permute-start | bytes 552968 | tf_op jit(solution)/shard_map/ppermute | solution.py:307

commit v5 on v4

--- a/solution.py
+++ b/solution.py
@@ -294,31 +294,39 @@
     ends_now, middle_now = (field, field), (field, field)
     for p in range(PASSES):
         last = p + 1 == PASSES
-        done, after = [], []
-        for is_far in (False, True):
+        def ends(is_far, after):
             far, near, far_got, near_got = ends_edges
-            one, two = call(
-                functools.partial(ends_kernel, is_far, p == 0),
-                [plane] * 2,
-                [VMEM] * 6,
-                staged(slots if p == 0 else 2),
-                after=after,
-            )(counts, table, far, near, far_got if is_far else near_got, maps)
-            got_one = lax.ppermute(one, ("lev", "lat"), one_pairs)
-            got_two = lax.ppermute(two, ("lev", "lat"), two_pairs)
+            one, two = call(functools.partial(ends_kernel, is_far, p == 0), [plane] * 2, [VMEM] * 6, staged(slots if p == 0 else 2), after=after)(
+                counts, table, far, near, far_got if is_far else near_got, maps
+            )
+            return one, two, lax.ppermute(one, ("lev", "lat"), one_pairs), lax.ppermute(two, ("lev", "lat"), two_pairs)
+
+        def middles(is_far, one, two, after):
             far, near, far_got, near_got = middle_edges
-            made = call(
+            return call(
                 functools.partial(middle_kernel, is_far, middle_at[is_far]),
                 [plane] * 2 + [edge(1)] * (not last),
                 [VMEM] * 10,
                 staged(1),
+                after=after,
             )(
-                table, far, near, far_got if is_far else near_got, maps,
-                one, two, middle_now[is_far], vert_weight[p], norm_gain,
+                table, far, near, far_got if is_far else near_got, maps, one, two, middle_now[is_far], vert_weight[p], norm_gain
             )
-            after = [made[0], one, two]
-            done.append(((one, two, made[0], got_one, got_two, vert_weight[p]), made[1:]))
-        (near_ends, near_made), (far_ends, far_made) = done
+
+        if last:
+            near_one, near_two, *near_all_got = ends(False, [])
+            far_one, far_two, *far_all_got = ends(True, [near_one, near_two])
+            near_made = middles(False, near_one, near_two, [far_one, far_two])
+            far_made = middles(True, far_one, far_two, [near_made[0], far_one, far_two])
+        else:
+            near_one, near_two, *near_all_got = ends(False, [])
+            near_made = middles(False, near_one, near_two, [])
+            far_one, far_two, *far_all_got = ends(True, [near_made[0], near_one, near_two])
+            far_made = middles(True, far_one, far_two, [])
+        after = [far_made[0], far_one, far_two]
+        near_ends = (near_one, near_two, near_made[0], *near_all_got, vert_weight[p])
+        far_ends = (far_one, far_two, far_made[0], *far_all_got, vert_weight[p])
+        near_made, far_made = near_made[1:], far_made[1:]
         if last:
             near_rows = call(last_kernel, edge(2), [VMEM] * 8, after=after)(counts, ends_now[0], *near_ends)
             return call(

time: 77.8 us -> 77.2 us (level)
  the two profiles are of different devices: /device:TPU:6 before, /device:TPU:49 now
where the time goes in v5:
time: 77.2 us; the launch traced here: 76.1 us
  starting transfers between devices  45 us (58%)
  Pallas kernels  19.2 us (25%)
  waiting for transfers between devices  7.95 us (10%)
  local copies, waits for them, and re-layouts  3.35 us (4%)
    ppermute x4, starting transfers between devices, ends(): lax.ppermute(two, ('lev', 'lat'), two_pairs)  32.3 us
    pallas_call x16, Pallas kernels, call(): return lambda *operands: made(*operands, *after)  19.2 us
    ppermute x4, waiting for transfers between devices, ends(): lax.ppermute(two, ('lev', 'lat'), two_pairs)  7.93 us
    ppermute x2, starting transfers between devices, on_device(): far_got = lax.ppermute(far, 'lat', far_pairs)  6.76 us
    ppermute x1, starting transfers between devices, on_device(): middle_far_got = lax.ppermute(middle_far, 'lat', far_pairs)  3.06 us
    ppermute x4, starting transfers between devices, ends(): lax.ppermute(one, ('lev', 'lat'), one_pairs)  2.69 us
    unnamed x20, local copies, waits for them, and re-layouts  2.13 us
  transfers between devices with their start and end apart: 13, of which 2 were waited for; matrix products, arithmetic and copies ran while one was open for 2% of the time, Pallas kernels for 23%

profile of v5, /device:TPU:49, one launch (start us, length us, event | category | flops | bytes accessed | tf_op | source)
XLA Modules:
  0.0 76.1 jit_solution(8721855732419762867)
XLA Ops:
  0.0 1.2 %copy-done.1 = bf16[3,4,360,128]{3,2,1,0:T(8,128)(2,1)S(1)} copy-done((bf16[3,4,360,128]{3,2,1,0:T(8,128)(2,1)S(1)}, bf16[3,4,360,128]{3,2,1,0:T(8,128)(2,1)}, u32[]{:S(2)}) %copy-start.1) | copy-done | bytes 1105944
  1.3 0.7 copy-done.3
  2.3 3.4 %collective-permute-start = (bf16[3,2,360,128]{3,2,1,0:T(8,128)(2,1)S(1)}, bf16[3,2,360,128]{3,2,1,0:T(8,128)(2,1)S(1)}, u32[]{:S(2)}, u32[]{:S(2)}) collective-permute-start(bf16[3,2,360,128]{3,2,1,0:T(8,128)(2,1)S(1)} %shard_map.82.refs_2_.refs_1_), channel_id=1, source_target_pairs={{1,2},{3,4},{5,6},{7,8},{9,10},{11,12},{13,14},{15,16},{17,18},{19... | collective-permute-start | bytes 1658888 | tf_op jit(solution)/shard_map/ppermute | solution.py:289
  6.4 1.7 %shard_map.84.refs_5_.refs_4_ = bf16[4,1024,128]{2,1,0:T(8,128)(2,1)S(1)} custom-call(f32[4,32]{1,0:T(4,128)S(1)} %copy.15.refs_0_, bf16[512,128]{1,0:T(8,128)(2,1)S(1)} %get-tuple-element.50.refs_1_, bf16[3,2,360,128]{3,2,1,0:T(8,128)(2,1)S(1)} %shard_map.83.refs_2_.refs_3_), custom_call_target="tpu_custom_call" | custom-call | flops 10000000000 | bytes 1 | tf_op jit(solution)/shard_map/pallas_call | solution.py:40
  8.5 1.0 %slice_bitcast_fusion.2 = (bf16[384,128]{1,0:T(8,128)(2,1)S(1)}, bf16[384,128]{1,0:T(8,128)(2,1)S(1)}) fusion(bf16[2,384,128]{2,1,0:T(8,128)(2,1)} %param.15), kind=kLoop, calls=%fused_computation.2 | loop fusion | bytes 393216 | tf_op jit(solution)/shard_map/squeeze | solution.py:313
  9.5 1.2 %shard_map.85 = (bf16[2,360,128]{2,1,0:T(8,128)(2,1)S(1)}, bf16[2,360,128]{2,1,0:T(8,128)(2,1)S(1)}) custom-call(s32[1,4]{1,0:T(1,128)S(1)} %bitcast.10, s32[4,16]{1,0:T(4,128)S(1)} %pad_add_fusion.refs_1_.refs_0_, bf16[3,2,360,128]{3,2,1,0:T(8,128)(2,1)S(1)} %shard_map.82.refs_2_.refs_1_, bf16[3,2,360,128]{3,2,1,0:T(8,128)(2,1)S(1)} %shard_map.83.refs_2_.refs_3_, ...), custom_call_target="tpu_custom_call" | custom-call | flops 1 | bytes 1 | tf_op jit(solution)/shard_map/pallas_call | solution.py:40
  11.4 10.3 %collective-permute-start.5 = (bf16[2,360,128]{2,1,0:T(8,128)(2,1)S(1)}, bf16[2,360,128]{2,1,0:T(8,128)(2,1)S(1)}, u32[]{:S(2)}, u32[]{:S(2)}) collective-permute-start(bf16[2,360,128]{2,1,0:T(8,128)(2,1)S(1)} %get-tuple-element.28.refs_6_.refs_8_.refs_3_), channel_id=1, source_target_pairs={{64,128},{128,64},{1,65},{129,193},{65,1},{193,129},{66,130},{130,... | collective-permute-start | bytes 552968 | tf_op jit(solution)/shard_map/ppermute | solution.py:302
  21.8 1.6 %shard_map.86 = (bf16[2,360,128]{2,1,0:T(8,128)(2,1)S(1)}, bf16[2,360,128]{2,1,0:T(8,128)(2,1)S(1)}, bf16[1,2,360,128]{3,2,1,0:T(8,128)(2,1)S(1)}) custom-call(s32[4,16]{1,0:T(4,128)S(1)} %pad_add_fusion.refs_1_.refs_0_, bf16[3,2,360,128]{3,2,1,0:T(8,128)(2,1)S(1)} %shard_map.82.refs_2_.refs_1_, bf16[3,2,360,128]{3,2,1,0:T(8,128)(2,1)S(1)} %shard_map.83.refs_2_.refs_3_, ...), custom_call_target="tpu_custom_call" | custom-call | flops 1 | bytes 1 | tf_op jit(solution)/shard_map/pallas_call | solution.py:40
  23.4 1.2 %shard_map.87 = (bf16[2,360,128]{2,1,0:T(8,128)(2,1)S(1)}, bf16[2,360,128]{2,1,0:T(8,128)(2,1)S(1)}) custom-call(s32[1,4]{1,0:T(1,128)S(1)} %bitcast.11, s32[4,16]{1,0:T(4,128)S(1)} %pad_add_fusion.refs_1_.refs_0_, bf16[3,2,360,128]{3,2,1,0:T(8,128)(2,1)S(1)} %shard_map.82.refs_2_.refs_1_, bf16[3,2,360,128]{3,2,1,0:T(8,128)(2,1)S(1)} %shard_map.83.refs_2_.refs_3_, ...), custom_call_target="tpu_custom_call" | custom-call | flops 1 | bytes 1 | tf_op jit(solution)/shard_map/pallas_call | solution.py:40
  25.4 8.3 %collective-permute-start.3 = (bf16[2,360,128]{2,1,0:T(8,128)(2,1)S(1)}, bf16[2,360,128]{2,1,0:T(8,128)(2,1)S(1)}, u32[]{:S(2)}, u32[]{:S(2)}) collective-permute-start(bf16[2,360,128]{2,1,0:T(8,128)(2,1)S(1)} %get-tuple-element.31.refs_6_.refs_4_.refs_3_), channel_id=1, source_target_pairs={{64,128},{128,64},{1,65},{129,193},{65,1},{193,129},{66,130},{130,... | collective-permute-start | bytes 552968 | tf_op jit(solution)/shard_map/ppermute | solution.py:302
  33.7 1.6 %shard_map.88 = (bf16[2,360,128]{2,1,0:T(8,128)(2,1)S(1)}, bf16[2,360,128]{2,1,0:T(8,128)(2,1)S(1)}, bf16[1,2,360,128]{3,2,1,0:T(8,128)(2,1)S(1)}) custom-call(s32[4,16]{1,0:T(4,128)S(1)} %pad_add_fusion.refs_1_.refs_0_, bf16[3,2,360,128]{3,2,1,0:T(8,128)(2,1)S(1)} %shard_map.82.refs_2_.refs_1_, bf16[3,2,360,128]{3,2,1,0:T(8,128)(2,1)S(1)} %shard_map.83.refs_2_.refs_3_, ...), custom_call_target="tpu_custom_call" | custom-call | flops 1 | bytes 1 | tf_op jit(solution)/shard_map/pallas_call | solution.py:40
  35.3 1.7 %shard_map.89.refs_10_.refs_5_.refs_4_ = bf16[4,1024,128]{2,1,0:T(8,128)(2,1)S(1)} custom-call(f32[4,32]{1,0:T(4,128)S(1)} %copy.15.refs_0_, bf16[512,128]{1,0:T(8,128)(2,1)S(1)} %get-tuple-element.49.refs_1_, bf16[2,360,128]{2,1,0:T(8,128)(2,1)S(1)} %get-tuple-element.32.refs_2_.refs_4_, bf16[2,360,128]{2,1,0:T(8,128)(2,1)S(1)} %get-tuple-element.30.refs_5_.refs_3_.refs_2_, ...), custom_call_target="tpu_custom_call" | custom-call | flops 1 | bytes 1 | tf_op jit(solution)/shard_map/pallas_call | solution.py:40
  37.1 0.8 %shard_map.90 = (bf16[2,2,360,128]{3,2,1,0:T(8,128)(2,1)S(1)}, bf16[3,2,360,128]{3,2,1,0:T(8,128)(2,1)S(1)}) custom-call(s32[1,4]{1,0:T(1,128)S(1)} %bitcast.12, bf16[3,4,360,128]{3,2,1,0:T(8,128)(2,1)S(1)} %copy-done.2, bf16[2,360,128]{2,1,0:T(8,128)(2,1)S(1)} %get-tuple-element.27.refs_5_.refs_7_.refs_2_, ...), custom_call_target="tpu_custom_call" | custom-call | flops 1 | bytes 1 | tf_op jit(solution)/shard_map/pallas_call | solution.py:40
  38.1 0.8 %shard_map.91 = (bf16[2,2,360,128]{3,2,1,0:T(8,128)(2,1)S(1)}, bf16[2,2,360,128]{3,2,1,0:T(8,128)(2,1)S(1)}) custom-call(s32[1,4]{1,0:T(1,128)S(1)} %bitcast.13, bf16[3,4,360,128]{3,2,1,0:T(8,128)(2,1)S(1)} %copy-done.2, bf16[2,360,128]{2,1,0:T(8,128)(2,1)S(1)} %get-tuple-element.30.refs_5_.refs_3_.refs_2_, ...), custom_call_target="tpu_custom_call" | custom-call | flops 10000000000 | bytes 1 | tf_op jit(solution)/shard_map/pallas_call | solution.py:40
  38.9 3.4 %collective-permute-start.6 = (bf16[2,2,360,128]{3,2,1,0:T(8,128)(2,1)S(1)}, bf16[2,2,360,128]{3,2,1,0:T(8,128)(2,1)S(1)}, u32[]{:S(2)}, u32[]{:S(2)}) collective-permute-start(bf16[2,2,360,128]{3,2,1,0:T(8,128)(2,1)S(1)} %get-tuple-element.37.refs_2_), channel_id=1, source_target_pairs={{1,2},{3,4},{5,6},{7,8},{9,10},{11,12},{13,14},{15,16},{17,18},{19... | collective-permute-start | bytes 1105928 | tf_op jit(solution)/shard_map/ppermute | solution.py:349
  42.3 3.1 %collective-permute-start.8 = (bf16[1,2,360,128]{3,2,1,0:T(8,128)(2,1)S(1)}, bf16[1,2,360,128]{3,2,1,0:T(8,128)(2,1)S(1)}, u32[]{:S(2)}, u32[]{:S(2)}) collective-permute-start(bf16[1,2,360,128]{3,2,1,0:T(8,128)(2,1)S(1)} %get-tuple-element.33.refs_9_.refs_1_), channel_id=1, source_target_pairs={{1,2},{3,4},{5,6},{7,8},{9,10},{11,12},{13,14},{15,16},{17,18},{19... | collective-permute-start | bytes 552968 | tf_op jit(solution)/shard_map/ppermute | solution.py:340
  45.3 1.2 %shard_map.92 = (bf16[2,360,128]{2,1,0:T(8,128)(2,1)S(1)}, bf16[2,360,128]{2,1,0:T(8,128)(2,1)S(1)}) custom-call(s32[1,4]{1,0:T(1,128)S(1)} %bitcast.14, s32[4,16]{1,0:T(4,128)S(1)} %pad_add_fusion.refs_1_.refs_0_, bf16[2,2,360,128]{3,2,1,0:T(8,128)(2,1)S(1)} %get-tuple-element.37.refs_2_, ...), custom_call_target="tpu_custom_call" | custom-call | flops 1 | bytes 1 | tf_op jit(solution)/shard_map/pallas_call | solution.py:40
  47.2 8.8 %collective-permute-start.12 = (bf16[2,360,128]{2,1,0:T(8,128)(2,1)S(1)}, bf16[2,360,128]{2,1,0:T(8,128)(2,1)S(1)}, u32[]{:S(2)}, u32[]{:S(2)}) collective-permute-start(bf16[2,360,128]{2,1,0:T(8,128)(2,1)S(1)} %get-tuple-element.39.refs_7_.refs_6_.refs_3_), channel_id=1, source_target_pairs={{64,128},{128,64},{1,65},{129,193},{65,1},{193,129},{66,130},{130,... | collective-permute-start | bytes 552968 | tf_op jit(solution)/shard_map/ppermute | solution.py:302
  56.0 1.2 %shard_map.93 = (bf16[2,360,128]{2,1,0:T(8,128)(2,1)S(1)}, bf16[2,360,128]{2,1,0:T(8,128)(2,1)S(1)}) custom-call(s32[1,4]{1,0:T(1,128)S(1)} %bitcast.15, s32[4,16]{1,0:T(4,128)S(1)} %pad_add_fusion.refs_1_.refs_0_, bf16[2,2,360,128]{3,2,1,0:T(8,128)(2,1)S(1)} %get-tuple-element.37.refs_2_, ...), custom_call_target="tpu_custom_call" | custom-call | flops 1 | bytes 1 | tf_op jit(solution)/shard_map/pallas_call | solution.py:40
  57.9 4.8 %collective-permute-start.10 = (bf16[2,360,128]{2,1,0:T(8,128)(2,1)S(1)}, bf16[2,360,128]{2,1,0:T(8,128)(2,1)S(1)}, u32[]{:S(2)}, u32[]{:S(2)}) collective-permute-start(bf16[2,360,128]{2,1,0:T(8,128)(2,1)S(1)} %get-tuple-element.41.refs_11_.refs_6_.refs_12_.refs_10_.refs_3_), channel_id=1, source_target_pairs={{64,128},{128,64},{1,65},{129,193},{65,1},{193,129},{66,130},{130,... | collective-permute-start | bytes 552968 | tf_op jit(solution)/shard_map/ppermute | solution.py:302
  62.7 1.5 %shard_map.94 = (bf16[2,360,128]{2,1,0:T(8,128)(2,1)S(1)}, bf16[2,360,128]{2,1,0:T(8,128)(2,1)S(1)}) custom-call(s32[4,16]{1,0:T(4,128)S(1)} %pad_add_fusion.refs_1_.refs_0_, bf16[1,2,360,128]{3,2,1,0:T(8,128)(2,1)S(1)} %get-tuple-element.33.refs_9_.refs_1_, bf16[3,2,360,128]{3,2,1,0:T(8,128)(2,1)S(1)} %get-tuple-element.35.refs_10_.refs_3_.refs_2_, ...), custom_call_target="tpu_custom_call" | custom-call | flops 1 | bytes 1 | tf_op jit(solution)/shard_map/pallas_call | solution.py:40
  64.3 1.5 %shard_map.95 = (bf16[2,360,128]{2,1,0:T(8,128)(2,1)S(1)}, bf16[2,360,128]{2,1,0:T(8,128)(2,1)S(1)}) custom-call(s32[4,16]{1,0:T(4,128)S(1)} %pad_add_fusion.refs_1_.refs_0_, bf16[1,2,360,128]{3,2,1,0:T(8,128)(2,1)S(1)} %get-tuple-element.33.refs_9_.refs_1_, bf16[3,2,360,128]{3,2,1,0:T(8,128)(2,1)S(1)} %get-tuple-element.35.refs_10_.refs_3_.refs_2_, ...), custom_call_target="tpu_custom_call" | custom-call | flops 1 | bytes 1 | tf_op jit(solution)/shard_map/pallas_call | solution.py:40
  66.4 7.9 %collective-permute-done.10.refs_6_ = bf16[2,360,128]{2,1,0:T(8,128)(2,1)S(1)} collective-permute-done((bf16[2,360,128]{2,1,0:T(8,128)(2,1)S(1)}, bf16[2,360,128]{2,1,0:T(8,128)(2,1)S(1)}, u32[]{:S(2)}, u32[]{:S(2)}) %collective-permute-start.10) | collective-permute-done | bytes 184352 | tf_op jit(solution)/shard_map/ppermute | solution.py:302
  74.3 1.6 %shard_map.97 = bf16[3,4,360,128]{3,2,1,0:T(8,128)(2,1)} custom-call(s32[1,4]{1,0:T(1,128)S(1)} %bitcast.17, bf16[2,2,360,128]{3,2,1,0:T(8,128)(2,1)S(1)} %get-tuple-element.36.refs_1_, bf16[2,360,128]{2,1,0:T(8,128)(2,1)S(1)} %get-tuple-element.40.refs_10_.refs_5_.refs_11_.refs_9_.refs_2_, ...), custom_call_target="tpu_custom_call" | custom-call | flops 1 | bytes 1 | tf_op jit(solution)/shard_map/pallas_call | solution.py:40
  (44 shorter events, 4.9 us)
Async XLA Ops:
  0.0 6.2 %copy-start = (f32[256,8,4]{0,2,1:T(4,128)S(1)}, f32[256,8,4]{0,2,1:T(4,128)}, u32[]{:S(2)}) copy-start(f32[256,8,4]{0,2,1:T(4,128)} %param.12) | copy-start | bytes 98308
  0.0 1.3 %copy-start.1 = (bf16[3,4,360,128]{3,2,1,0:T(8,128)(2,1)S(1)}, bf16[3,4,360,128]{3,2,1,0:T(8,128)(2,1)}, u32[]{:S(2)}) copy-start(bf16[3,4,360,128]{3,2,1,0:T(8,128)(2,1)} %refs_1_.7) | copy-start | bytes 3317764
  1.3 0.7 copy-start.3
  2.3 4.1 %copy-start.6 = (bf16[2,512,128]{2,1,0:T(8,128)(2,1)S(1)}, bf16[2,512,128]{2,1,0:T(8,128)(2,1)}, u32[]{:S(2)}) copy-start(bf16[2,512,128]{2,1,0:T(8,128)(2,1)} %param.14) | copy-start | bytes 786436
  2.3 21.1 %collective-permute-start = (bf16[3,2,360,128]{3,2,1,0:T(8,128)(2,1)S(1)}, bf16[3,2,360,128]{3,2,1,0:T(8,128)(2,1)S(1)}, u32[]{:S(2)}, u32[]{:S(2)}) collective-permute-start(bf16[3,2,360,128]{3,2,1,0:T(8,128)(2,1)S(1)} %shard_map.82.refs_2_.refs_1_), channel_id=1, source_target_pairs={{1,2},{3,4},{5,6},{7,8},{9,10},{11,12},{13,14},{15,16},{17,18},{19... | collective-permute-start | bytes 1658888 | tf_op jit(solution)/shard_map/ppermute | solution.py:289
  6.1 3.4 %collective-permute-start.1 = (bf16[3,2,360,128]{3,2,1,0:T(8,128)(2,1)S(1)}, bf16[3,2,360,128]{3,2,1,0:T(8,128)(2,1)S(1)}, u32[]{:S(2)}, u32[]{:S(2)}) collective-permute-start(bf16[3,2,360,128]{3,2,1,0:T(8,128)(2,1)S(1)} %shard_map.83.refs_2_.refs_3_), channel_id=1, source_target_pairs={{0,1},{2,3},{4,5},{6,7},{8,9},{10,11},{12,13},{14,15},{16,17},{18,... | collective-permute-start | bytes 1658888 | tf_op jit(solution)/shard_map/ppermute | solution.py:288
  6.4 1.8 %copy-start.7 = (s32[256,8]{0,1:T(8,128)S(1)}, s32[256,8]{0,1:T(8,128)}, u32[]{:S(2)}) copy-start(s32[256,8]{0,1:T(8,128)} %param.11) | copy-start | bytes 24580
  6.4 1.8 %copy-start.8 = (s32[256,8]{0,1:T(8,128)S(1)}, s32[256,8]{0,1:T(8,128)}, u32[]{:S(2)}) copy-start(s32[256,8]{0,1:T(8,128)} %param.10) | copy-start | bytes 24580
  6.4 3.1 %copy-start.5 = (s32[4]{0:T(128)S(1)}, s32[4]{0:T(128)}, u32[]{:S(2)}) copy-start(s32[4]{0:T(128)} %param.9) | copy-start | bytes 52
  9.5 12.3 %copy-start.2 = (bf16[3,4,360,128]{3,2,1,0:T(8,128)(2,1)S(1)}, bf16[3,4,360,128]{3,2,1,0:T(8,128)(2,1)}, u32[]{:S(2)}) copy-start(bf16[3,4,360,128]{3,2,1,0:T(8,128)(2,1)} %refs_1_.7) | copy-start | bytes 3317764
  9.5 12.3 %copy-start.4 = (f32[2,128]{1,0:T(2,128)S(1)}, f32[2,128]{1,0:T(2,128)}, u32[]{:S(2)}) copy-start(f32[2,128]{1,0:T(2,128)} %refs_9_.7) | copy-start | bytes 3076
  10.8 26.3 %collective-permute-start.4 = (bf16[2,360,128]{2,1,0:T(8,128)(2,1)S(1)}, bf16[2,360,128]{2,1,0:T(8,128)(2,1)S(1)}, u32[]{:S(2)}, u32[]{:S(2)}) collective-permute-start(bf16[2,360,128]{2,1,0:T(8,128)(2,1)S(1)} %get-tuple-element.27.refs_5_.refs_7_.refs_2_), channel_id=1, source_target_pairs={{0,64},{128,192},{64,0},{192,128},{65,129},{129,65},{2,66},{130,19... | collective-permute-start | bytes 552968 | tf_op jit(solution)/shard_map/ppermute | solution.py:302
  11.4 25.6 %collective-permute-start.5 = (bf16[2,360,128]{2,1,0:T(8,128)(2,1)S(1)}, bf16[2,360,128]{2,1,0:T(8,128)(2,1)S(1)}, u32[]{:S(2)}, u32[]{:S(2)}) collective-permute-start(bf16[2,360,128]{2,1,0:T(8,128)(2,1)S(1)} %get-tuple-element.28.refs_6_.refs_8_.refs_3_), channel_id=1, source_target_pairs={{64,128},{128,64},{1,65},{129,193},{65,1},{193,129},{66,130},{130,... | collective-permute-start | bytes 552968 | tf_op jit(solution)/shard_map/ppermute | solution.py:302
  24.7 13.3 %collective-permute-start.2 = (bf16[2,360,128]{2,1,0:T(8,128)(2,1)S(1)}, bf16[2,360,128]{2,1,0:T(8,128)(2,1)S(1)}, u32[]{:S(2)}, u32[]{:S(2)}) collective-permute-start(bf16[2,360,128]{2,1,0:T(8,128)(2,1)S(1)} %get-tuple-element.30.refs_5_.refs_3_.refs_2_), channel_id=1, source_target_pairs={{0,64},{128,192},{64,0},{192,128},{65,129},{129,65},{2,66},{130,19... | collective-permute-start | bytes 552968 | tf_op jit(solution)/shard_map/ppermute | solution.py:302
  25.4 12.7 %collective-permute-start.3 = (bf16[2,360,128]{2,1,0:T(8,128)(2,1)S(1)}, bf16[2,360,128]{2,1,0:T(8,128)(2,1)S(1)}, u32[]{:S(2)}, u32[]{:S(2)}) collective-permute-start(bf16[2,360,128]{2,1,0:T(8,128)(2,1)S(1)} %get-tuple-element.31.refs_6_.refs_4_.refs_3_), channel_id=1, source_target_pairs={{64,128},{128,64},{1,65},{129,193},{65,1},{193,129},{66,130},{130,... | collective-permute-start | bytes 552968 | tf_op jit(solution)/shard_map/ppermute | solution.py:302
  37.9 7.4 %collective-permute-start.7 = (bf16[3,2,360,128]{3,2,1,0:T(8,128)(2,1)S(1)}, bf16[3,2,360,128]{3,2,1,0:T(8,128)(2,1)S(1)}, u32[]{:S(2)}, u32[]{:S(2)}) collective-permute-start(bf16[3,2,360,128]{3,2,1,0:T(8,128)(2,1)S(1)} %get-tuple-element.35.refs_10_.refs_3_.refs_2_), channel_id=1, source_target_pairs={{0,1},{2,3},{4,5},{6,7},{8,9},{10,11},{12,13},{14,15},{16,17},{18,... | collective-permute-start | bytes 1658888 | tf_op jit(solution)/shard_map/ppermute | solution.py:345
  38.9 17.2 %collective-permute-start.6 = (bf16[2,2,360,128]{3,2,1,0:T(8,128)(2,1)S(1)}, bf16[2,2,360,128]{3,2,1,0:T(8,128)(2,1)S(1)}, u32[]{:S(2)}, u32[]{:S(2)}) collective-permute-start(bf16[2,2,360,128]{3,2,1,0:T(8,128)(2,1)S(1)} %get-tuple-element.37.refs_2_), channel_id=1, source_target_pairs={{1,2},{3,4},{5,6},{7,8},{9,10},{11,12},{13,14},{15,16},{17,18},{19... | collective-permute-start | bytes 1105928 | tf_op jit(solution)/shard_map/ppermute | solution.py:349
  42.3 22.0 %collective-permute-start.8 = (bf16[1,2,360,128]{3,2,1,0:T(8,128)(2,1)S(1)}, bf16[1,2,360,128]{3,2,1,0:T(8,128)(2,1)S(1)}, u32[]{:S(2)}, u32[]{:S(2)}) collective-permute-start(bf16[1,2,360,128]{3,2,1,0:T(8,128)(2,1)S(1)} %get-tuple-element.33.refs_9_.refs_1_), channel_id=1, source_target_pairs={{1,2},{3,4},{5,6},{7,8},{9,10},{11,12},{13,14},{15,16},{17,18},{19... | collective-permute-start | bytes 552968 | tf_op jit(solution)/shard_map/ppermute | solution.py:340
  46.5 19.3 %collective-permute-start.11 = (bf16[2,360,128]{2,1,0:T(8,128)(2,1)S(1)}, bf16[2,360,128]{2,1,0:T(8,128)(2,1)S(1)}, u32[]{:S(2)}, u32[]{:S(2)}) collective-permute-start(bf16[2,360,128]{2,1,0:T(8,128)(2,1)S(1)} %get-tuple-element.38.refs_6_.refs_5_.refs_2_), channel_id=1, source_target_pairs={{0,64},{128,192},{64,0},{192,128},{65,129},{129,65},{2,66},{130,19... | collective-permute-start | bytes 552968 | tf_op jit(solution)/shard_map/ppermute | solution.py:302
  47.2 18.6 %collective-permute-start.12 = (bf16[2,360,128]{2,1,0:T(8,128)(2,1)S(1)}, bf16[2,360,128]{2,1,0:T(8,128)(2,1)S(1)}, u32[]{:S(2)}, u32[]{:S(2)}) collective-permute-start(bf16[2,360,128]{2,1,0:T(8,128)(2,1)S(1)} %get-tuple-element.39.refs_7_.refs_6_.refs_3_), channel_id=1, source_target_pairs={{64,128},{128,64},{1,65},{129,193},{65,1},{193,129},{66,130},{130,... | collective-permute-start | bytes 552968 | tf_op jit(solution)/shard_map/ppermute | solution.py:302
  57.2 9.2 %collective-permute-start.9 = (bf16[2,360,128]{2,1,0:T(8,128)(2,1)S(1)}, bf16[2,360,128]{2,1,0:T(8,128)(2,1)S(1)}, u32[]{:S(2)}, u32[]{:S(2)}) collective-permute-start(bf16[2,360,128]{2,1,0:T(8,128)(2,1)S(1)} %get-tuple-element.40.refs_10_.refs_5_.refs_11_.refs_9_.refs_2_), channel_id=1, source_target_pairs={{0,64},{128,192},{64,0},{192,128},{65,129},{129,65},{2,66},{130,19... | collective-permute-start | bytes 552968 | tf_op jit(solution)/shard_map/ppermute | solution.py:302
  57.9 16.4 %collective-permute-start.10 = (bf16[2,360,128]{2,1,0:T(8,128)(2,1)S(1)}, bf16[2,360,128]{2,1,0:T(8,128)(2,1)S(1)}, u32[]{:S(2)}, u32[]{:S(2)}) collective-permute-start(bf16[2,360,128]{2,1,0:T(8,128)(2,1)S(1)} %get-tuple-element.41.refs_11_.refs_6_.refs_12_.refs_10_.refs_3_), channel_id=1, source_target_pairs={{64,128},{128,64},{1,65},{129,193},{65,1},{193,129},{66,130},{130,... | collective-permute-start | bytes 552968 | tf_op jit(solution)/shard_map/ppermute | solution.py:302

commit v6 on v5

--- a/solution.py
+++ b/solution.py
@@ -42,7 +42,8 @@
 
 def here():
     lat_odd = lax.axis_index("lat") % 2
-    return (lax.axis_index("lev") + lat_odd) % 2 == 1, lat_odd
+    lat = lax.axis_index("lat")
+    return (lax.axis_index("lev") + lat + lat // 2) % 2 == 1, lat_odd
 
 
 def own_levels(level_count):
@@ -255,7 +256,7 @@
     lats, levs = lax.axis_size("lat"), lax.axis_size("lev")
     near_pairs, far_pairs = pairs(lats, 0), pairs(lats, 1)
     one_pairs, two_pairs = [
-        [(a * lats + lat, b * lats + lat) for lat in range(lats) for a, b in pairs(levs, (lat + turn) % 2)] for turn in (0, 1)
+        [(a * lats + lat, b * lats + lat) for lat in range(lats) for a, b in pairs(levs, (lat + lat // 2 + turn) % 2)] for turn in (0, 1)
     ]
     plane = jax.ShapeDtypeStruct((H, lons, channels), BF16)
 

time: 77.2 us -> 77.2 us (level)
  waiting for transfers between devices: 7.95 us -> 12.7 us
  starting transfers between devices: 45 us -> 40.9 us
    ppermute x4, starting transfers between devices: 32.3 us -> 2.87 us  [ends(): lax.ppermute(two, ('lev', 'lat'), two_pairs)]
    ppermute x4, starting transfers between devices: 2.69 us -> 25.8 us  [ends(): lax.ppermute(one, ('lev', 'lat'), one_pairs)]
    ppermute x4, waiting for transfers between devices: 0.01 us -> 10.7 us  [ends(): lax.ppermute(one, ('lev', 'lat'), one_pairs)]
    ppermute x4, waiting for transfers between devices: 7.93 us -> 0.01 us  [ends(): lax.ppermute(two, ('lev', 'lat'), two_pairs)]
    ppermute x2, starting transfers between devices: 6.76 us -> 9.53 us  [on_device(): far_got = lax.ppermute(far, 'lat', far_pairs)]
    ppermute x2, waiting for transfers between devices: 0.01 us -> 2.06 us  [on_device(): far_got = lax.ppermute(far, 'lat', far_pairs)]
    ppermute x1, starting transfers between devices: 3.06 us -> 1.92 us  [on_device(): middle_far_got = lax.ppermute(middle_far, 'lat', far_pairs)]
  transfers between devices with their start and end apart: 13 -> 13, of which waited for: 2 -> 4; matrix products, arithmetic and copies ran while one was open for 2% -> 2% of each run, Pallas kernels for 23% -> 22%
where the time goes in v6:
time: 77.2 us; the launch traced here: 76.7 us
  starting transfers between devices  40.9 us (53%)
  Pallas kernels  19.2 us (25%)
  waiting for transfers between devices  12.7 us (16%)
  local copies, waits for them, and re-layouts  3.35 us (4%)
    ppermute x4, starting transfers between devices, ends(): lax.ppermute(one, ('lev', 'lat'), one_pairs)  25.8 us
    pallas_call x16, Pallas kernels, call(): return lambda *operands: made(*operands, *after)  19.2 us
    ppermute x4, waiting for transfers between devices, ends(): lax.ppermute(one, ('lev', 'lat'), one_pairs)  10.7 us
    ppermute x2, starting transfers between devices, on_device(): far_got = lax.ppermute(far, 'lat', far_pairs)  9.53 us
    ppermute x4, starting transfers between devices, ends(): lax.ppermute(two, ('lev', 'lat'), two_pairs)  2.87 us
    unnamed x20, local copies, waits for them, and re-layouts  2.13 us
    ppermute x2, waiting for transfers between devices, on_device(): far_got = lax.ppermute(far, 'lat', far_pairs)  2.06 us
    ppermute x1, starting transfers between devices, on_device(): middle_far_got = lax.ppermute(middle_far, 'lat', far_pairs)  1.92 us
  transfers between devices with their start and end apart: 13, of which 4 were waited for; matrix products, arithmetic and copies ran while one was open for 2% of the time, Pallas kernels for 22%

profile of v6, /device:TPU:49, one launch (start us, length us, event | category | flops | bytes accessed | tf_op | source)
XLA Modules:
  0.0 76.7 jit_solution(7730549489846257442)
XLA Ops:
  0.0 1.2 %copy-done.1 = bf16[3,4,360,128]{3,2,1,0:T(8,128)(2,1)S(1)} copy-done((bf16[3,4,360,128]{3,2,1,0:T(8,128)(2,1)S(1)}, bf16[3,4,360,128]{3,2,1,0:T(8,128)(2,1)}, u32[]{:S(2)}) %copy-start.1) | copy-done | bytes 1105944
  2.3 3.4 %collective-permute-start = (bf16[3,2,360,128]{3,2,1,0:T(8,128)(2,1)S(1)}, bf16[3,2,360,128]{3,2,1,0:T(8,128)(2,1)S(1)}, u32[]{:S(2)}, u32[]{:S(2)}) collective-permute-start(bf16[3,2,360,128]{3,2,1,0:T(8,128)(2,1)S(1)} %shard_map.82.refs_2_.refs_1_), channel_id=1, source_target_pairs={{1,2},{3,4},{5,6},{7,8},{9,10},{11,12},{13,14},{15,16},{17,18},{19... | collective-permute-start | bytes 1658888 | tf_op jit(solution)/shard_map/ppermute | solution.py:290
  6.4 1.7 %shard_map.84.refs_5_.refs_4_ = bf16[4,1024,128]{2,1,0:T(8,128)(2,1)S(1)} custom-call(f32[4,32]{1,0:T(4,128)S(1)} %copy.15.refs_0_, bf16[512,128]{1,0:T(8,128)(2,1)S(1)} %get-tuple-element.50.refs_1_, bf16[3,2,360,128]{3,2,1,0:T(8,128)(2,1)S(1)} %shard_map.83.refs_2_.refs_3_), custom_call_target="tpu_custom_call" | custom-call | flops 10000000000 | bytes 1 | tf_op jit(solution)/shard_map/pallas_call | solution.py:40
  8.5 1.0 %slice_bitcast_fusion.2 = (bf16[384,128]{1,0:T(8,128)(2,1)S(1)}, bf16[384,128]{1,0:T(8,128)(2,1)S(1)}) fusion(bf16[2,384,128]{2,1,0:T(8,128)(2,1)} %param.15), kind=kLoop, calls=%fused_computation.2 | loop fusion | bytes 393216 | tf_op jit(solution)/shard_map/squeeze | solution.py:314
  9.5 1.2 %shard_map.85 = (bf16[2,360,128]{2,1,0:T(8,128)(2,1)S(1)}, bf16[2,360,128]{2,1,0:T(8,128)(2,1)S(1)}) custom-call(s32[1,4]{1,0:T(1,128)S(1)} %bitcast.10, s32[4,16]{1,0:T(4,128)S(1)} %pad_add_fusion.refs_1_.refs_0_, bf16[3,2,360,128]{3,2,1,0:T(8,128)(2,1)S(1)} %shard_map.82.refs_2_.refs_1_, bf16[3,2,360,128]{3,2,1,0:T(8,128)(2,1)S(1)} %shard_map.83.refs_2_.refs_3_, ...), custom_call_target="tpu_custom_call" | custom-call | flops 1 | bytes 1 | tf_op jit(solution)/shard_map/pallas_call | solution.py:40
  10.8 4.9 %collective-permute-start.4 = (bf16[2,360,128]{2,1,0:T(8,128)(2,1)S(1)}, bf16[2,360,128]{2,1,0:T(8,128)(2,1)S(1)}, u32[]{:S(2)}, u32[]{:S(2)}) collective-permute-start(bf16[2,360,128]{2,1,0:T(8,128)(2,1)S(1)} %get-tuple-element.27.refs_5_.refs_7_.refs_2_), channel_id=1, source_target_pairs={{0,64},{128,192},{64,0},{192,128},{65,129},{129,65},{66,130},{130,... | collective-permute-start | bytes 552968 | tf_op jit(solution)/shard_map/ppermute | solution.py:303
  16.4 1.6 %shard_map.86 = (bf16[2,360,128]{2,1,0:T(8,128)(2,1)S(1)}, bf16[2,360,128]{2,1,0:T(8,128)(2,1)S(1)}, bf16[1,2,360,128]{3,2,1,0:T(8,128)(2,1)S(1)}) custom-call(s32[4,16]{1,0:T(4,128)S(1)} %pad_add_fusion.refs_1_.refs_0_, bf16[3,2,360,128]{3,2,1,0:T(8,128)(2,1)S(1)} %shard_map.82.refs_2_.refs_1_, bf16[3,2,360,128]{3,2,1,0:T(8,128)(2,1)S(1)} %shard_map.83.refs_2_.refs_3_, ...), custom_call_target="tpu_custom_call" | custom-call | flops 1 | bytes 1 | tf_op jit(solution)/shard_map/pallas_call | solution.py:40
  18.0 2.1 %collective-permute-done.refs_4_.refs_3_ = bf16[3,2,360,128]{3,2,1,0:T(8,128)(2,1)S(1)} collective-permute-done((bf16[3,2,360,128]{3,2,1,0:T(8,128)(2,1)S(1)}, bf16[3,2,360,128]{3,2,1,0:T(8,128)(2,1)S(1)}, u32[]{:S(2)}, u32[]{:S(2)}) %collective-permute-start) | collective-permute-done | bytes 552992 | tf_op jit(solution)/shard_map/ppermute | solution.py:290
  20.1 1.2 %shard_map.87 = (bf16[2,360,128]{2,1,0:T(8,128)(2,1)S(1)}, bf16[2,360,128]{2,1,0:T(8,128)(2,1)S(1)}) custom-call(s32[1,4]{1,0:T(1,128)S(1)} %bitcast.11, s32[4,16]{1,0:T(4,128)S(1)} %pad_add_fusion.refs_1_.refs_0_, bf16[3,2,360,128]{3,2,1,0:T(8,128)(2,1)S(1)} %shard_map.82.refs_2_.refs_1_, bf16[3,2,360,128]{3,2,1,0:T(8,128)(2,1)S(1)} %shard_map.83.refs_2_.refs_3_, ...), custom_call_target="tpu_custom_call" | custom-call | flops 1 | bytes 1 | tf_op jit(solution)/shard_map/pallas_call | solution.py:40
  21.3 7.2 %collective-permute-start.2 = (bf16[2,360,128]{2,1,0:T(8,128)(2,1)S(1)}, bf16[2,360,128]{2,1,0:T(8,128)(2,1)S(1)}, u32[]{:S(2)}, u32[]{:S(2)}) collective-permute-start(bf16[2,360,128]{2,1,0:T(8,128)(2,1)S(1)} %get-tuple-element.30.refs_5_.refs_3_.refs_2_), channel_id=1, source_target_pairs={{0,64},{128,192},{64,0},{192,128},{65,129},{129,65},{66,130},{130,... | collective-permute-start | bytes 552968 | tf_op jit(solution)/shard_map/ppermute | solution.py:303
  29.2 1.6 %shard_map.88 = (bf16[2,360,128]{2,1,0:T(8,128)(2,1)S(1)}, bf16[2,360,128]{2,1,0:T(8,128)(2,1)S(1)}, bf16[1,2,360,128]{3,2,1,0:T(8,128)(2,1)S(1)}) custom-call(s32[4,16]{1,0:T(4,128)S(1)} %pad_add_fusion.refs_1_.refs_0_, bf16[3,2,360,128]{3,2,1,0:T(8,128)(2,1)S(1)} %shard_map.82.refs_2_.refs_1_, bf16[3,2,360,128]{3,2,1,0:T(8,128)(2,1)S(1)} %shard_map.83.refs_2_.refs_3_, ...), custom_call_target="tpu_custom_call" | custom-call | flops 1 | bytes 1 | tf_op jit(solution)/shard_map/pallas_call | solution.py:40
  30.8 1.7 %shard_map.89.refs_10_.refs_5_.refs_4_ = bf16[4,1024,128]{2,1,0:T(8,128)(2,1)S(1)} custom-call(f32[4,32]{1,0:T(4,128)S(1)} %copy.15.refs_0_, bf16[512,128]{1,0:T(8,128)(2,1)S(1)} %get-tuple-element.49.refs_1_, bf16[2,360,128]{2,1,0:T(8,128)(2,1)S(1)} %get-tuple-element.32.refs_2_.refs_4_, bf16[2,360,128]{2,1,0:T(8,128)(2,1)S(1)} %get-tuple-element.30.refs_5_.refs_3_.refs_2_, ...), custom_call_target="tpu_custom_call" | custom-call | flops 1 | bytes 1 | tf_op jit(solution)/shard_map/pallas_call | solution.py:40
  34.1 1.2 %collective-permute-done.2.refs_5_ = bf16[2,360,128]{2,1,0:T(8,128)(2,1)S(1)} collective-permute-done((bf16[2,360,128]{2,1,0:T(8,128)(2,1)S(1)}, bf16[2,360,128]{2,1,0:T(8,128)(2,1)S(1)}, u32[]{:S(2)}, u32[]{:S(2)}) %collective-permute-start.2) | collective-permute-done | bytes 184352 | tf_op jit(solution)/shard_map/ppermute | solution.py:303
  36.1 6.2 %collective-permute-start.6 = (bf16[2,2,360,128]{3,2,1,0:T(8,128)(2,1)S(1)}, bf16[2,2,360,128]{3,2,1,0:T(8,128)(2,1)S(1)}, u32[]{:S(2)}, u32[]{:S(2)}) collective-permute-start(bf16[2,2,360,128]{3,2,1,0:T(8,128)(2,1)S(1)} %get-tuple-element.37.refs_2_), channel_id=1, source_target_pairs={{1,2},{3,4},{5,6},{7,8},{9,10},{11,12},{13,14},{15,16},{17,18},{19... | collective-permute-start | bytes 1105928 | tf_op jit(solution)/shard_map/ppermute | solution.py:350
  42.2 1.9 %collective-permute-start.8 = (bf16[1,2,360,128]{3,2,1,0:T(8,128)(2,1)S(1)}, bf16[1,2,360,128]{3,2,1,0:T(8,128)(2,1)S(1)}, u32[]{:S(2)}, u32[]{:S(2)}) collective-permute-start(bf16[1,2,360,128]{3,2,1,0:T(8,128)(2,1)S(1)} %get-tuple-element.33.refs_9_.refs_1_), channel_id=1, source_target_pairs={{1,2},{3,4},{5,6},{7,8},{9,10},{11,12},{13,14},{15,16},{17,18},{19... | collective-permute-start | bytes 552968 | tf_op jit(solution)/shard_map/ppermute | solution.py:341
  44.2 1.2 %shard_map.92 = (bf16[2,360,128]{2,1,0:T(8,128)(2,1)S(1)}, bf16[2,360,128]{2,1,0:T(8,128)(2,1)S(1)}) custom-call(s32[1,4]{1,0:T(1,128)S(1)} %bitcast.14, s32[4,16]{1,0:T(4,128)S(1)} %pad_add_fusion.refs_1_.refs_0_, bf16[2,2,360,128]{3,2,1,0:T(8,128)(2,1)S(1)} %get-tuple-element.37.refs_2_, ...), custom_call_target="tpu_custom_call" | custom-call | flops 1 | bytes 1 | tf_op jit(solution)/shard_map/pallas_call | solution.py:40
  45.4 8.3 %collective-permute-start.11 = (bf16[2,360,128]{2,1,0:T(8,128)(2,1)S(1)}, bf16[2,360,128]{2,1,0:T(8,128)(2,1)S(1)}, u32[]{:S(2)}, u32[]{:S(2)}) collective-permute-start(bf16[2,360,128]{2,1,0:T(8,128)(2,1)S(1)} %get-tuple-element.38.refs_6_.refs_5_.refs_2_), channel_id=1, source_target_pairs={{0,64},{128,192},{64,0},{192,128},{65,129},{129,65},{66,130},{130,... | collective-permute-start | bytes 552968 | tf_op jit(solution)/shard_map/ppermute | solution.py:303
  54.4 1.2 %shard_map.93 = (bf16[2,360,128]{2,1,0:T(8,128)(2,1)S(1)}, bf16[2,360,128]{2,1,0:T(8,128)(2,1)S(1)}) custom-call(s32[1,4]{1,0:T(1,128)S(1)} %bitcast.15, s32[4,16]{1,0:T(4,128)S(1)} %pad_add_fusion.refs_1_.refs_0_, bf16[2,2,360,128]{3,2,1,0:T(8,128)(2,1)S(1)} %get-tuple-element.37.refs_2_, ...), custom_call_target="tpu_custom_call" | custom-call | flops 1 | bytes 1 | tf_op jit(solution)/shard_map/pallas_call | solution.py:40
  55.6 5.4 %collective-permute-start.9 = (bf16[2,360,128]{2,1,0:T(8,128)(2,1)S(1)}, bf16[2,360,128]{2,1,0:T(8,128)(2,1)S(1)}, u32[]{:S(2)}, u32[]{:S(2)}) collective-permute-start(bf16[2,360,128]{2,1,0:T(8,128)(2,1)S(1)} %get-tuple-element.40.refs_10_.refs_5_.refs_11_.refs_9_.refs_2_), channel_id=1, source_target_pairs={{0,64},{128,192},{64,0},{192,128},{65,129},{129,65},{66,130},{130,... | collective-permute-start | bytes 552968 | tf_op jit(solution)/shard_map/ppermute | solution.py:303
  61.8 1.5 %shard_map.94 = (bf16[2,360,128]{2,1,0:T(8,128)(2,1)S(1)}, bf16[2,360,128]{2,1,0:T(8,128)(2,1)S(1)}) custom-call(s32[4,16]{1,0:T(4,128)S(1)} %pad_add_fusion.refs_1_.refs_0_, bf16[1,2,360,128]{3,2,1,0:T(8,128)(2,1)S(1)} %get-tuple-element.33.refs_9_.refs_1_, bf16[3,2,360,128]{3,2,1,0:T(8,128)(2,1)S(1)} %get-tuple-element.35.refs_10_.refs_3_.refs_2_, ...), custom_call_target="tpu_custom_call" | custom-call | flops 1 | bytes 1 | tf_op jit(solution)/shard_map/pallas_call | solution.py:40
  63.4 1.5 %shard_map.95 = (bf16[2,360,128]{2,1,0:T(8,128)(2,1)S(1)}, bf16[2,360,128]{2,1,0:T(8,128)(2,1)S(1)}) custom-call(s32[4,16]{1,0:T(4,128)S(1)} %pad_add_fusion.refs_1_.refs_0_, bf16[1,2,360,128]{3,2,1,0:T(8,128)(2,1)S(1)} %get-tuple-element.33.refs_9_.refs_1_, bf16[3,2,360,128]{3,2,1,0:T(8,128)(2,1)S(1)} %get-tuple-element.35.refs_10_.refs_3_.refs_2_, ...), custom_call_target="tpu_custom_call" | custom-call | flops 1 | bytes 1 | tf_op jit(solution)/shard_map/pallas_call | solution.py:40
  64.9 2.1 %collective-permute-done.11.refs_5_ = bf16[2,360,128]{2,1,0:T(8,128)(2,1)S(1)} collective-permute-done((bf16[2,360,128]{2,1,0:T(8,128)(2,1)S(1)}, bf16[2,360,128]{2,1,0:T(8,128)(2,1)S(1)}, u32[]{:S(2)}, u32[]{:S(2)}) %collective-permute-start.11) | collective-permute-done | bytes 184352 | tf_op jit(solution)/shard_map/ppermute | solution.py:303
  67.6 7.3 %collective-permute-done.9.refs_5_ = bf16[2,360,128]{2,1,0:T(8,128)(2,1)S(1)} collective-permute-done((bf16[2,360,128]{2,1,0:T(8,128)(2,1)S(1)}, bf16[2,360,128]{2,1,0:T(8,128)(2,1)S(1)}, u32[]{:S(2)}, u32[]{:S(2)}) %collective-permute-start.9) | collective-permute-done | bytes 184352 | tf_op jit(solution)/shard_map/ppermute | solution.py:303
  74.9 1.6 %shard_map.97 = bf16[3,4,360,128]{3,2,1,0:T(8,128)(2,1)} custom-call(s32[1,4]{1,0:T(1,128)S(1)} %bitcast.17, bf16[2,2,360,128]{3,2,1,0:T(8,128)(2,1)S(1)} %get-tuple-element.36.refs_1_, bf16[2,360,128]{2,1,0:T(8,128)(2,1)S(1)} %get-tuple-element.40.refs_10_.refs_5_.refs_11_.refs_9_.refs_2_, ...), custom_call_target="tpu_custom_call" | custom-call | flops 1 | bytes 1 | tf_op jit(solution)/shard_map/pallas_call | solution.py:40
  (44 shorter events, 7.8 us)
Async XLA Ops:
  0.0 6.2 %copy-start = (f32[256,8,4]{0,2,1:T(4,128)S(1)}, f32[256,8,4]{0,2,1:T(4,128)}, u32[]{:S(2)}) copy-start(f32[256,8,4]{0,2,1:T(4,128)} %param.12) | copy-start | bytes 98308
  0.0 1.3 %copy-start.1 = (bf16[3,4,360,128]{3,2,1,0:T(8,128)(2,1)S(1)}, bf16[3,4,360,128]{3,2,1,0:T(8,128)(2,1)}, u32[]{:S(2)}) copy-start(bf16[3,4,360,128]{3,2,1,0:T(8,128)(2,1)} %refs_1_.7) | copy-start | bytes 3317764
  1.3 0.7 copy-start.3
  2.3 4.1 %copy-start.6 = (bf16[2,512,128]{2,1,0:T(8,128)(2,1)S(1)}, bf16[2,512,128]{2,1,0:T(8,128)(2,1)}, u32[]{:S(2)}) copy-start(bf16[2,512,128]{2,1,0:T(8,128)(2,1)} %param.14) | copy-start | bytes 786436
  2.3 17.7 %collective-permute-start = (bf16[3,2,360,128]{3,2,1,0:T(8,128)(2,1)S(1)}, bf16[3,2,360,128]{3,2,1,0:T(8,128)(2,1)S(1)}, u32[]{:S(2)}, u32[]{:S(2)}) collective-permute-start(bf16[3,2,360,128]{3,2,1,0:T(8,128)(2,1)S(1)} %shard_map.82.refs_2_.refs_1_), channel_id=1, source_target_pairs={{1,2},{3,4},{5,6},{7,8},{9,10},{11,12},{13,14},{15,16},{17,18},{19... | collective-permute-start | bytes 1658888 | tf_op jit(solution)/shard_map/ppermute | solution.py:290
  6.1 3.4 %collective-permute-start.1 = (bf16[3,2,360,128]{3,2,1,0:T(8,128)(2,1)S(1)}, bf16[3,2,360,128]{3,2,1,0:T(8,128)(2,1)S(1)}, u32[]{:S(2)}, u32[]{:S(2)}) collective-permute-start(bf16[3,2,360,128]{3,2,1,0:T(8,128)(2,1)S(1)} %shard_map.83.refs_2_.refs_3_), channel_id=1, source_target_pairs={{0,1},{2,3},{4,5},{6,7},{8,9},{10,11},{12,13},{14,15},{16,17},{18,... | collective-permute-start | bytes 1658888 | tf_op jit(solution)/shard_map/ppermute | solution.py:289
  6.4 1.8 %copy-start.7 = (s32[256,8]{0,1:T(8,128)S(1)}, s32[256,8]{0,1:T(8,128)}, u32[]{:S(2)}) copy-start(s32[256,8]{0,1:T(8,128)} %param.11) | copy-start | bytes 24580
  6.4 1.8 %copy-start.8 = (s32[256,8]{0,1:T(8,128)S(1)}, s32[256,8]{0,1:T(8,128)}, u32[]{:S(2)}) copy-start(s32[256,8]{0,1:T(8,128)} %param.10) | copy-start | bytes 24580
  6.4 3.1 %copy-start.5 = (s32[4]{0:T(128)S(1)}, s32[4]{0:T(128)}, u32[]{:S(2)}) copy-start(s32[4]{0:T(128)} %param.9) | copy-start | bytes 52
  9.5 6.9 %copy-start.2 = (bf16[3,4,360,128]{3,2,1,0:T(8,128)(2,1)S(1)}, bf16[3,4,360,128]{3,2,1,0:T(8,128)(2,1)}, u32[]{:S(2)}) copy-start(bf16[3,4,360,128]{3,2,1,0:T(8,128)(2,1)} %refs_1_.7) | copy-start | bytes 3317764
  9.5 6.9 %copy-start.4 = (f32[2,128]{1,0:T(2,128)S(1)}, f32[2,128]{1,0:T(2,128)}, u32[]{:S(2)}) copy-start(f32[2,128]{1,0:T(2,128)} %refs_9_.7) | copy-start | bytes 3076
  10.8 21.8 %collective-permute-start.4 = (bf16[2,360,128]{2,1,0:T(8,128)(2,1)S(1)}, bf16[2,360,128]{2,1,0:T(8,128)(2,1)S(1)}, u32[]{:S(2)}, u32[]{:S(2)}) collective-permute-start(bf16[2,360,128]{2,1,0:T(8,128)(2,1)S(1)} %get-tuple-element.27.refs_5_.refs_7_.refs_2_), channel_id=1, source_target_pairs={{0,64},{128,192},{64,0},{192,128},{65,129},{129,65},{66,130},{130,... | collective-permute-start | bytes 552968 | tf_op jit(solution)/shard_map/ppermute | solution.py:303
  15.7 16.9 %collective-permute-start.5 = (bf16[2,360,128]{2,1,0:T(8,128)(2,1)S(1)}, bf16[2,360,128]{2,1,0:T(8,128)(2,1)S(1)}, u32[]{:S(2)}, u32[]{:S(2)}) collective-permute-start(bf16[2,360,128]{2,1,0:T(8,128)(2,1)S(1)} %get-tuple-element.28.refs_6_.refs_8_.refs_3_), channel_id=1, source_target_pairs={{64,128},{128,64},{1,65},{129,193},{65,1},{193,129},{2,66},{130,19... | collective-permute-start | bytes 552968 | tf_op jit(solution)/shard_map/ppermute | solution.py:303
  21.3 14.0 %collective-permute-start.2 = (bf16[2,360,128]{2,1,0:T(8,128)(2,1)S(1)}, bf16[2,360,128]{2,1,0:T(8,128)(2,1)S(1)}, u32[]{:S(2)}, u32[]{:S(2)}) collective-permute-start(bf16[2,360,128]{2,1,0:T(8,128)(2,1)S(1)} %get-tuple-element.30.refs_5_.refs_3_.refs_2_), channel_id=1, source_target_pairs={{0,64},{128,192},{64,0},{192,128},{65,129},{129,65},{66,130},{130,... | collective-permute-start | bytes 552968 | tf_op jit(solution)/shard_map/ppermute | solution.py:303
  28.5 6.8 %collective-permute-start.3 = (bf16[2,360,128]{2,1,0:T(8,128)(2,1)S(1)}, bf16[2,360,128]{2,1,0:T(8,128)(2,1)S(1)}, u32[]{:S(2)}, u32[]{:S(2)}) collective-permute-start(bf16[2,360,128]{2,1,0:T(8,128)(2,1)S(1)} %get-tuple-element.31.refs_6_.refs_4_.refs_3_), channel_id=1, source_target_pairs={{64,128},{128,64},{1,65},{129,193},{65,1},{193,129},{2,66},{130,19... | collective-permute-start | bytes 552968 | tf_op jit(solution)/shard_map/ppermute | solution.py:303
  33.4 10.8 %collective-permute-start.7 = (bf16[3,2,360,128]{3,2,1,0:T(8,128)(2,1)S(1)}, bf16[3,2,360,128]{3,2,1,0:T(8,128)(2,1)S(1)}, u32[]{:S(2)}, u32[]{:S(2)}) collective-permute-start(bf16[3,2,360,128]{3,2,1,0:T(8,128)(2,1)S(1)} %get-tuple-element.35.refs_10_.refs_3_.refs_2_), channel_id=1, source_target_pairs={{0,1},{2,3},{4,5},{6,7},{8,9},{10,11},{12,13},{14,15},{16,17},{18,... | collective-permute-start | bytes 1658888 | tf_op jit(solution)/shard_map/ppermute | solution.py:346
  36.1 18.3 %collective-permute-start.6 = (bf16[2,2,360,128]{3,2,1,0:T(8,128)(2,1)S(1)}, bf16[2,2,360,128]{3,2,1,0:T(8,128)(2,1)S(1)}, u32[]{:S(2)}, u32[]{:S(2)}) collective-permute-start(bf16[2,2,360,128]{3,2,1,0:T(8,128)(2,1)S(1)} %get-tuple-element.37.refs_2_), channel_id=1, source_target_pairs={{1,2},{3,4},{5,6},{7,8},{9,10},{11,12},{13,14},{15,16},{17,18},{19... | collective-permute-start | bytes 1105928 | tf_op jit(solution)/shard_map/ppermute | solution.py:350
  42.2 21.1 %collective-permute-start.8 = (bf16[1,2,360,128]{3,2,1,0:T(8,128)(2,1)S(1)}, bf16[1,2,360,128]{3,2,1,0:T(8,128)(2,1)S(1)}, u32[]{:S(2)}, u32[]{:S(2)}) collective-permute-start(bf16[1,2,360,128]{3,2,1,0:T(8,128)(2,1)S(1)} %get-tuple-element.33.refs_9_.refs_1_), channel_id=1, source_target_pairs={{1,2},{3,4},{5,6},{7,8},{9,10},{11,12},{13,14},{15,16},{17,18},{19... | collective-permute-start | bytes 552968 | tf_op jit(solution)/shard_map/ppermute | solution.py:341
  45.4 21.6 %collective-permute-start.11 = (bf16[2,360,128]{2,1,0:T(8,128)(2,1)S(1)}, bf16[2,360,128]{2,1,0:T(8,128)(2,1)S(1)}, u32[]{:S(2)}, u32[]{:S(2)}) collective-permute-start(bf16[2,360,128]{2,1,0:T(8,128)(2,1)S(1)} %get-tuple-element.38.refs_6_.refs_5_.refs_2_), channel_id=1, source_target_pairs={{0,64},{128,192},{64,0},{192,128},{65,129},{129,65},{66,130},{130,... | collective-permute-start | bytes 552968 | tf_op jit(solution)/shard_map/ppermute | solution.py:303
  53.7 13.3 %collective-permute-start.12 = (bf16[2,360,128]{2,1,0:T(8,128)(2,1)S(1)}, bf16[2,360,128]{2,1,0:T(8,128)(2,1)S(1)}, u32[]{:S(2)}, u32[]{:S(2)}) collective-permute-start(bf16[2,360,128]{2,1,0:T(8,128)(2,1)S(1)} %get-tuple-element.39.refs_7_.refs_6_.refs_3_), channel_id=1, source_target_pairs={{64,128},{128,64},{1,65},{129,193},{65,1},{193,129},{2,66},{130,19... | collective-permute-start | bytes 552968 | tf_op jit(solution)/shard_map/ppermute | solution.py:303
  55.6 19.4 %collective-permute-start.9 = (bf16[2,360,128]{2,1,0:T(8,128)(2,1)S(1)}, bf16[2,360,128]{2,1,0:T(8,128)(2,1)S(1)}, u32[]{:S(2)}, u32[]{:S(2)}) collective-permute-start(bf16[2,360,128]{2,1,0:T(8,128)(2,1)S(1)} %get-tuple-element.40.refs_10_.refs_5_.refs_11_.refs_9_.refs_2_), channel_id=1, source_target_pairs={{0,64},{128,192},{64,0},{192,128},{65,129},{129,65},{66,130},{130,... | collective-permute-start | bytes 552968 | tf_op jit(solution)/shard_map/ppermute | solution.py:303
  61.0 14.0 %collective-permute-start.10 = (bf16[2,360,128]{2,1,0:T(8,128)(2,1)S(1)}, bf16[2,360,128]{2,1,0:T(8,128)(2,1)S(1)}, u32[]{:S(2)}, u32[]{:S(2)}) collective-permute-start(bf16[2,360,128]{2,1,0:T(8,128)(2,1)S(1)} %get-tuple-element.41.refs_11_.refs_6_.refs_12_.refs_10_.refs_3_), channel_id=1, source_target_pairs={{64,128},{128,64},{1,65},{129,193},{65,1},{193,129},{2,66},{130,19... | collective-permute-start | bytes 552968 | tf_op jit(solution)/shard_map/ppermute | solution.py:303

commit v7 on v6

--- a/solution.py
+++ b/solution.py
@@ -201,20 +201,25 @@
     lax.fori_loop(0, H, each, 0, unroll=True)
 
 
-def last_kernel(level_count, current, one, two, middle, got_one, got_two, weight, out):
+def put(rows, row, own, one_low, a, b, m):
+    bottom, top = jnp.where(one_low, a, b), jnp.where(one_low, b, a)
+    zero = jnp.zeros_like(m)
+    rows[0, row] = bottom
+    rows[1, row] = choose(own == 3, m, choose(own == 2, top, zero))
+    rows[2, row] = choose(own == 3, top, zero)
+
+
+def last_kernel(level_count, current, one, two, middle, got_one, got_two, weight, new_middle, out):
     own = own_levels(level_count)
     one_low, _ = here()
-
-    def each(h, carry):
-        for plane, value in enumerate(ends_mixed(h, own, one_low, one, two, middle, got_one, got_two, weight)):
-            out[plane, h] = (current[plane, h].astype(F32) + value).astype(BF16)
-        return carry
-
-    lax.fori_loop(0, H, each, 0, unroll=True)
+    for h in range(H):
+        values = ends_mixed(h, own, one_low, one, two, middle, got_one, got_two, weight)
+        a, b = [(current[plane, h].astype(F32) + value).astype(BF16) for plane, value in enumerate(values)]
+        put(out, h, own, one_low, a, b, new_middle[h])
 
 
 def final_kernel(
-    level_count, current, one, two, middle, got_one, got_two, weight, new_middle, near_ends, near_middle, out, rows, sems
+    level_count, current, one, two, middle, got_one, got_two, weight, new_middle, near_rows, out, rows, sems
 ):
     own = own_levels(level_count)
     one_low, lat_odd = here()
@@ -222,26 +227,18 @@
 
     copies = []
 
-    def send(row, part):
+    def send(source, row, part):
         for slot in range(out.shape[0]):
-            copies.append(pltpu.make_async_copy(rows.at[slot, row], out.at[slot, row], sems.at[part, slot]))
+            copies.append(pltpu.make_async_copy(source.at[slot], out.at[slot, row], sems.at[part, slot]))
             copies[-1].start()
 
-    def put(row, a, b, m):
-        bottom, top = jnp.where(one_low, a, b), jnp.where(one_low, b, a)
-        zero = jnp.zeros_like(m)
-        rows[0, row] = bottom
-        rows[1, row] = choose(own == 3, m, choose(own == 2, top, zero))
-        rows[2, row] = choose(own == 3, top, zero)
-
     for h in range(H):
-        put(near + h, near_ends[0, h], near_ends[1, h], near_middle[h])
-        send(near + h, h)
+        send(near_rows.at[:, h], near + h, h)
     for h in range(H):
         values = ends_mixed(h, own, one_low, one, two, middle, got_one, got_two, weight)
         a, b = [(current[plane, h].astype(F32) + value).astype(BF16) for plane, value in enumerate(values)]
-        put(far + h, a, b, new_middle[h])
-        send(far + h, H + h)
+        put(rows, h, own, one_low, a, b, new_middle[h])
+        send(rows.at[:, h], far + h, H + h)
     for copy in copies:
         copy.wait()
 
@@ -329,14 +326,14 @@
         far_ends = (far_one, far_two, far_made[0], *far_all_got, vert_weight[p])
         near_made, far_made = near_made[1:], far_made[1:]
         if last:
-            near_rows = call(last_kernel, edge(2), [VMEM] * 8, after=after)(counts, ends_now[0], *near_ends)
+            near_rows = call(last_kernel, edge(slots), [VMEM] * 9, after=after)(counts, ends_now[0], *near_ends, near_made[0])
             return call(
                 final_kernel,
                 jax.ShapeDtypeStruct(field.shape, BF16),
-                [VMEM] * 11,
-                [pltpu.VMEM(field.shape, BF16), pltpu.SemaphoreType.DMA((2 * H, slots))],
+                [VMEM] * 10,
+                [pltpu.VMEM((slots, H, lons, channels), BF16), pltpu.SemaphoreType.DMA((2 * H, slots))],
                 out_specs=hbm,
-            )(counts, ends_now[1], *far_ends, far_made[0], near_rows, near_made[0])
+            )(counts, ends_now[1], *far_ends, far_made[0], near_rows)
         middle_far = far_made[1]
         middle_far_got = lax.ppermute(middle_far, "lat", far_pairs)
         maps = maps_of(p + 1, after)

time: 77.2 us -> 77.1 us (level)
  no operation moved by 1% of the time
where the time goes in v7:
time: 77.1 us; the launch traced here: 76.6 us
  starting transfers between devices  40.9 us (53%)
  Pallas kernels  19.1 us (25%)
  waiting for transfers between devices  12.6 us (16%)
  local copies, waits for them, and re-layouts  3.35 us (4%)
    ppermute x4, starting transfers between devices, ends(): lax.ppermute(one, ('lev', 'lat'), one_pairs)  25.7 us
    pallas_call x16, Pallas kernels, call(): return lambda *operands: made(*operands, *after)  19.1 us
    ppermute x4, waiting for transfers between devices, ends(): lax.ppermute(one, ('lev', 'lat'), one_pairs)  10.5 us
    ppermute x2, starting transfers between devices, on_device(): far_got = lax.ppermute(far, 'lat', far_pairs)  9.57 us
    ppermute x4, starting transfers between devices, ends(): lax.ppermute(two, ('lev', 'lat'), two_pairs)  2.87 us
    unnamed x20, local copies, waits for them, and re-layouts  2.13 us
    ppermute x2, waiting for transfers between devices, on_device(): far_got = lax.ppermute(far, 'lat', far_pairs)  2.08 us
    ppermute x1, starting transfers between devices, on_device(): middle_far_got = lax.ppermute(middle_far, 'lat', far_pairs)  1.92 us
  transfers between devices with their start and end apart: 13, of which 4 were waited for; matrix products, arithmetic and copies ran while one was open for 2% of the time, Pallas kernels for 22%

profile of v7, /device:TPU:49, one launch (start us, length us, event | category | flops | bytes accessed | tf_op | source)
XLA Modules:
  0.0 76.6 jit_solution(10909710965053273296)
XLA Ops:
  0.0 1.2 %copy-done.1 = bf16[3,4,360,128]{3,2,1,0:T(8,128)(2,1)S(1)} copy-done((bf16[3,4,360,128]{3,2,1,0:T(8,128)(2,1)S(1)}, bf16[3,4,360,128]{3,2,1,0:T(8,128)(2,1)}, u32[]{:S(2)}) %copy-start.1) | copy-done | bytes 1105944
  2.3 3.4 %collective-permute-start = (bf16[3,2,360,128]{3,2,1,0:T(8,128)(2,1)S(1)}, bf16[3,2,360,128]{3,2,1,0:T(8,128)(2,1)S(1)}, u32[]{:S(2)}, u32[]{:S(2)}) collective-permute-start(bf16[3,2,360,128]{3,2,1,0:T(8,128)(2,1)S(1)} %shard_map.82.refs_2_.refs_1_), channel_id=1, source_target_pairs={{1,2},{3,4},{5,6},{7,8},{9,10},{11,12},{13,14},{15,16},{17,18},{19... | collective-permute-start | bytes 1658888 | tf_op jit(solution)/shard_map/ppermute | solution.py:287
  6.4 1.7 %shard_map.84.refs_5_.refs_4_ = bf16[4,1024,128]{2,1,0:T(8,128)(2,1)S(1)} custom-call(f32[4,32]{1,0:T(4,128)S(1)} %copy.15.refs_0_, bf16[512,128]{1,0:T(8,128)(2,1)S(1)} %get-tuple-element.50.refs_1_, bf16[3,2,360,128]{3,2,1,0:T(8,128)(2,1)S(1)} %shard_map.83.refs_2_.refs_3_), custom_call_target="tpu_custom_call" | custom-call | flops 10000000000 | bytes 1 | tf_op jit(solution)/shard_map/pallas_call | solution.py:40
  8.5 1.0 %slice_bitcast_fusion.2 = (bf16[384,128]{1,0:T(8,128)(2,1)S(1)}, bf16[384,128]{1,0:T(8,128)(2,1)S(1)}) fusion(bf16[2,384,128]{2,1,0:T(8,128)(2,1)} %param.15), kind=kLoop, calls=%fused_computation.2 | loop fusion | bytes 393216 | tf_op jit(solution)/shard_map/squeeze | solution.py:311
  9.5 1.2 %shard_map.85 = (bf16[2,360,128]{2,1,0:T(8,128)(2,1)S(1)}, bf16[2,360,128]{2,1,0:T(8,128)(2,1)S(1)}) custom-call(s32[1,4]{1,0:T(1,128)S(1)} %bitcast.10, s32[4,16]{1,0:T(4,128)S(1)} %pad_add_fusion.refs_1_.refs_0_, bf16[3,2,360,128]{3,2,1,0:T(8,128)(2,1)S(1)} %shard_map.82.refs_2_.refs_1_, bf16[3,2,360,128]{3,2,1,0:T(8,128)(2,1)S(1)} %shard_map.83.refs_2_.refs_3_, ...), custom_call_target="tpu_custom_call" | custom-call | flops 1 | bytes 1 | tf_op jit(solution)/shard_map/pallas_call | solution.py:40
  10.8 4.9 %collective-permute-start.4 = (bf16[2,360,128]{2,1,0:T(8,128)(2,1)S(1)}, bf16[2,360,128]{2,1,0:T(8,128)(2,1)S(1)}, u32[]{:S(2)}, u32[]{:S(2)}) collective-permute-start(bf16[2,360,128]{2,1,0:T(8,128)(2,1)S(1)} %get-tuple-element.27.refs_5_.refs_7_.refs_2_), channel_id=1, source_target_pairs={{0,64},{128,192},{64,0},{192,128},{65,129},{129,65},{66,130},{130,... | collective-permute-start | bytes 552968 | tf_op jit(solution)/shard_map/ppermute | solution.py:300
  16.4 1.6 %shard_map.86 = (bf16[2,360,128]{2,1,0:T(8,128)(2,1)S(1)}, bf16[2,360,128]{2,1,0:T(8,128)(2,1)S(1)}, bf16[1,2,360,128]{3,2,1,0:T(8,128)(2,1)S(1)}) custom-call(s32[4,16]{1,0:T(4,128)S(1)} %pad_add_fusion.refs_1_.refs_0_, bf16[3,2,360,128]{3,2,1,0:T(8,128)(2,1)S(1)} %shard_map.82.refs_2_.refs_1_, bf16[3,2,360,128]{3,2,1,0:T(8,128)(2,1)S(1)} %shard_map.83.refs_2_.refs_3_, ...), custom_call_target="tpu_custom_call" | custom-call | flops 1 | bytes 1 | tf_op jit(solution)/shard_map/pallas_call | solution.py:40
  18.0 2.1 %collective-permute-done.refs_4_.refs_3_ = bf16[3,2,360,128]{3,2,1,0:T(8,128)(2,1)S(1)} collective-permute-done((bf16[3,2,360,128]{3,2,1,0:T(8,128)(2,1)S(1)}, bf16[3,2,360,128]{3,2,1,0:T(8,128)(2,1)S(1)}, u32[]{:S(2)}, u32[]{:S(2)}) %collective-permute-start) | collective-permute-done | bytes 552992 | tf_op jit(solution)/shard_map/ppermute | solution.py:287
  20.1 1.2 %shard_map.87 = (bf16[2,360,128]{2,1,0:T(8,128)(2,1)S(1)}, bf16[2,360,128]{2,1,0:T(8,128)(2,1)S(1)}) custom-call(s32[1,4]{1,0:T(1,128)S(1)} %bitcast.11, s32[4,16]{1,0:T(4,128)S(1)} %pad_add_fusion.refs_1_.refs_0_, bf16[3,2,360,128]{3,2,1,0:T(8,128)(2,1)S(1)} %shard_map.82.refs_2_.refs_1_, bf16[3,2,360,128]{3,2,1,0:T(8,128)(2,1)S(1)} %shard_map.83.refs_2_.refs_3_, ...), custom_call_target="tpu_custom_call" | custom-call | flops 1 | bytes 1 | tf_op jit(solution)/shard_map/pallas_call | solution.py:40
  21.3 7.2 %collective-permute-start.2 = (bf16[2,360,128]{2,1,0:T(8,128)(2,1)S(1)}, bf16[2,360,128]{2,1,0:T(8,128)(2,1)S(1)}, u32[]{:S(2)}, u32[]{:S(2)}) collective-permute-start(bf16[2,360,128]{2,1,0:T(8,128)(2,1)S(1)} %get-tuple-element.30.refs_5_.refs_3_.refs_2_), channel_id=1, source_target_pairs={{0,64},{128,192},{64,0},{192,128},{65,129},{129,65},{66,130},{130,... | collective-permute-start | bytes 552968 | tf_op jit(solution)/shard_map/ppermute | solution.py:300
  29.2 1.6 %shard_map.88 = (bf16[2,360,128]{2,1,0:T(8,128)(2,1)S(1)}, bf16[2,360,128]{2,1,0:T(8,128)(2,1)S(1)}, bf16[1,2,360,128]{3,2,1,0:T(8,128)(2,1)S(1)}) custom-call(s32[4,16]{1,0:T(4,128)S(1)} %pad_add_fusion.refs_1_.refs_0_, bf16[3,2,360,128]{3,2,1,0:T(8,128)(2,1)S(1)} %shard_map.82.refs_2_.refs_1_, bf16[3,2,360,128]{3,2,1,0:T(8,128)(2,1)S(1)} %shard_map.83.refs_2_.refs_3_, ...), custom_call_target="tpu_custom_call" | custom-call | flops 1 | bytes 1 | tf_op jit(solution)/shard_map/pallas_call | solution.py:40
  30.8 1.7 %shard_map.89.refs_10_.refs_5_.refs_4_ = bf16[4,1024,128]{2,1,0:T(8,128)(2,1)S(1)} custom-call(f32[4,32]{1,0:T(4,128)S(1)} %copy.15.refs_0_, bf16[512,128]{1,0:T(8,128)(2,1)S(1)} %get-tuple-element.49.refs_1_, bf16[2,360,128]{2,1,0:T(8,128)(2,1)S(1)} %get-tuple-element.32.refs_2_.refs_4_, bf16[2,360,128]{2,1,0:T(8,128)(2,1)S(1)} %get-tuple-element.30.refs_5_.refs_3_.refs_2_, ...), custom_call_target="tpu_custom_call" | custom-call | flops 1 | bytes 1 | tf_op jit(solution)/shard_map/pallas_call | solution.py:40
  34.1 1.2 %collective-permute-done.2.refs_5_ = bf16[2,360,128]{2,1,0:T(8,128)(2,1)S(1)} collective-permute-done((bf16[2,360,128]{2,1,0:T(8,128)(2,1)S(1)}, bf16[2,360,128]{2,1,0:T(8,128)(2,1)S(1)}, u32[]{:S(2)}, u32[]{:S(2)}) %collective-permute-start.2) | collective-permute-done | bytes 184352 | tf_op jit(solution)/shard_map/ppermute | solution.py:300
  36.0 6.2 %collective-permute-start.6 = (bf16[2,2,360,128]{3,2,1,0:T(8,128)(2,1)S(1)}, bf16[2,2,360,128]{3,2,1,0:T(8,128)(2,1)S(1)}, u32[]{:S(2)}, u32[]{:S(2)}) collective-permute-start(bf16[2,2,360,128]{3,2,1,0:T(8,128)(2,1)S(1)} %get-tuple-element.37.refs_2_), channel_id=1, source_target_pairs={{1,2},{3,4},{5,6},{7,8},{9,10},{11,12},{13,14},{15,16},{17,18},{19... | collective-permute-start | bytes 1105928 | tf_op jit(solution)/shard_map/ppermute | solution.py:347
  42.2 1.9 %collective-permute-start.8 = (bf16[1,2,360,128]{3,2,1,0:T(8,128)(2,1)S(1)}, bf16[1,2,360,128]{3,2,1,0:T(8,128)(2,1)S(1)}, u32[]{:S(2)}, u32[]{:S(2)}) collective-permute-start(bf16[1,2,360,128]{3,2,1,0:T(8,128)(2,1)S(1)} %get-tuple-element.33.refs_9_.refs_1_), channel_id=1, source_target_pairs={{1,2},{3,4},{5,6},{7,8},{9,10},{11,12},{13,14},{15,16},{17,18},{19... | collective-permute-start | bytes 552968 | tf_op jit(solution)/shard_map/ppermute | solution.py:338
  44.2 1.2 %shard_map.92 = (bf16[2,360,128]{2,1,0:T(8,128)(2,1)S(1)}, bf16[2,360,128]{2,1,0:T(8,128)(2,1)S(1)}) custom-call(s32[1,4]{1,0:T(1,128)S(1)} %bitcast.14, s32[4,16]{1,0:T(4,128)S(1)} %pad_add_fusion.refs_1_.refs_0_, bf16[2,2,360,128]{3,2,1,0:T(8,128)(2,1)S(1)} %get-tuple-element.37.refs_2_, ...), custom_call_target="tpu_custom_call" | custom-call | flops 1 | bytes 1 | tf_op jit(solution)/shard_map/pallas_call | solution.py:40
  45.4 8.3 %collective-permute-start.11 = (bf16[2,360,128]{2,1,0:T(8,128)(2,1)S(1)}, bf16[2,360,128]{2,1,0:T(8,128)(2,1)S(1)}, u32[]{:S(2)}, u32[]{:S(2)}) collective-permute-start(bf16[2,360,128]{2,1,0:T(8,128)(2,1)S(1)} %get-tuple-element.38.refs_6_.refs_5_.refs_2_), channel_id=1, source_target_pairs={{0,64},{128,192},{64,0},{192,128},{65,129},{129,65},{66,130},{130,... | collective-permute-start | bytes 552968 | tf_op jit(solution)/shard_map/ppermute | solution.py:300
  54.4 1.2 %shard_map.93 = (bf16[2,360,128]{2,1,0:T(8,128)(2,1)S(1)}, bf16[2,360,128]{2,1,0:T(8,128)(2,1)S(1)}) custom-call(s32[1,4]{1,0:T(1,128)S(1)} %bitcast.15, s32[4,16]{1,0:T(4,128)S(1)} %pad_add_fusion.refs_1_.refs_0_, bf16[2,2,360,128]{3,2,1,0:T(8,128)(2,1)S(1)} %get-tuple-element.37.refs_2_, ...), custom_call_target="tpu_custom_call" | custom-call | flops 1 | bytes 1 | tf_op jit(solution)/shard_map/pallas_call | solution.py:40
  55.6 5.4 %collective-permute-start.9 = (bf16[2,360,128]{2,1,0:T(8,128)(2,1)S(1)}, bf16[2,360,128]{2,1,0:T(8,128)(2,1)S(1)}, u32[]{:S(2)}, u32[]{:S(2)}) collective-permute-start(bf16[2,360,128]{2,1,0:T(8,128)(2,1)S(1)} %get-tuple-element.40.refs_10_.refs_5_.refs_11_.refs_2_), channel_id=1, source_target_pairs={{0,64},{128,192},{64,0},{192,128},{65,129},{129,65},{66,130},{130,... | collective-permute-start | bytes 552968 | tf_op jit(solution)/shard_map/ppermute | solution.py:300
  61.8 1.5 %shard_map.94 = (bf16[2,360,128]{2,1,0:T(8,128)(2,1)S(1)}, bf16[2,360,128]{2,1,0:T(8,128)(2,1)S(1)}) custom-call(s32[4,16]{1,0:T(4,128)S(1)} %pad_add_fusion.refs_1_.refs_0_, bf16[1,2,360,128]{3,2,1,0:T(8,128)(2,1)S(1)} %get-tuple-element.33.refs_9_.refs_1_, bf16[3,2,360,128]{3,2,1,0:T(8,128)(2,1)S(1)} %get-tuple-element.35.refs_10_.refs_3_.refs_2_, ...), custom_call_target="tpu_custom_call" | custom-call | flops 1 | bytes 1 | tf_op jit(solution)/shard_map/pallas_call | solution.py:40
  63.4 1.5 %shard_map.95 = (bf16[2,360,128]{2,1,0:T(8,128)(2,1)S(1)}, bf16[2,360,128]{2,1,0:T(8,128)(2,1)S(1)}) custom-call(s32[4,16]{1,0:T(4,128)S(1)} %pad_add_fusion.refs_1_.refs_0_, bf16[1,2,360,128]{3,2,1,0:T(8,128)(2,1)S(1)} %get-tuple-element.33.refs_9_.refs_1_, bf16[3,2,360,128]{3,2,1,0:T(8,128)(2,1)S(1)} %get-tuple-element.35.refs_10_.refs_3_.refs_2_, ...), custom_call_target="tpu_custom_call" | custom-call | flops 1 | bytes 1 | tf_op jit(solution)/shard_map/pallas_call | solution.py:40
  64.9 2.1 %collective-permute-done.11.refs_5_ = bf16[2,360,128]{2,1,0:T(8,128)(2,1)S(1)} collective-permute-done((bf16[2,360,128]{2,1,0:T(8,128)(2,1)S(1)}, bf16[2,360,128]{2,1,0:T(8,128)(2,1)S(1)}, u32[]{:S(2)}, u32[]{:S(2)}) %collective-permute-start.11) | collective-permute-done | bytes 184352 | tf_op jit(solution)/shard_map/ppermute | solution.py:300
  67.7 7.2 %collective-permute-done.9.refs_5_ = bf16[2,360,128]{2,1,0:T(8,128)(2,1)S(1)} collective-permute-done((bf16[2,360,128]{2,1,0:T(8,128)(2,1)S(1)}, bf16[2,360,128]{2,1,0:T(8,128)(2,1)S(1)}, u32[]{:S(2)}, u32[]{:S(2)}) %collective-permute-start.9) | collective-permute-done | bytes 184352 | tf_op jit(solution)/shard_map/ppermute | solution.py:300
  74.9 1.5 %shard_map.97 = bf16[3,4,360,128]{3,2,1,0:T(8,128)(2,1)} custom-call(s32[1,4]{1,0:T(1,128)S(1)} %bitcast.17, bf16[2,2,360,128]{3,2,1,0:T(8,128)(2,1)S(1)} %get-tuple-element.36.refs_1_, bf16[2,360,128]{2,1,0:T(8,128)(2,1)S(1)} %get-tuple-element.40.refs_10_.refs_5_.refs_11_.refs_2_, ...), custom_call_target="tpu_custom_call" | custom-call | flops 1 | bytes 1 | tf_op jit(solution)/shard_map/pallas_call | solution.py:40
  (44 shorter events, 8.0 us)
Async XLA Ops:
  0.0 6.2 %copy-start = (f32[256,8,4]{0,2,1:T(4,128)S(1)}, f32[256,8,4]{0,2,1:T(4,128)}, u32[]{:S(2)}) copy-start(f32[256,8,4]{0,2,1:T(4,128)} %param.12) | copy-start | bytes 98308
  0.0 1.3 %copy-start.1 = (bf16[3,4,360,128]{3,2,1,0:T(8,128)(2,1)S(1)}, bf16[3,4,360,128]{3,2,1,0:T(8,128)(2,1)}, u32[]{:S(2)}) copy-start(bf16[3,4,360,128]{3,2,1,0:T(8,128)(2,1)} %refs_1_.7) | copy-start | bytes 3317764
  1.3 0.7 copy-start.3
  2.3 4.1 %copy-start.6 = (bf16[2,512,128]{2,1,0:T(8,128)(2,1)S(1)}, bf16[2,512,128]{2,1,0:T(8,128)(2,1)}, u32[]{:S(2)}) copy-start(bf16[2,512,128]{2,1,0:T(8,128)(2,1)} %param.14) | copy-start | bytes 786436
  2.3 17.7 %collective-permute-start = (bf16[3,2,360,128]{3,2,1,0:T(8,128)(2,1)S(1)}, bf16[3,2,360,128]{3,2,1,0:T(8,128)(2,1)S(1)}, u32[]{:S(2)}, u32[]{:S(2)}) collective-permute-start(bf16[3,2,360,128]{3,2,1,0:T(8,128)(2,1)S(1)} %shard_map.82.refs_2_.refs_1_), channel_id=1, source_target_pairs={{1,2},{3,4},{5,6},{7,8},{9,10},{11,12},{13,14},{15,16},{17,18},{19... | collective-permute-start | bytes 1658888 | tf_op jit(solution)/shard_map/ppermute | solution.py:287
  6.1 3.4 %collective-permute-start.1 = (bf16[3,2,360,128]{3,2,1,0:T(8,128)(2,1)S(1)}, bf16[3,2,360,128]{3,2,1,0:T(8,128)(2,1)S(1)}, u32[]{:S(2)}, u32[]{:S(2)}) collective-permute-start(bf16[3,2,360,128]{3,2,1,0:T(8,128)(2,1)S(1)} %shard_map.83.refs_2_.refs_3_), channel_id=1, source_target_pairs={{0,1},{2,3},{4,5},{6,7},{8,9},{10,11},{12,13},{14,15},{16,17},{18,... | collective-permute-start | bytes 1658888 | tf_op jit(solution)/shard_map/ppermute | solution.py:286
  6.4 1.8 %copy-start.7 = (s32[256,8]{0,1:T(8,128)S(1)}, s32[256,8]{0,1:T(8,128)}, u32[]{:S(2)}) copy-start(s32[256,8]{0,1:T(8,128)} %param.11) | copy-start | bytes 24580
  6.4 1.8 %copy-start.8 = (s32[256,8]{0,1:T(8,128)S(1)}, s32[256,8]{0,1:T(8,128)}, u32[]{:S(2)}) copy-start(s32[256,8]{0,1:T(8,128)} %param.10) | copy-start | bytes 24580
  6.4 3.1 %copy-start.5 = (s32[4]{0:T(128)S(1)}, s32[4]{0:T(128)}, u32[]{:S(2)}) copy-start(s32[4]{0:T(128)} %param.9) | copy-start | bytes 52
  9.5 6.8 %copy-start.2 = (bf16[3,4,360,128]{3,2,1,0:T(8,128)(2,1)S(1)}, bf16[3,4,360,128]{3,2,1,0:T(8,128)(2,1)}, u32[]{:S(2)}) copy-start(bf16[3,4,360,128]{3,2,1,0:T(8,128)(2,1)} %refs_1_.7) | copy-start | bytes 3317764
  9.5 6.8 %copy-start.4 = (f32[2,128]{1,0:T(2,128)S(1)}, f32[2,128]{1,0:T(2,128)}, u32[]{:S(2)}) copy-start(f32[2,128]{1,0:T(2,128)} %refs_9_.7) | copy-start | bytes 3076
  10.8 21.8 %collective-permute-start.4 = (bf16[2,360,128]{2,1,0:T(8,128)(2,1)S(1)}, bf16[2,360,128]{2,1,0:T(8,128)(2,1)S(1)}, u32[]{:S(2)}, u32[]{:S(2)}) collective-permute-start(bf16[2,360,128]{2,1,0:T(8,128)(2,1)S(1)} %get-tuple-element.27.refs_5_.refs_7_.refs_2_), channel_id=1, source_target_pairs={{0,64},{128,192},{64,0},{192,128},{65,129},{129,65},{66,130},{130,... | collective-permute-start | bytes 552968 | tf_op jit(solution)/shard_map/ppermute | solution.py:300
  15.7 16.9 %collective-permute-start.5 = (bf16[2,360,128]{2,1,0:T(8,128)(2,1)S(1)}, bf16[2,360,128]{2,1,0:T(8,128)(2,1)S(1)}, u32[]{:S(2)}, u32[]{:S(2)}) collective-permute-start(bf16[2,360,128]{2,1,0:T(8,128)(2,1)S(1)} %get-tuple-element.28.refs_6_.refs_8_.refs_3_), channel_id=1, source_target_pairs={{64,128},{128,64},{1,65},{129,193},{65,1},{193,129},{2,66},{130,19... | collective-permute-start | bytes 552968 | tf_op jit(solution)/shard_map/ppermute | solution.py:300
  21.3 14.0 %collective-permute-start.2 = (bf16[2,360,128]{2,1,0:T(8,128)(2,1)S(1)}, bf16[2,360,128]{2,1,0:T(8,128)(2,1)S(1)}, u32[]{:S(2)}, u32[]{:S(2)}) collective-permute-start(bf16[2,360,128]{2,1,0:T(8,128)(2,1)S(1)} %get-tuple-element.30.refs_5_.refs_3_.refs_2_), channel_id=1, source_target_pairs={{0,64},{128,192},{64,0},{192,128},{65,129},{129,65},{66,130},{130,... | collective-permute-start | bytes 552968 | tf_op jit(solution)/shard_map/ppermute | solution.py:300
  28.5 6.8 %collective-permute-start.3 = (bf16[2,360,128]{2,1,0:T(8,128)(2,1)S(1)}, bf16[2,360,128]{2,1,0:T(8,128)(2,1)S(1)}, u32[]{:S(2)}, u32[]{:S(2)}) collective-permute-start(bf16[2,360,128]{2,1,0:T(8,128)(2,1)S(1)} %get-tuple-element.31.refs_6_.refs_4_.refs_3_), channel_id=1, source_target_pairs={{64,128},{128,64},{1,65},{129,193},{65,1},{193,129},{2,66},{130,19... | collective-permute-start | bytes 552968 | tf_op jit(solution)/shard_map/ppermute | solution.py:300
  33.3 10.8 %collective-permute-start.7 = (bf16[3,2,360,128]{3,2,1,0:T(8,128)(2,1)S(1)}, bf16[3,2,360,128]{3,2,1,0:T(8,128)(2,1)S(1)}, u32[]{:S(2)}, u32[]{:S(2)}) collective-permute-start(bf16[3,2,360,128]{3,2,1,0:T(8,128)(2,1)S(1)} %get-tuple-element.35.refs_10_.refs_3_.refs_2_), channel_id=1, source_target_pairs={{0,1},{2,3},{4,5},{6,7},{8,9},{10,11},{12,13},{14,15},{16,17},{18,... | collective-permute-start | bytes 1658888 | tf_op jit(solution)/shard_map/ppermute | solution.py:343
  36.0 18.4 %collective-permute-start.6 = (bf16[2,2,360,128]{3,2,1,0:T(8,128)(2,1)S(1)}, bf16[2,2,360,128]{3,2,1,0:T(8,128)(2,1)S(1)}, u32[]{:S(2)}, u32[]{:S(2)}) collective-permute-start(bf16[2,2,360,128]{3,2,1,0:T(8,128)(2,1)S(1)} %get-tuple-element.37.refs_2_), channel_id=1, source_target_pairs={{1,2},{3,4},{5,6},{7,8},{9,10},{11,12},{13,14},{15,16},{17,18},{19... | collective-permute-start | bytes 1105928 | tf_op jit(solution)/shard_map/ppermute | solution.py:347
  42.2 21.1 %collective-permute-start.8 = (bf16[1,2,360,128]{3,2,1,0:T(8,128)(2,1)S(1)}, bf16[1,2,360,128]{3,2,1,0:T(8,128)(2,1)S(1)}, u32[]{:S(2)}, u32[]{:S(2)}) collective-permute-start(bf16[1,2,360,128]{3,2,1,0:T(8,128)(2,1)S(1)} %get-tuple-element.33.refs_9_.refs_1_), channel_id=1, source_target_pairs={{1,2},{3,4},{5,6},{7,8},{9,10},{11,12},{13,14},{15,16},{17,18},{19... | collective-permute-start | bytes 552968 | tf_op jit(solution)/shard_map/ppermute | solution.py:338
  45.4 21.6 %collective-permute-start.11 = (bf16[2,360,128]{2,1,0:T(8,128)(2,1)S(1)}, bf16[2,360,128]{2,1,0:T(8,128)(2,1)S(1)}, u32[]{:S(2)}, u32[]{:S(2)}) collective-permute-start(bf16[2,360,128]{2,1,0:T(8,128)(2,1)S(1)} %get-tuple-element.38.refs_6_.refs_5_.refs_2_), channel_id=1, source_target_pairs={{0,64},{128,192},{64,0},{192,128},{65,129},{129,65},{66,130},{130,... | collective-permute-start | bytes 552968 | tf_op jit(solution)/shard_map/ppermute | solution.py:300
  53.7 13.2 %collective-permute-start.12 = (bf16[2,360,128]{2,1,0:T(8,128)(2,1)S(1)}, bf16[2,360,128]{2,1,0:T(8,128)(2,1)S(1)}, u32[]{:S(2)}, u32[]{:S(2)}) collective-permute-start(bf16[2,360,128]{2,1,0:T(8,128)(2,1)S(1)} %get-tuple-element.39.refs_7_.refs_6_.refs_3_), channel_id=1, source_target_pairs={{64,128},{128,64},{1,65},{129,193},{65,1},{193,129},{2,66},{130,19... | collective-permute-start | bytes 552968 | tf_op jit(solution)/shard_map/ppermute | solution.py:300
  55.6 19.3 %collective-permute-start.9 = (bf16[2,360,128]{2,1,0:T(8,128)(2,1)S(1)}, bf16[2,360,128]{2,1,0:T(8,128)(2,1)S(1)}, u32[]{:S(2)}, u32[]{:S(2)}) collective-permute-start(bf16[2,360,128]{2,1,0:T(8,128)(2,1)S(1)} %get-tuple-element.40.refs_10_.refs_5_.refs_11_.refs_2_), channel_id=1, source_target_pairs={{0,64},{128,192},{64,0},{192,128},{65,129},{129,65},{66,130},{130,... | collective-permute-start | bytes 552968 | tf_op jit(solution)/shard_map/ppermute | solution.py:300
  61.0 14.0 %collective-permute-start.10 = (bf16[2,360,128]{2,1,0:T(8,128)(2,1)S(1)}, bf16[2,360,128]{2,1,0:T(8,128)(2,1)S(1)}, u32[]{:S(2)}, u32[]{:S(2)}) collective-permute-start(bf16[2,360,128]{2,1,0:T(8,128)(2,1)S(1)} %get-tuple-element.41.refs_11_.refs_6_.refs_12_.refs_3_), channel_id=1, source_target_pairs={{64,128},{128,64},{1,65},{129,193},{65,1},{193,129},{2,66},{130,19... | collective-permute-start | bytes 552968 | tf_op jit(solution)/shard_map/ppermute | solution.py:300
